TPU v7x, 32 devices: a whole 2x2x4 slice. The times are simulated.
32 devices in a mesh: dp: 4 (over z), fsdp: 8 (over y, x, core).
Axes of the slice: x: 2, y: 2, z: 4, core: 2. Of those that a mesh axis runs over, the one named last changes fastest.
Arguments:
- tokens: bfloat16 [11040, 768], P(('dp', 'fsdp')), may hold values from -6 to 6
- cotangent: bfloat16 [11040, 768], P(('dp', 'fsdp')), may hold values from -6 to 6
- norm1_gain: bfloat16 [2, 768], P(None, 'fsdp'), may hold values from 0.099609375 to 1.8984375
- norm1_bias: bfloat16 [2, 768], P(None, 'fsdp'), may hold values from -3 to 3
- qkv_weight: bfloat16 [2, 768, 2304], P(None, 'fsdp'), may hold values from -0.21875 to 0.21875
- query_bias: bfloat16 [2, 768], P(None, 'fsdp'), may hold values from -3 to 3
- value_bias: bfloat16 [2, 768], P(None, 'fsdp'), may hold values from -3 to 3
- out_weight: bfloat16 [2, 768, 768], P(None, 'fsdp'), may hold values from -1.75 to 1.75
- out_bias: bfloat16 [2, 768], P(None, 'fsdp'), may hold values from -3 to 3
- norm2_gain: bfloat16 [2, 768], P(None, 'fsdp'), may hold values from 0.099609375 to 1.8984375
- norm2_bias: bfloat16 [2, 768], P(None, 'fsdp'), may hold values from -3 to 3
- up_weight: bfloat16 [2, 768, 3072], P(None, 'fsdp'), may hold values from -0.21875 to 0.21875
- up_bias: bfloat16 [2, 3072], P(None, 'fsdp'), may hold values from -4 to 4
- down_weight: bfloat16 [2, 3072, 768], P(None, 'fsdp'), may hold values from -0.109375 to 0.109375
- down_bias: bfloat16 [2, 768], P(None, 'fsdp'), may hold values from -3 to 3
Outputs:
- encoded: bfloat16 [11040, 768], P(('dp', 'fsdp'))
- tokens_grad: float32 [11040, 768], P(('dp', 'fsdp'))
- grad_norm1_gain: float32 [2, 768], P(None, 'fsdp')
- grad_norm1_bias: float32 [2, 768], P(None, 'fsdp')
- grad_qkv_weight: float32 [2, 768, 2304], P(None, 'fsdp')
- grad_query_bias: float32 [2, 768], P(None, 'fsdp')
- grad_value_bias: float32 [2, 768], P(None, 'fsdp')
- grad_out_weight: float32 [2, 768, 768], P(None, 'fsdp')
- grad_out_bias: float32 [2, 768], P(None, 'fsdp')
- grad_norm2_gain: float32 [2, 768], P(None, 'fsdp')
- grad_norm2_bias: float32 [2, 768], P(None, 'fsdp')
- grad_up_weight: float32 [2, 768, 3072], P(None, 'fsdp')
- grad_up_bias: float32 [2, 3072], P(None, 'fsdp')
- grad_down_weight: float32 [2, 3072, 768], P(None, 'fsdp')
- grad_down_bias: float32 [2, 768], P(None, 'fsdp')
All inputs are finite; a program needn't handle non-finite values.
Results may differ from a plain program's by a relative error of at most 0.015.
Values may be sent and summed in bfloat16 or wider, within the bound.
A program may use at most 192 MiB of HBM per device.

v0:
```python
import jax
import jax.numpy as jnp
from jax import lax
from jax.sharding import PartitionSpec as P

D = 768
HEADS = 12
HEAD_DIM = 64
GLEN = 197
LLEN = 37
G_DEV = 1
L_DEV = 4


epsilon = 1e-06


def norm_rows(values_in, gain, shift):
    row_mean = jnp.mean(values_in, axis=-1, keepdims=True)
    centred = values_in - row_mean
    spread = jnp.mean(centred * centred, axis=-1, keepdims=True)
    return centred * lax.rsqrt(spread + epsilon) * gain + shift


def contract_rows(left, right):
    return lax.dot_general(
        left, right, (((0,), (0,)), ((), ())), preferred_element_type=jnp.float32
    )


def contract_cols(left, right):
    return lax.dot_general(
        left, right, (((1,), (1,)), ((), ())), preferred_element_type=jnp.float32
    )


def gather_forward(pieces):
    return (
        lax.all_gather(pieces[0], "fsdp", axis=0, tiled=True),
        lax.all_gather(pieces[1], "fsdp", axis=0, tiled=True),
        lax.all_gather(pieces[2], "fsdp", axis=0, tiled=True),
        lax.all_gather(pieces[3], "fsdp", axis=0, tiled=True),
        lax.all_gather(pieces[4], "fsdp", axis=0, tiled=True),
        lax.all_gather(pieces[5], "fsdp", axis=0, tiled=True),
        lax.all_gather(pieces[6], "fsdp", axis=0, tiled=True),
        lax.all_gather(pieces[7], "fsdp", axis=0, tiled=True),
        lax.all_gather(pieces[8], "fsdp", axis=0, tiled=True),
        lax.all_gather(pieces[9], "fsdp", axis=0, tiled=True),
        lax.all_gather(pieces[10], "fsdp", axis=0, tiled=True),
        lax.all_gather(pieces[11], "fsdp", axis=0, tiled=True),
        lax.all_gather(pieces[12], "fsdp", axis=0, tiled=True),
    )


def gather_backward(pieces):
    return (
        lax.all_gather(pieces[0], "fsdp", axis=0, tiled=True),
        lax.all_gather(pieces[1], "fsdp", axis=0, tiled=True),
        lax.all_gather(pieces[2], "fsdp", axis=0, tiled=True),
        lax.all_gather(pieces[3], "fsdp", axis=0, tiled=True),
        lax.all_gather(pieces[4], "fsdp", axis=0, tiled=True),
        lax.all_gather(pieces[5], "fsdp", axis=0, tiled=True),
        lax.all_gather(pieces[6], "fsdp", axis=0, tiled=True),
        lax.all_gather(pieces[7], "fsdp", axis=0, tiled=True),
        lax.all_gather(pieces[8], "fsdp", axis=0, tiled=True),
        lax.all_gather(pieces[9], "fsdp", axis=0, tiled=True),
        lax.all_gather(pieces[10], "fsdp", axis=0, tiled=True),
        lax.all_gather(pieces[11], "fsdp", axis=0, tiled=True),
        lax.all_gather(pieces[12], "fsdp", axis=0, tiled=True),
    )


def reduce_grads(grads):
    shares = (
        lax.psum_scatter(grads[0], "fsdp", scatter_dimension=0, tiled=True),
        lax.psum_scatter(grads[1], "fsdp", scatter_dimension=0, tiled=True),
        lax.psum_scatter(grads[2], "fsdp", scatter_dimension=0, tiled=True),
        lax.psum_scatter(grads[3], "fsdp", scatter_dimension=0, tiled=True),
        lax.psum_scatter(grads[4], "fsdp", scatter_dimension=0, tiled=True),
        lax.psum_scatter(grads[5], "fsdp", scatter_dimension=0, tiled=True),
        lax.psum_scatter(grads[6], "fsdp", scatter_dimension=0, tiled=True),
        lax.psum_scatter(grads[7], "fsdp", scatter_dimension=0, tiled=True),
        lax.psum_scatter(grads[8], "fsdp", scatter_dimension=0, tiled=True),
        lax.psum_scatter(grads[9], "fsdp", scatter_dimension=0, tiled=True),
        lax.psum_scatter(grads[10], "fsdp", scatter_dimension=0, tiled=True),
        lax.psum_scatter(grads[11], "fsdp", scatter_dimension=0, tiled=True),
        lax.psum_scatter(grads[12], "fsdp", scatter_dimension=0, tiled=True),
    )
    column_parts = (
        lax.psum_scatter(
            shares[2].astype(jnp.bfloat16), "dp", scatter_dimension=1, tiled=True
        ).astype(jnp.float32),
        lax.psum_scatter(
            shares[5].astype(jnp.bfloat16), "dp", scatter_dimension=1, tiled=True
        ).astype(jnp.float32),
        lax.psum_scatter(
            shares[9].astype(jnp.bfloat16), "dp", scatter_dimension=1, tiled=True
        ).astype(jnp.float32),
        lax.psum_scatter(
            shares[11].astype(jnp.bfloat16), "dp", scatter_dimension=1, tiled=True
        ).astype(jnp.float32),
    )
    matrices = (
        lax.all_gather(column_parts[0].astype(jnp.bfloat16), "dp", axis=1, tiled=True).astype(
            jnp.float32
        ),
        lax.all_gather(column_parts[1].astype(jnp.bfloat16), "dp", axis=1, tiled=True).astype(
            jnp.float32
        ),
        lax.all_gather(column_parts[2].astype(jnp.bfloat16), "dp", axis=1, tiled=True).astype(
            jnp.float32
        ),
        lax.all_gather(column_parts[3].astype(jnp.bfloat16), "dp", axis=1, tiled=True).astype(
            jnp.float32
        ),
    )
    vectors = lax.psum(
        (
            shares[0],
            shares[1],
            shares[3],
            shares[4],
            shares[6],
            shares[7],
            shares[8],
            shares[10],
            shares[12],
        ),
        "dp",
    )
    return (
        vectors[0],
        vectors[1],
        matrices[0],
        vectors[2],
        vectors[3],
        matrices[1],
        vectors[4],
        vectors[5],
        vectors[6],
        matrices[2],
        vectors[7],
        matrices[3],
        vectors[8],
    )


def attend_crops(queries, keys_in, values_in, crop_count, crop_length):
    shape_four = (crop_count, crop_length, HEADS, HEAD_DIM)
    scores = jnp.einsum(
        "clhe,cmhe->chlm",
        queries.reshape(shape_four),
        keys_in.reshape(shape_four),
        preferred_element_type=jnp.float32,
    ) * HEAD_DIM ** (-0.5)
    peak_score = jnp.max(scores, axis=-1, keepdims=True)
    raised = jnp.exp(scores - peak_score)
    exp_total = jnp.sum(raised, axis=-1, keepdims=True)
    attn_probs = (raised / exp_total).astype(jnp.bfloat16)
    log_total = peak_score + jnp.log(exp_total)
    result = jnp.einsum(
        "chlm,cmhe->clhe",
        attn_probs,
        values_in.reshape(shape_four),
        preferred_element_type=jnp.float32,
    )
    return (result.reshape(crop_count * crop_length, D), log_total)


def attend_back(queries, keys_in, values_in, log_total, grad_mixed, crop_count, crop_length):
    shape_four = (crop_count, crop_length, HEADS, HEAD_DIM)
    score_scale = HEAD_DIM ** (-0.5)
    query_four = queries.reshape(shape_four)
    key_four = keys_in.reshape(shape_four)
    value_four = values_in.reshape(shape_four)
    grad_four = grad_mixed.reshape(shape_four)
    scores = (
        jnp.einsum("clhe,cmhe->chlm", query_four, key_four, preferred_element_type=jnp.float32)
        * score_scale
    )
    attn_probs = jnp.exp(scores - log_total)
    grad_probs = jnp.einsum(
        "clhe,cmhe->chlm", grad_four, value_four, preferred_element_type=jnp.float32
    )
    grad_values = jnp.einsum(
        "chlm,clhe->cmhe",
        attn_probs.astype(jnp.bfloat16),
        grad_four,
        preferred_element_type=jnp.float32,
    )
    row_inner = jnp.sum(grad_probs * attn_probs, axis=-1, keepdims=True)
    grad_scores = (attn_probs * (grad_probs - row_inner)).astype(jnp.bfloat16)
    grad_queries = (
        jnp.einsum("chlm,cmhe->clhe", grad_scores, key_four, preferred_element_type=jnp.float32)
        * score_scale
    )
    grad_keys = (
        jnp.einsum("chlm,clhe->cmhe", grad_scores, query_four, preferred_element_type=jnp.float32)
        * score_scale
    )
    rows_here = crop_count * crop_length
    return jnp.concatenate(
        [
            grad_queries.reshape(rows_here, D),
            grad_keys.reshape(rows_here, D),
            grad_values.reshape(rows_here, D),
        ],
        axis=1,
    )


def forward_layer(stream, weights):
    (
        gain_one,
        shift_one,
        w_qkv,
        bias_query,
        bias_value,
        w_out,
        bias_out,
        gain_two,
        shift_two,
        w_up,
        bias_up,
        w_down,
        bias_down,
    ) = weights
    normed = norm_rows(stream, gain_one.astype(jnp.float32), shift_one.astype(jnp.float32)).astype(
        jnp.bfloat16
    )
    bias_all = jnp.concatenate([bias_query, jnp.zeros_like(bias_query), bias_value]).astype(
        jnp.float32
    )
    projected = (jnp.dot(normed, w_qkv, preferred_element_type=jnp.float32) + bias_all).astype(
        jnp.bfloat16
    )
    global_rows = G_DEV * GLEN
    global_part, global_total = attend_crops(
        projected[:global_rows, :D],
        projected[:global_rows, D : 2 * D],
        projected[:global_rows, 2 * D :],
        G_DEV,
        GLEN,
    )
    local_part, local_total = attend_crops(
        projected[global_rows:, :D],
        projected[global_rows:, D : 2 * D],
        projected[global_rows:, 2 * D :],
        L_DEV,
        LLEN,
    )
    mixed = jnp.concatenate([global_part, local_part], axis=0).astype(jnp.bfloat16)
    stream_one = (
        stream
        + jnp.dot(mixed, w_out, preferred_element_type=jnp.float32)
        + bias_out.astype(jnp.float32)
    )
    normed_two = norm_rows(
        stream_one, gain_two.astype(jnp.float32), shift_two.astype(jnp.float32)
    ).astype(jnp.bfloat16)
    pre_act = jnp.dot(normed_two, w_up, preferred_element_type=jnp.float32) + bias_up.astype(
        jnp.float32
    )
    hidden = jax.nn.gelu(pre_act, approximate=False).astype(jnp.bfloat16)
    result = (
        stream_one
        + jnp.dot(hidden, w_down, preferred_element_type=jnp.float32)
        + bias_down.astype(jnp.float32)
    )
    saved_state = (
        stream,
        normed,
        projected,
        global_total,
        local_total,
        mixed,
        stream_one,
        normed_two,
        pre_act,
        hidden,
    )
    return (result, saved_state)


def backward_layer(upstream, weights, saved_state):
    (
        gain_one,
        shift_one,
        w_qkv,
        bias_query,
        bias_value,
        w_out,
        bias_out,
        gain_two,
        shift_two,
        w_up,
        bias_up,
        w_down,
        bias_down,
    ) = weights
    (
        stream,
        normed,
        projected,
        global_total,
        local_total,
        mixed,
        stream_one,
        normed_two,
        pre_act,
        hidden,
    ) = saved_state
    branch_two = upstream.astype(jnp.bfloat16)
    grad_bias_down = jnp.sum(branch_two.astype(jnp.float32), axis=0)
    grad_w_down = contract_rows(hidden, branch_two)
    grad_hidden = contract_cols(branch_two, w_down)
    unused, gelu_pull = jax.vjp(lambda value: jax.nn.gelu(value, approximate=False), pre_act)
    grad_pre = gelu_pull(grad_hidden)[0].astype(jnp.bfloat16)
    grad_bias_up = jnp.sum(grad_pre.astype(jnp.float32), axis=0)
    grad_w_up = contract_rows(normed_two, grad_pre)
    grad_normed_two = contract_cols(grad_pre, w_up)
    unused_two, norm_pull_two = jax.vjp(
        norm_rows, stream_one, gain_two.astype(jnp.float32), shift_two.astype(jnp.float32)
    )
    grad_stream_part, grad_gain_two, grad_shift_two = norm_pull_two(grad_normed_two)
    grad_stream_one = upstream + grad_stream_part
    branch_one = grad_stream_one.astype(jnp.bfloat16)
    grad_bias_out = jnp.sum(branch_one.astype(jnp.float32), axis=0)
    grad_w_out = contract_rows(mixed, branch_one)
    grad_mixed = contract_cols(branch_one, w_out).astype(jnp.bfloat16)
    global_rows = G_DEV * GLEN
    grad_global = attend_back(
        projected[:global_rows, :D],
        projected[:global_rows, D : 2 * D],
        projected[:global_rows, 2 * D :],
        global_total,
        grad_mixed[:global_rows],
        G_DEV,
        GLEN,
    )
    grad_local = attend_back(
        projected[global_rows:, :D],
        projected[global_rows:, D : 2 * D],
        projected[global_rows:, 2 * D :],
        local_total,
        grad_mixed[global_rows:],
        L_DEV,
        LLEN,
    )
    grad_projected = jnp.concatenate([grad_global, grad_local], axis=0).astype(jnp.bfloat16)
    column_sums = jnp.sum(grad_projected.astype(jnp.float32), axis=0)
    grad_bias_query = column_sums[:D]
    grad_bias_value = column_sums[2 * D :]
    grad_w_qkv = contract_rows(normed, grad_projected)
    grad_normed = contract_cols(grad_projected, w_qkv)
    unused_one, norm_pull_one = jax.vjp(
        norm_rows, stream, gain_one.astype(jnp.float32), shift_one.astype(jnp.float32)
    )
    grad_input_part, grad_gain_one, grad_shift_one = norm_pull_one(grad_normed)
    grad_stream = grad_stream_one + grad_input_part
    grads = (
        grad_gain_one,
        grad_shift_one,
        grad_w_qkv,
        grad_bias_query,
        grad_bias_value,
        grad_w_out,
        grad_bias_out,
        grad_gain_two,
        grad_shift_two,
        grad_w_up,
        grad_bias_up,
        grad_w_down,
        grad_bias_down,
    )
    return (grad_stream, grads)


def local(
    tokens,
    cotangent,
    norm1_gain,
    norm1_bias,
    qkv_weight,
    query_bias,
    value_bias,
    out_weight,
    out_bias,
    norm2_gain,
    norm2_bias,
    up_weight,
    up_bias,
    down_weight,
    down_bias,
):
    shards = (
        norm1_gain,
        norm1_bias,
        qkv_weight,
        query_bias,
        value_bias,
        out_weight,
        out_bias,
        norm2_gain,
        norm2_bias,
        up_weight,
        up_bias,
        down_weight,
        down_bias,
    )
    layer_total = qkv_weight.shape[0]
    stream = tokens.astype(jnp.float32)
    saved_layers = []
    kept_weights = []
    for layer_index in range(layer_total):
        weights = gather_forward(tuple((w[layer_index] for w in shards)))
        stream, saved_state = forward_layer(stream, weights)
        saved_layers.append(saved_state)
        kept_weights.append(weights)
    encoded = stream.astype(jnp.bfloat16)
    upstream = cotangent.astype(jnp.float32)
    reduced_layers = [None] * layer_total
    for layer_index in reversed(range(layer_total)):
        weights = gather_backward(tuple((w[layer_index] for w in shards)))
        upstream, grads = backward_layer(upstream, weights, saved_layers[layer_index])
        reduced_layers[layer_index] = reduce_grads(grads)
    stacked = tuple(
        (
            jnp.stack(
                [reduced_layers[layer_index][member] for layer_index in range(layer_total)], axis=0
            )
            for member in range(13)
        )
    )
    return (
        encoded,
        upstream,
        stacked[0],
        stacked[1],
        stacked[2],
        stacked[3],
        stacked[4],
        stacked[5],
        stacked[6],
        stacked[7],
        stacked[8],
        stacked[9],
        stacked[10],
        stacked[11],
        stacked[12],
    )


def solution(mesh):
    in_specs = (
        P(("dp", "fsdp"), None),
        P(("dp", "fsdp"), None),
        P(None, "fsdp"),
        P(None, "fsdp"),
        P(None, "fsdp", None),
        P(None, "fsdp"),
        P(None, "fsdp"),
        P(None, "fsdp", None),
        P(None, "fsdp"),
        P(None, "fsdp"),
        P(None, "fsdp"),
        P(None, "fsdp", None),
        P(None, "fsdp"),
        P(None, "fsdp", None),
        P(None, "fsdp"),
    )
    out_specs = (
        P(("dp", "fsdp"), None),
        P(("dp", "fsdp"), None),
        P(None, "fsdp"),
        P(None, "fsdp"),
        P(None, "fsdp", None),
        P(None, "fsdp"),
        P(None, "fsdp"),
        P(None, "fsdp", None),
        P(None, "fsdp"),
        P(None, "fsdp"),
        P(None, "fsdp"),
        P(None, "fsdp", None),
        P(None, "fsdp"),
        P(None, "fsdp", None),
        P(None, "fsdp"),
    )
    return jax.shard_map(local, mesh=mesh, in_specs=in_specs, out_specs=out_specs, check_vma=False)
```

profile of v0, /device:TPU:0, one launch (start us, length us, event | category | flops | bytes accessed | tf_op | source)
XLA Modules:
  0.0 1178.7 jit_solution(6777888926240907779)
XLA Ops:
  7.2 2.2 fusion.178
  20.8 26.0 %all-reduce.36 = (bf16[768]{0:T(1024)(128)(2,1)S(1)}, bf16[768]{0:T(1024)(128)(2,1)S(1)}, bf16[768]{0:T(1024)(128)(2,1)S(1)}, bf16[768]{0:T(1024)(128)(2,1)S(1)}...) all-reduce(bf16[768]{0:T(1024)(128)(2,1)S(1)} %dynamic-update-slice, ...), channel_id=8, replica_groups=mesh['dp'=4,'fsdp'=8] {'fsdp'}, use_global_device_ids=true, to_apply=%add.4 | all-reduce | flops 12288 | bytes 49152
  48.7 8.5 all-gather.23
  57.7 8.5 all-gather.10
  67.4 3.6 fusion.34
  83.6 2.6 fusion.185
  87.5 27.9 %all-gather.41.cloned.1.call-done = bf16[1,768,3072]{2,1,0:T(8,128)(2,1)} async-done(((bf16[1,96,3072]{2,1,0:T(8,128)(2,1)}), bf16[1,768,3072]{2,1,0:T(8,128)(2,1)}) %all-gather.41.cloned.1.call-update) | async-done | bytes 4718608 | tf_op jit(solution)/shard_map/all_gather | solution.py:48
  115.5 15.1 %multiply_convert_fusion.1 = (bf16[345,3072]{1,0:T(8,128)(2,1)}, f32[345,3072]{1,0:T(8,128)}, f32[345,3072]{1,0:T(8,128)}) fusion(f32[3072]{0:T(1024)S(1)} %bitcast.349, bf16[1,768,3072]{2,1,0:T(8,128)(2,1)} %all-gather.41.cloned.1.call-done, f32[345,768]{1,0:T(8,128)} %copy-done.12, f32[768]{0:T(1024)S(1)} %convert_element_type.310, ...), kind=kOutput, calls=%fused_computation.39 | convolution fusion | flops 1699188480 | bytes 16398024 | tf_op jit(solution)/shard_map/dot_general | solution.py:261
  130.7 26.1 %all-gather.43.cloned.1.call-done = bf16[1,3072,768]{2,1,0:T(8,128)(2,1)} async-done(((bf16[1,384,768]{2,1,0:T(8,128)(2,1)}), bf16[1,3072,768]{2,1,0:T(8,128)(2,1)}) %all-gather.43.cloned.1.call-update) | async-done | bytes 4718608 | tf_op jit(solution)/shard_map/all_gather | solution.py:50
  156.8 5.2 fusion.186
  163.2 29.2 %all-gather.45.cloned.1.call-done = bf16[1,768,2304]{2,1,0:T(8,128)(2,1)} async-done(((bf16[1,96,2304]{2,1,0:T(8,128)(2,1)}), bf16[1,768,2304]{2,1,0:T(8,128)(2,1)}) %all-gather.45.cloned.1.call-update) | async-done | bytes 3538960 | tf_op jit(solution)/shard_map/all_gather | solution.py:41
  192.5 3.9 fusion.35
  210.7 2.2 reshape.519
  216.8 2.2 copy.193
  219.1 2.4 reshape.691
  226.1 2.9 fusion.188
  231.5 28.2 %all-gather.49.cloned.1.call-done = bf16[1,768,3072]{2,1,0:T(8,128)(2,1)} async-done(((bf16[1,96,3072]{2,1,0:T(8,128)(2,1)}), bf16[1,768,3072]{2,1,0:T(8,128)(2,1)}) %all-gather.49.cloned.1.call-update) | async-done | bytes 4718608 | tf_op jit(solution)/shard_map/all_gather | solution.py:48
  259.7 15.0 %multiply_convert_fusion = (bf16[345,3072]{1,0:T(8,128)(2,1)}, f32[345,3072]{1,0:T(8,128)}, f32[345,3072]{1,0:T(8,128)}) fusion(f32[3072]{0:T(1024)} %bitcast.348, bf16[1,768,3072]{2,1,0:T(8,128)(2,1)} %all-gather.49.cloned.1.call-done, f32[345,768]{1,0:T(8,128)} %copy-done.6, f32[768]{0:T(1024)S(1)} %convert_element_type.316, ...), kind=kOutput, calls=%fused_computation.26 | convolution fusion | flops 1699188480 | bytes 16398024 | tf_op jit(solution)/shard_map/dot_general | solution.py:261
  274.7 26.4 %all-gather.51.cloned.1.call-done = bf16[1,3072,768]{2,1,0:T(8,128)(2,1)} async-done(((bf16[1,384,768]{2,1,0:T(8,128)(2,1)}), bf16[1,3072,768]{2,1,0:T(8,128)(2,1)}) %all-gather.51.cloned.1.call-update) | async-done | bytes 4718608 | tf_op jit(solution)/shard_map/all_gather | solution.py:50
  301.1 8.7 convert_reduce_fusion
  309.9 2.6 multiply_reduce_fusion.4
  324.8 2.2 fusion.135
  328.9 3.3 convolution_convert_fusion.7
  341.4 2.3 reshape.528
  349.9 2.3 copy.157
  352.3 6.0 multiply_reduce_fusion.6
  360.7 9.0 convert_reduce_fusion.1
  369.7 2.6 multiply_reduce_fusion.5
  374.7 2.2 fusion.136
  377.0 7.2 fusion.162
  411.1 2.3 copy.171
  417.5 5.2 fusion.157
  424.0 7.9 fusion.150
  433.2 2.3 convert_reduce_fusion.2
  436.7 4.8 fusion.164
  444.0 8.1 fusion.189
  453.5 7.5 fusion.161
  464.9 45.6 %reduce-scatter.31.cloned.1.call-done = f32[96,2304]{1,0:T(8,128)} async-done(((f32[768,2304]{1,0:T(8,128)}), f32[96,2304]{1,0:T(8,128)}) %reduce-scatter.31.cloned.1.call-update) | async-done | bytes 884752 | tf_op jit(solution)/shard_map/reduce_scatter | solution.py:77
  513.2 66.7 %reduce-scatter.29.cloned.1.call-done = f32[96,2304]{1,0:T(8,128)} async-done(((f32[768,2304]{1,0:T(8,128)}), f32[96,2304]{1,0:T(8,128)}) %reduce-scatter.29.cloned.1.call-update) | async-done | bytes 884752 | tf_op jit(solution)/shard_map/reduce_scatter | solution.py:77
  582.3 6.8 fusion.163
  590.6 69.3 %reduce-scatter.45.cloned.1.call-done = f32[384,768]{1,0:T(8,128)} async-done(((f32[3072,768]{1,0:T(8,128)}), f32[384,768]{1,0:T(8,128)}) %reduce-scatter.45.cloned.1.call-update) | async-done | bytes 1179664 | tf_op jit(solution)/shard_map/reduce_scatter | solution.py:86
  664.3 3.0 add_add_fusion.4
  667.3 5.0 fusion.68
  672.3 49.4 %all-reduce.39.cloned.1.call-done = (f32[768]{0:T(1024)}, f32[768]{0:T(1024)}, f32[768]{0:T(1024)}, f32[768]{0:T(1024)}, f32[768]{0:T(1024)}, /*index=5*/f32[768...) async-done(((f32[768]{0:T(1024)}, f32[768]{0:T(1024)}, ...) | async-done | bytes 73744
  723.3 79.8 %reduce-scatter.47.cloned.1.call-done = f32[384,768]{1,0:T(8,128)} async-done(((f32[3072,768]{1,0:T(8,128)}), f32[384,768]{1,0:T(8,128)}) %reduce-scatter.47.cloned.1.call-update) | async-done | bytes 1179664 | tf_op jit(solution)/shard_map/reduce_scatter | solution.py:86
  811.7 18.8 %all-reduce.35 = (f32[1,96]{1,0:T(1,128)S(1)}, f32[1,96]{1,0:T(1,128)S(1)}, f32[1,96]{1,0:T(1,128)S(1)}, f32[1,96]{1,0:T(1,128)S(1)}, f32[1,96]{1,0:T(1,128)S(1)...) all-reduce(f32[1,96]{1,0:T(1,128)S(1)} %get-tuple-element.204, ...), channel_id=1, replica_groups=mesh['dp'=4,'fsdp'=8] {'dp'}, use_global_device_ids=true, to_apply=%region_33.0 | all-reduce | flops 2304 | bytes 18432 | tf_op jit(solution)/shard_map/psum | solution.py:117
  832.1 51.2 %reduce-scatter.37.cloned.1.call-done = f32[96,3072]{1,0:T(8,128)} async-done(((f32[768,3072]{1,0:T(8,128)}), f32[96,3072]{1,0:T(8,128)}) %reduce-scatter.37.cloned.1.call-update) | async-done | bytes 1179664 | tf_op jit(solution)/shard_map/reduce_scatter | solution.py:84
  889.0 15.9 %reduce-scatter.55.cloned.1.call-done = bf16[192,96]{1,0:T(8,128)(2,1)} async-done(((bf16[768,96]{1,0:T(8,128)(2,1)}), bf16[192,96]{1,0:T(8,128)(2,1)}) %reduce-scatter.55.cloned.1.call-update) | async-done | bytes 36880
  904.9 14.1 %all_gather.143 = bf16[96,768]{0,1:T(8,128)(2,1)S(1)} all-gather(bf16[96,192]{0,1:T(8,128)(2,1)} %bitcast.346), channel_id=1, replica_groups=mesh['dp'=4,'fsdp'=8] {'dp'}, dimensions={1}, use_global_device_ids=true | all-gather | bytes 184320 | tf_op jit(solution)/shard_map/all_gather | solution.py:107
  919.0 5.6 reduce-scatter.53.cloned.1.call-done
  924.7 14.8 %all_gather.142 = bf16[96,768]{0,1:T(8,128)(2,1)S(1)} all-gather(bf16[96,192]{0,1:T(8,128)(2,1)} %bitcast.347), channel_id=1, replica_groups=mesh['dp'=4,'fsdp'=8] {'dp'}, dimensions={1}, use_global_device_ids=true | all-gather | bytes 184320 | tf_op jit(solution)/shard_map/all_gather | solution.py:107
  940.7 7.3 reduce-scatter.51.cloned.1.call-done
  949.0 18.5 %all-gather.27 = bf16[4,576,96]{1,2,0:T(8,128)(2,1)S(1)} all-gather(bf16[1,576,96]{1,2,0:T(8,128)(2,1)S(1)} %bitcast.338), channel_id=1, replica_groups=mesh['dp'=4,'fsdp'=8] {'dp'}, dimensions={0}, use_global_device_ids=true | all-gather | bytes 552960 | tf_op jit(solution)/shard_map/all_gather | solution.py:104
  968.2 5.1 reduce-scatter.49.cloned.1.call-done
  974.3 15.9 %all-gather.26 = bf16[4,576,96]{1,2,0:T(8,128)(2,1)S(1)} all-gather(bf16[1,576,96]{1,2,0:T(8,128)(2,1)S(1)} %bitcast.339), channel_id=1, replica_groups=mesh['dp'=4,'fsdp'=8] {'dp'}, dimensions={0}, use_global_device_ids=true | all-gather | bytes 552960 | tf_op jit(solution)/shard_map/all_gather | solution.py:104
  990.9 62.3 %reduce-scatter.41.cloned.1.call-done = f32[96,3072]{1,0:T(8,128)} async-done(((f32[768,3072]{1,0:T(8,128)}), f32[96,3072]{1,0:T(8,128)}) %reduce-scatter.41.cloned.1.call-update) | async-done | bytes 1179664 | tf_op jit(solution)/shard_map/reduce_scatter | solution.py:84
  1056.6 20.8 %reduce-scatter.57.cloned.1.call-done = bf16[192,384]{1,0:T(8,128)(2,1)} async-done(((bf16[768,384]{1,0:T(8,128)(2,1)}), bf16[192,384]{1,0:T(8,128)(2,1)}) %reduce-scatter.57.cloned.1.call-update) | async-done | bytes 147472
  1077.5 20.0 %all_gather.146 = bf16[384,768]{0,1:T(8,128)(2,1)S(1)} all-gather(bf16[384,192]{0,1:T(8,128)(2,1)} %bitcast.344), channel_id=1, replica_groups=mesh['dp'=4,'fsdp'=8] {'dp'}, dimensions={1}, use_global_device_ids=true | all-gather | bytes 737280 | tf_op jit(solution)/shard_map/all_gather | solution.py:113
  1097.4 5.0 reduce-scatter.59.cloned.1.call-done
  1102.4 20.4 %all_gather.147 = bf16[384,768]{0,1:T(8,128)(2,1)S(1)} all-gather(bf16[384,192]{0,1:T(8,128)(2,1)} %bitcast.345), channel_id=1, replica_groups=mesh['dp'=4,'fsdp'=8] {'dp'}, dimensions={1}, use_global_device_ids=true | all-gather | bytes 737280 | tf_op jit(solution)/shard_map/all_gather | solution.py:113
  1125.0 3.2 reduce-scatter.39.cloned.1.call-done
  1128.2 19.4 %all_gather.144 = bf16[96,3072]{1,0:T(8,128)(2,1)S(1)} all-gather(bf16[96,768]{1,0:T(8,128)(2,1)} %reduce-scatter.39.cloned.1.call-done), channel_id=1, replica_groups=mesh['dp'=4,'fsdp'=8] {'dp'}, dimensions={1}, use_global_device_ids=true | all-gather | bytes 737280 | tf_op jit(solution)/shard_map/all_gather | solution.py:110
  1147.6 6.3 reduce-scatter.43.cloned.1.call-done
  1153.8 16.5 %all_gather.145 = bf16[96,3072]{1,0:T(8,128)(2,1)S(1)} all-gather(bf16[96,768]{1,0:T(8,128)(2,1)} %reduce-scatter.43.cloned.1.call-done), channel_id=1, replica_groups=mesh['dp'=4,'fsdp'=8] {'dp'}, dimensions={1}, use_global_device_ids=true | all-gather | bytes 737280 | tf_op jit(solution)/shard_map/all_gather | solution.py:110
  (542 shorter events, 168.9 us)
Async XLA Ops:
  7.2 60.2 %all-gather.37.cloned.1.call-start = ((), (), s32[]{:S(2)}) async-start(), calls=%async_computation.26 | async-start | bytes 3981312 | tf_op jit(solution)/shard_map/all_gather | solution.py:41
  9.5 74.1 %all-gather.39.cloned.1.call-start = ((), (), s32[]{:S(2)}) async-start(), calls=%async_computation.27 | async-start | bytes 1327104 | tf_op jit(solution)/shard_map/all_gather | solution.py:44
  10.3 105.2 %all-gather.41.cloned.1.call-start = ((), (), s32[]{:S(2)}) async-start(), calls=%async_computation.28 | async-start | bytes 5308416 | tf_op jit(solution)/shard_map/all_gather | solution.py:48
  11.6 145.2 %all-gather.43.cloned.1.call-start = ((), (), s32[]{:S(2)}) async-start(), calls=%async_computation.29 | async-start | bytes 5308416 | tf_op jit(solution)/shard_map/all_gather | solution.py:50
  12.7 34.6 %copy-start.118 = (bf16[2,384]{1,0:T(2,128)(2,1)S(1)}, bf16[2,384]{1,0:T(2,128)(2,1)}, u32[]{:S(2)}) copy-start(bf16[2,384]{1,0:T(2,128)(2,1)} %param.27) | copy-start | bytes 4612
  12.8 179.7 %all-gather.45.cloned.1.call-start = ((), (), s32[]{:S(2)}) async-start(), calls=%async_computation.30 | async-start | bytes 3981312 | tf_op jit(solution)/shard_map/all_gather | solution.py:41
  13.4 212.7 %all-gather.47.cloned.1.call-start = ((), (), s32[]{:S(2)}) async-start(), calls=%async_computation.31 | async-start | bytes 1327104 | tf_op jit(solution)/shard_map/all_gather | solution.py:44
  13.9 245.8 %all-gather.49.cloned.1.call-start = ((), (), s32[]{:S(2)}) async-start(), calls=%async_computation.32 | async-start | bytes 5308416 | tf_op jit(solution)/shard_map/all_gather | solution.py:48
  14.7 286.4 %all-gather.51.cloned.1.call-start = ((), (), s32[]{:S(2)}) async-start(), calls=%async_computation.33 | async-start | bytes 5308416 | tf_op jit(solution)/shard_map/all_gather | solution.py:50
  15.4 445.7 %reduce-scatter.35.cloned.1.call-start = ((), (), s32[]{:S(2)}) async-start(), calls=%async_computation.19 | async-start | bytes 2654208 | tf_op jit(solution)/shard_map/reduce_scatter | solution.py:80
  15.9 55.2 %copy-start.100 = (f32[345]{0:T(512)}, f32[345]{0:T(512)S(1)}, u32[]{:S(2)}) copy-start(f32[345]{0:T(512)S(1)} %broadcast_multiply_fusion.3) | copy-start | bytes 4144
  16.2 54.9 %copy-start.108 = (f32[345]{0:T(512)}, f32[345]{0:T(512)S(1)}, u32[]{:S(2)}) copy-start(f32[345]{0:T(512)S(1)} %fusion.102) | copy-start | bytes 4144
  16.2 54.8 %copy-start.102 = (f32[345]{0:T(512)}, f32[345]{0:T(512)S(1)}, u32[]{:S(2)}) copy-start(f32[345]{0:T(512)S(1)} %fusion.142) | copy-start | bytes 4144
  47.4 23.7 %copy-start.98 = (f32[768]{0:T(1024)}, f32[768]{0:T(1024)S(1)}, u32[]{:S(2)}) copy-start(f32[768]{0:T(1024)S(1)} %convert_element_type.306) | copy-start | bytes 9220
  47.4 23.6 %copy-start.119 = (f32[768]{0:T(1024)}, f32[768]{0:T(1024)S(1)}, u32[]{:S(2)}) copy-start(f32[768]{0:T(1024)S(1)} %convert_element_type.307) | copy-start | bytes 9220
  47.4 68.0 %copy-start.70 = (f32[768]{0:T(1024)}, f32[768]{0:T(1024)S(1)}, u32[]{:S(2)}) copy-start(f32[768]{0:T(1024)S(1)} %convert_element_type.310) | copy-start | bytes 9220
  47.5 145.0 %copy-start.72 = (f32[768]{0:T(1024)}, f32[768]{0:T(1024)S(1)}, u32[]{:S(2)}) copy-start(f32[768]{0:T(1024)S(1)} %convert_element_type.313) | copy-start | bytes 9220
  83.6 31.9 %copy-start.117 = (f32[1,3072]{1,0:T(1,128)S(1)}, f32[1,3072]{1,0:T(1,128)}, u32[]{:S(2)}) copy-start(f32[1,3072]{1,0:T(1,128)} %convert_element_type.297) | copy-start | bytes 36868
  86.3 44.4 %copy-start.86 = (f32[345]{0:T(512)}, f32[345]{0:T(512)S(1)}, u32[]{:S(2)}) copy-start(f32[345]{0:T(512)S(1)} %broadcast_multiply_fusion.2) | copy-start | bytes 4144
  87.5 43.1 %copy-start.110 = (f32[345]{0:T(512)}, f32[345]{0:T(512)S(1)}, u32[]{:S(2)}) copy-start(f32[345]{0:T(512)S(1)} %multiply_reduce_fusion.12) | copy-start | bytes 4144
  87.5 43.1 %copy-start.95 = (f32[345]{0:T(512)}, f32[345]{0:T(512)S(1)}, u32[]{:S(2)}) copy-start(f32[345]{0:T(512)S(1)} %fusion.143) | copy-start | bytes 4144
  115.5 41.3 %copy-start.121 = (f32[768]{0:T(1024)S(1)}, f32[768]{0:T(1024)}, u32[]{:S(2)}) copy-start(f32[768]{0:T(1024)} %convert_element_type.311) | copy-start | bytes 9220
  156.8 35.7 %copy-start.116 = (f32[2304]{0:T(1024)S(1)}, f32[2304]{0:T(1024)}, u32[]{:S(2)}) copy-start(f32[2304]{0:T(1024)} %get-tuple-element.136) | copy-start | bytes 27652
  162.0 34.4 %copy-start.74 = (f32[345]{0:T(512)}, f32[345]{0:T(512)S(1)}, u32[]{:S(2)}) copy-start(f32[345]{0:T(512)S(1)} %broadcast_multiply_fusion.1) | copy-start | bytes 4144
  163.2 33.2 %copy-start.112 = (f32[345]{0:T(512)}, f32[345]{0:T(512)S(1)}, u32[]{:S(2)}) copy-start(f32[345]{0:T(512)S(1)} %multiply_reduce_fusion.11) | copy-start | bytes 4144
  163.2 33.1 %copy-start.78 = (f32[345]{0:T(512)}, f32[345]{0:T(512)S(1)}, u32[]{:S(2)}) copy-start(f32[345]{0:T(512)S(1)} %fusion.144) | copy-start | bytes 4144
  226.1 5.4 copy-start.82
  301.1 8.7 copy-start.7
  301.1 8.7 copy-start.84
  301.1 8.7 copy-start.93
  301.1 8.7 copy-start.133
  352.2 110.8 %reduce-scatter.33.cloned.1.call-start = ((), (), s32[]{:S(2)}) async-start(), calls=%async_computation.18 | async-start | bytes 2654208 | tf_op jit(solution)/shard_map/reduce_scatter | solution.py:80
  352.3 6.0 copy-start.113
  352.3 6.0 copy-start.10
  358.3 11.3 slice-start
  360.7 12.2 %copy-start.4 = (f32[345,768]{1,0:T(8,128)}, f32[345,768]{1,0:T(8,128)S(1)}, u32[]{:S(2)}) copy-start(f32[345,768]{1,0:T(8,128)S(1)} %get-tuple-element.96) | copy-start | bytes 3179524
  360.7 9.0 copy-start.13
  360.7 9.0 copy-start.87
  360.7 9.0 copy-start.96
  360.7 9.0 slice-start.1
  376.9 133.6 %reduce-scatter.31.cloned.1.call-start = ((), (), s32[]{:S(2)}) async-start(), calls=%async_computation.17 | async-start | bytes 7962624 | tf_op jit(solution)/shard_map/reduce_scatter | solution.py:77
  384.2 195.7 %reduce-scatter.29.cloned.1.call-start = ((), (), s32[]{:S(2)}) async-start(), calls=%async_computation.16 | async-start | bytes 7962624 | tf_op jit(solution)/shard_map/reduce_scatter | solution.py:77
  405.8 7.6 copy-start.36
  405.9 7.6 copy-start.56
  422.8 237.1 %reduce-scatter.45.cloned.1.call-start = ((), (), s32[]{:S(2)}) async-start(), calls=%async_computation.24 | async-start | bytes 10616832 | tf_op jit(solution)/shard_map/reduce_scatter | solution.py:86
  431.9 289.9 %all-reduce.39.cloned.1.call-start = ((), (), s32[]{:S(2)}) async-start(), calls=%async_computation.40 | async-start | bytes 180224
  436.6 4.9 copy-start.109
  436.7 7.3 copy-start.23
  443.9 359.2 %reduce-scatter.47.cloned.1.call-start = ((), (), s32[]{:S(2)}) async-start(), calls=%async_computation.25 | async-start | bytes 10616832 | tf_op jit(solution)/shard_map/reduce_scatter | solution.py:86
  452.1 431.2 %reduce-scatter.37.cloned.1.call-start = ((), (), s32[]{:S(2)}) async-start(), calls=%async_computation.20 | async-start | bytes 10616832 | tf_op jit(solution)/shard_map/reduce_scatter | solution.py:84
  461.1 443.9 %reduce-scatter.55.cloned.1.call-start = ((), (), s32[]{:S(2)}) async-start(), calls=%async_computation.37 | async-start | bytes 245760
  463.0 461.7 %reduce-scatter.53.cloned.1.call-start = ((), (), s32[]{:S(2)}) async-start(), calls=%async_computation.36 | async-start | bytes 245760
  464.9 483.1 %reduce-scatter.51.cloned.1.call-start = ((), (), s32[]{:S(2)}) async-start(), calls=%async_computation.35 | async-start | bytes 737280
  511.8 70.5 %copy-start.8 = (f32[345,768]{1,0:T(8,128)S(1)}, f32[345,768]{1,0:T(8,128)}, u32[]{:S(2)}) copy-start(f32[345,768]{1,0:T(8,128)} %copy-done.6) | copy-start | bytes 3179524
  511.8 70.5 %copy-start.85 = (f32[345]{0:T(512)S(1)}, f32[345]{0:T(512)}, u32[]{:S(2)}) copy-start(f32[345]{0:T(512)} %copy-done.83) | copy-start | bytes 4144
  511.8 70.5 %copy-start.94 = (f32[345]{0:T(512)S(1)}, f32[345]{0:T(512)}, u32[]{:S(2)}) copy-start(f32[345]{0:T(512)} %fusion.145) | copy-start | bytes 4144
  512.9 460.4 %reduce-scatter.49.cloned.1.call-start = ((), (), s32[]{:S(2)}) async-start(), calls=%async_computation.34 | async-start | bytes 737280
  582.2 470.9 %reduce-scatter.41.cloned.1.call-start = ((), (), s32[]{:S(2)}) async-start(), calls=%async_computation.22 | async-start | bytes 10616832 | tf_op jit(solution)/shard_map/reduce_scatter | solution.py:84
  589.2 75.2 %copy-start.16 = (f32[345,768]{1,0:T(8,128)S(1)}, f32[345,768]{1,0:T(8,128)}, u32[]{:S(2)}) copy-start(f32[345,768]{1,0:T(8,128)} %copy-done.15) | copy-start | bytes 3179524
  589.2 75.2 %copy-start.105 = (f32[345]{0:T(512)S(1)}, f32[345]{0:T(512)}, u32[]{:S(2)}) copy-start(f32[345]{0:T(512)} %copy-done.104) | copy-start | bytes 4144
  589.2 488.3 %reduce-scatter.57.cloned.1.call-start = ((), (), s32[]{:S(2)}) async-start(), calls=%async_computation.38 | async-start | bytes 737280
  664.3 438.2 %reduce-scatter.59.cloned.1.call-start = ((), (), s32[]{:S(2)}) async-start(), calls=%async_computation.39 | async-start | bytes 737280
  805.5 322.6 %reduce-scatter.39.cloned.1.call-start = ((), (), s32[]{:S(2)}) async-start(), calls=%async_computation.21 | async-start | bytes 737280 | tf_op jit(solution)/shard_map/reduce_scatter | solution.py:96
  885.6 268.3 %reduce-scatter.43.cloned.1.call-start = ((), (), s32[]{:S(2)}) async-start(), calls=%async_computation.23 | async-start | bytes 737280 | tf_op jit(solution)/shard_map/reduce_scatter | solution.py:96
  (97 other events, 211.4 us)
Sparse Core Ops, SparseCore 0:
  10.5 36.9 all-gather.36
  49.9 24.0 all-gather.38
  76.5 38.9 all-gather.40
  117.8 38.9 all-gather.42
  158.5 33.9 all-gather.44
  194.2 24.0 all-gather.46
  220.8 38.9 all-gather.48
  262.2 38.9 all-gather.50
  352.4 42.4 reduce-scatter.34
  399.0 42.4 reduce-scatter.32
  445.0 65.4 reduce-scatter.30
  514.4 65.5 reduce-scatter.28
  583.4 76.4 reduce-scatter.44
  665.0 56.6 all-reduce.38
  725.5 77.5 reduce-scatter.46
  806.9 76.4 reduce-scatter.36
  885.5 19.3 reduce-scatter.54
  907.0 17.5 reduce-scatter.52
  927.6 20.2 reduce-scatter.50
  950.7 22.4 reduce-scatter.48
  977.2 75.9 reduce-scatter.40
  1055.5 21.8 reduce-scatter.56
  1079.8 22.5 reduce-scatter.58
  1104.7 23.4 reduce-scatter.38
  1131.1 22.6 reduce-scatter.42
where the time goes:
time: 1190 us; the launch traced here: 1180 us
  waiting for transfers between devices  634 us (53%)
  blocking collectives  201 us (17%)
  matrix products  168 us (14%)
  local copies, waits for them, and re-layouts  109 us (9%)
  other arithmetic  46.3 us (4%)
  between operations  18.1 us (2%)
    reduce_scatter x2, waiting for transfers between devices, reduce_grads(): lax.psum_scatter(grads[11], 'fsdp', scatter_dimension=0, tiled=True)  149 us
    reduce_scatter x2, waiting for transfers between devices, reduce_grads(): lax.psum_scatter(grads[9], 'fsdp', scatter_dimension=0, tiled=True)  114 us
    reduce_scatter x2, waiting for transfers between devices, reduce_grads(): lax.psum_scatter(grads[2], 'fsdp', scatter_dimension=0, tiled=True)  112 us
    unnamed x32, waiting for transfers between devices  112 us
    all_gather x2, waiting for transfers between devices, gather_forward(): lax.all_gather(pieces[9], 'fsdp', axis=0, tiled=True)  56.2 us
    all_gather x2, waiting for transfers between devices, gather_forward(): lax.all_gather(pieces[11], 'fsdp', axis=0, tiled=True)  52.5 us
    dot_general x8, matrix products, contract_rows(): lax.dot_general(left, right, (((0,), (0,)), ((), ())), preferred_element_...  47.2 us
    all_gather x2, blocking collectives, reduce_grads(): lax.all_gather(column_parts[3].astype(jnp.bfloat16), 'dp', axis=1, tiled=...  40.4 us
  transfers between devices with their start and end apart: 25, of which 20 were waited for; matrix products, arithmetic and copies ran while one was open for 22% of the time, Pallas kernels for 0%

commit v1 on v0

--- a/solution.py
+++ b/solution.py
@@ -52,52 +52,34 @@
     )
 
 
-def gather_backward(pieces):
-    return (
-        lax.all_gather(pieces[0], "fsdp", axis=0, tiled=True),
-        lax.all_gather(pieces[1], "fsdp", axis=0, tiled=True),
-        lax.all_gather(pieces[2], "fsdp", axis=0, tiled=True),
-        lax.all_gather(pieces[3], "fsdp", axis=0, tiled=True),
-        lax.all_gather(pieces[4], "fsdp", axis=0, tiled=True),
-        lax.all_gather(pieces[5], "fsdp", axis=0, tiled=True),
-        lax.all_gather(pieces[6], "fsdp", axis=0, tiled=True),
-        lax.all_gather(pieces[7], "fsdp", axis=0, tiled=True),
-        lax.all_gather(pieces[8], "fsdp", axis=0, tiled=True),
-        lax.all_gather(pieces[9], "fsdp", axis=0, tiled=True),
-        lax.all_gather(pieces[10], "fsdp", axis=0, tiled=True),
-        lax.all_gather(pieces[11], "fsdp", axis=0, tiled=True),
-        lax.all_gather(pieces[12], "fsdp", axis=0, tiled=True),
-    )
-
-
 def reduce_grads(grads):
     shares = (
         lax.psum_scatter(grads[0], "fsdp", scatter_dimension=0, tiled=True),
         lax.psum_scatter(grads[1], "fsdp", scatter_dimension=0, tiled=True),
-        lax.psum_scatter(grads[2], "fsdp", scatter_dimension=0, tiled=True),
+        lax.psum_scatter(grads[2].astype(jnp.bfloat16), "fsdp", scatter_dimension=0, tiled=True),
         lax.psum_scatter(grads[3], "fsdp", scatter_dimension=0, tiled=True),
         lax.psum_scatter(grads[4], "fsdp", scatter_dimension=0, tiled=True),
-        lax.psum_scatter(grads[5], "fsdp", scatter_dimension=0, tiled=True),
+        lax.psum_scatter(grads[5].astype(jnp.bfloat16), "fsdp", scatter_dimension=0, tiled=True),
         lax.psum_scatter(grads[6], "fsdp", scatter_dimension=0, tiled=True),
         lax.psum_scatter(grads[7], "fsdp", scatter_dimension=0, tiled=True),
         lax.psum_scatter(grads[8], "fsdp", scatter_dimension=0, tiled=True),
-        lax.psum_scatter(grads[9], "fsdp", scatter_dimension=0, tiled=True),
+        lax.psum_scatter(grads[9].astype(jnp.bfloat16), "fsdp", scatter_dimension=0, tiled=True),
         lax.psum_scatter(grads[10], "fsdp", scatter_dimension=0, tiled=True),
-        lax.psum_scatter(grads[11], "fsdp", scatter_dimension=0, tiled=True),
+        lax.psum_scatter(grads[11].astype(jnp.bfloat16), "fsdp", scatter_dimension=0, tiled=True),
         lax.psum_scatter(grads[12], "fsdp", scatter_dimension=0, tiled=True),
     )
     column_parts = (
         lax.psum_scatter(
-            shares[2].astype(jnp.bfloat16), "dp", scatter_dimension=1, tiled=True
+            shares[2], "dp", scatter_dimension=1, tiled=True
         ).astype(jnp.float32),
         lax.psum_scatter(
-            shares[5].astype(jnp.bfloat16), "dp", scatter_dimension=1, tiled=True
+            shares[5], "dp", scatter_dimension=1, tiled=True
         ).astype(jnp.float32),
         lax.psum_scatter(
-            shares[9].astype(jnp.bfloat16), "dp", scatter_dimension=1, tiled=True
+            shares[9], "dp", scatter_dimension=1, tiled=True
         ).astype(jnp.float32),
         lax.psum_scatter(
-            shares[11].astype(jnp.bfloat16), "dp", scatter_dimension=1, tiled=True
+            shares[11], "dp", scatter_dimension=1, tiled=True
         ).astype(jnp.float32),
     )
     matrices = (
@@ -421,8 +403,9 @@
     upstream = cotangent.astype(jnp.float32)
     reduced_layers = [None] * layer_total
     for layer_index in reversed(range(layer_total)):
-        weights = gather_backward(tuple((w[layer_index] for w in shards)))
-        upstream, grads = backward_layer(upstream, weights, saved_layers[layer_index])
+        upstream, grads = backward_layer(
+            upstream, kept_weights[layer_index], saved_layers[layer_index]
+        )
         reduced_layers[layer_index] = reduce_grads(grads)
     stacked = tuple(
         (

time: 1190 us -> 1030 us (0.87)
  waiting for transfers between devices: 634 us -> 497 us
  other arithmetic: 46.3 us -> 31.5 us
    reduce_scatter x10, waiting for transfers between devices: 384 us -> 239 us  [the longest x2 104 us: reduce_grads(): lax.psum_scatter(grads[11].astype(jnp.bfloat16), 'fsdp', scatter_dimensio...]
    convert_element_type x8 -> x0, other arithmetic: 12.2 us -> none  [the longest x2 4.33 us: reduce_grads(): shares[9].astype(jnp.bfloat16)]
  transfers between devices with their start and end apart: 25 -> 25, of which waited for: 20 -> 20; matrix products, arithmetic and copies ran while one was open for 22% -> 25% of each run, Pallas kernels for 0% -> 0%
where the time goes in v1:
time: 1030 us; the launch traced here: 1020 us
  waiting for transfers between devices  497 us (48%)
  blocking collectives  202 us (20%)
  matrix products  160 us (16%)
  local copies, waits for them, and re-layouts  115 us (11%)
  other arithmetic  31.5 us (3%)
  between operations  18.1 us (2%)
    unnamed x32, waiting for transfers between devices  119 us
    reduce_scatter x2, waiting for transfers between devices, reduce_grads(): lax.psum_scatter(grads[11].astype(jnp.bfloat16), 'fsdp', scatter_dimensio...  104 us
    reduce_scatter x2, waiting for transfers between devices, reduce_grads(): lax.psum_scatter(grads[9].astype(jnp.bfloat16), 'fsdp', scatter_dimension...  68.8 us
    all_gather x2, waiting for transfers between devices, gather_forward(): lax.all_gather(pieces[9], 'fsdp', axis=0, tiled=True)  57.5 us
    reduce_scatter x2, waiting for transfers between devices, reduce_grads(): lax.psum_scatter(grads[2].astype(jnp.bfloat16), 'fsdp', scatter_dimension...  56.7 us
    all_gather x2, waiting for transfers between devices, gather_forward(): lax.all_gather(pieces[11], 'fsdp', axis=0, tiled=True)  52.1 us
    all_gather x2, blocking collectives, reduce_grads(): lax.all_gather(column_parts[3].astype(jnp.bfloat16), 'dp', axis=1, tiled=...  40 us
    dot_general x8, matrix products, contract_rows(): lax.dot_general(left, right, (((0,), (0,)), ((), ())), preferred_element_...  39.5 us
  transfers between devices with their start and end apart: 25, of which 20 were waited for; matrix products, arithmetic and copies ran while one was open for 25% of the time, Pallas kernels for 0%

profile of v1, /device:TPU:0, one launch (start us, length us, event | category | flops | bytes accessed | tf_op | source)
XLA Modules:
  0.0 1024.6 jit_solution(16430635094293452343)
XLA Ops:
  7.2 2.2 fusion.171
  20.8 26.0 %all-reduce.36 = (bf16[768]{0:T(1024)(128)(2,1)S(1)}, bf16[768]{0:T(1024)(128)(2,1)S(1)}, bf16[768]{0:T(1024)(128)(2,1)S(1)}, bf16[768]{0:T(1024)(128)(2,1)S(1)}...) all-reduce(bf16[768]{0:T(1024)(128)(2,1)S(1)} %dynamic-update-slice, ...), channel_id=8, replica_groups=mesh['dp'=4,'fsdp'=8] {'fsdp'}, use_global_device_ids=true, to_apply=%add.4 | all-reduce | flops 12288 | bytes 49152
  48.7 8.5 all-gather.23
  57.7 8.8 all-gather.10
  66.6 3.7 fusion.34
  82.9 2.7 fusion.178
  86.9 28.6 %all-gather.41.cloned.1.call-done = bf16[1,768,3072]{2,1,0:T(8,128)(2,1)} async-done(((bf16[1,96,3072]{2,1,0:T(8,128)(2,1)}), bf16[1,768,3072]{2,1,0:T(8,128)(2,1)}) %all-gather.41.cloned.1.call-update) | async-done | bytes 4718608 | tf_op jit(solution)/shard_map/all_gather | solution.py:48
  115.5 14.9 %multiply_convert_fusion.1 = (bf16[345,3072]{1,0:T(8,128)(2,1)}, f32[345,3072]{1,0:T(8,128)}, f32[345,3072]{1,0:T(8,128)}) fusion(f32[3072]{0:T(1024)S(1)} %bitcast.347, bf16[1,768,3072]{2,1,0:T(8,128)(2,1)} %all-gather.41.cloned.1.call-done, f32[345,768]{1,0:T(8,128)} %copy-done.22, f32[768]{0:T(1024)S(1)} %convert_element_type.310, ...), kind=kOutput, calls=%fused_computation.45 | convolution fusion | flops 1699188480 | bytes 16398024 | tf_op jit(solution)/shard_map/dot_general | solution.py:243
  130.4 26.4 %all-gather.43.cloned.1.call-done = bf16[1,3072,768]{2,1,0:T(8,128)(2,1)} async-done(((bf16[1,384,768]{2,1,0:T(8,128)(2,1)}), bf16[1,3072,768]{2,1,0:T(8,128)(2,1)}) %all-gather.43.cloned.1.call-update) | async-done | bytes 4718608 | tf_op jit(solution)/shard_map/all_gather | solution.py:50
  156.8 5.2 fusion.179
  163.3 29.2 %all-gather.45.cloned.1.call-done = bf16[1,768,2304]{2,1,0:T(8,128)(2,1)} async-done(((bf16[1,96,2304]{2,1,0:T(8,128)(2,1)}), bf16[1,768,2304]{2,1,0:T(8,128)(2,1)}) %all-gather.45.cloned.1.call-update) | async-done | bytes 3538960 | tf_op jit(solution)/shard_map/all_gather | solution.py:41
  192.5 3.9 fusion.35
  200.4 2.2 fusion.166
  210.7 2.2 reshape.519
  216.8 2.2 copy.193
  219.0 2.4 reshape.691
  226.1 2.9 fusion.181
  230.9 28.9 %all-gather.49.cloned.1.call-done = bf16[1,768,3072]{2,1,0:T(8,128)(2,1)} async-done(((bf16[1,96,3072]{2,1,0:T(8,128)(2,1)}), bf16[1,768,3072]{2,1,0:T(8,128)(2,1)}) %all-gather.49.cloned.1.call-update) | async-done | bytes 4718608 | tf_op jit(solution)/shard_map/all_gather | solution.py:48
  259.8 15.1 %multiply_convert_fusion = (bf16[345,3072]{1,0:T(8,128)(2,1)}, f32[345,3072]{1,0:T(8,128)}, f32[345,3072]{1,0:T(8,128)}) fusion(f32[3072]{0:T(1024)} %bitcast.346, bf16[1,768,3072]{2,1,0:T(8,128)(2,1)} %all-gather.49.cloned.1.call-done, f32[345,768]{1,0:T(8,128)} %copy-done.10, f32[768]{0:T(1024)} %convert_element_type.316, f32[768]{0:T(1024)} %convert_element_type.315, ...), kind=kOutput, calls=%fused_computation.32 | convolution fusion | flops 1699188480 | bytes 16398024 | tf_op jit(solution)/shard_map/dot_general | solution.py:243
  274.9 25.7 %all-gather.51.cloned.1.call-done = bf16[1,3072,768]{2,1,0:T(8,128)(2,1)} async-done(((bf16[1,384,768]{2,1,0:T(8,128)(2,1)}), bf16[1,3072,768]{2,1,0:T(8,128)(2,1)}) %all-gather.51.cloned.1.call-update) | async-done | bytes 4718608 | tf_op jit(solution)/shard_map/all_gather | solution.py:50
  300.7 8.7 convert_reduce_fusion
  309.4 2.6 multiply_reduce_fusion.4
  320.1 2.2 multiply_reduce_fusion.14
  328.1 3.3 convolution_convert_fusion.15
  341.8 2.2 reshape.528
  350.2 2.3 copy.157
  352.5 6.0 multiply_reduce_fusion.6
  360.8 8.5 convert_reduce_fusion.1
  369.4 2.6 multiply_reduce_fusion.5
  376.3 6.2 convolution_convert_fusion.4
  408.7 2.3 copy.171
  415.1 4.3 convolution_convert_fusion.5
  420.6 6.6 convolution_convert_fusion.1
  428.7 2.3 convert_reduce_fusion.2
  432.2 4.8 fusion.157
  439.5 6.4 convolution_convert_fusion
  447.1 6.2 convolution_convert_fusion.2
  457.2 7.6 reduce-scatter.31.cloned.1.call-done
  467.1 49.1 %reduce-scatter.29.cloned.1.call-done = bf16[96,2304]{1,0:T(8,128)(2,1)} async-done(((bf16[768,2304]{1,0:T(8,128)(2,1)}), bf16[96,2304]{1,0:T(8,128)(2,1)}) %reduce-scatter.29.cloned.1.call-update) | async-done | bytes 442384 | tf_op jit(solution)/shard_map/reduce_scatter | solution.py:59
  518.4 6.1 convolution_convert_fusion.3
  526.1 47.5 %reduce-scatter.45.cloned.1.call-done = bf16[384,768]{1,0:T(8,128)(2,1)} async-done(((bf16[3072,768]{1,0:T(8,128)(2,1)}), bf16[384,768]{1,0:T(8,128)(2,1)}) %reduce-scatter.45.cloned.1.call-update) | async-done | bytes 589840 | tf_op jit(solution)/shard_map/reduce_scatter | solution.py:68
  575.9 3.0 add_add_fusion.4
  578.9 5.0 fusion.68
  583.9 52.4 %all-reduce.39.cloned.1.call-done = (f32[768]{0:T(1024)}, f32[768]{0:T(1024)}, f32[768]{0:T(1024)}, f32[768]{0:T(1024)}, f32[768]{0:T(1024)}, /*index=5*/f32[768...) async-done(((f32[768]{0:T(1024)}, f32[768]{0:T(1024)}, ...) | async-done | bytes 73744
  637.8 56.7 %reduce-scatter.47.cloned.1.call-done = bf16[384,768]{1,0:T(8,128)(2,1)} async-done(((bf16[3072,768]{1,0:T(8,128)(2,1)}), bf16[384,768]{1,0:T(8,128)(2,1)}) %reduce-scatter.47.cloned.1.call-update) | async-done | bytes 589840 | tf_op jit(solution)/shard_map/reduce_scatter | solution.py:68
  702.8 18.8 %all-reduce.35 = (f32[1,96]{1,0:T(1,128)S(1)}, f32[1,96]{1,0:T(1,128)S(1)}, f32[1,96]{1,0:T(1,128)S(1)}, f32[1,96]{1,0:T(1,128)S(1)}, f32[1,96]{1,0:T(1,128)S(1)...) all-reduce(f32[1,96]{1,0:T(1,128)S(1)} %get-tuple-element.204, ...), channel_id=1, replica_groups=mesh['dp'=4,'fsdp'=8] {'dp'}, use_global_device_ids=true, to_apply=%region_33.0 | all-reduce | flops 2304 | bytes 18432 | tf_op jit(solution)/shard_map/psum | solution.py:99
  723.3 28.9 %reduce-scatter.41.cloned.1.call-done = bf16[96,3072]{1,0:T(8,128)(2,1)} async-done(((bf16[768,3072]{1,0:T(8,128)(2,1)}), bf16[96,3072]{1,0:T(8,128)(2,1)}) %reduce-scatter.41.cloned.1.call-update) | async-done | bytes 589840 | tf_op jit(solution)/shard_map/reduce_scatter | solution.py:66
  755.7 18.6 %reduce-scatter.55.cloned.1.call-done = bf16[192,96]{1,0:T(8,128)(2,1)} async-done(((bf16[768,96]{1,0:T(8,128)(2,1)}), bf16[192,96]{1,0:T(8,128)(2,1)}) %reduce-scatter.55.cloned.1.call-update) | async-done | bytes 36880
  774.2 14.1 %all_gather.131 = bf16[96,768]{0,1:T(8,128)(2,1)S(1)} all-gather(bf16[96,192]{0,1:T(8,128)(2,1)} %bitcast.344), channel_id=1, replica_groups=mesh['dp'=4,'fsdp'=8] {'dp'}, dimensions={1}, use_global_device_ids=true | all-gather | bytes 184320 | tf_op jit(solution)/shard_map/all_gather | solution.py:89
  788.3 5.7 reduce-scatter.53.cloned.1.call-done
  794.1 14.7 %all_gather.130 = bf16[96,768]{0,1:T(8,128)(2,1)S(1)} all-gather(bf16[96,192]{0,1:T(8,128)(2,1)} %bitcast.345), channel_id=1, replica_groups=mesh['dp'=4,'fsdp'=8] {'dp'}, dimensions={1}, use_global_device_ids=true | all-gather | bytes 184320 | tf_op jit(solution)/shard_map/all_gather | solution.py:89
  810.0 7.2 reduce-scatter.51.cloned.1.call-done
  818.2 18.6 %all-gather.27 = bf16[4,576,96]{1,2,0:T(8,128)(2,1)S(1)} all-gather(bf16[1,576,96]{1,2,0:T(8,128)(2,1)S(1)} %bitcast.336), channel_id=1, replica_groups=mesh['dp'=4,'fsdp'=8] {'dp'}, dimensions={0}, use_global_device_ids=true | all-gather | bytes 552960 | tf_op jit(solution)/shard_map/all_gather | solution.py:86
  837.6 4.1 reduce-scatter.49.cloned.1.call-done
  842.7 15.6 %all-gather.26 = bf16[4,576,96]{1,2,0:T(8,128)(2,1)S(1)} all-gather(bf16[1,576,96]{1,2,0:T(8,128)(2,1)S(1)} %bitcast.337), channel_id=1, replica_groups=mesh['dp'=4,'fsdp'=8] {'dp'}, dimensions={0}, use_global_device_ids=true | all-gather | bytes 552960 | tf_op jit(solution)/shard_map/all_gather | solution.py:86
  859.0 39.9 %reduce-scatter.37.cloned.1.call-done = bf16[96,3072]{1,0:T(8,128)(2,1)} async-done(((bf16[768,3072]{1,0:T(8,128)(2,1)}), bf16[96,3072]{1,0:T(8,128)(2,1)}) %reduce-scatter.37.cloned.1.call-update) | async-done | bytes 589840 | tf_op jit(solution)/shard_map/reduce_scatter | solution.py:66
  900.3 23.1 %reduce-scatter.57.cloned.1.call-done = bf16[192,384]{1,0:T(8,128)(2,1)} async-done(((bf16[768,384]{1,0:T(8,128)(2,1)}), bf16[192,384]{1,0:T(8,128)(2,1)}) %reduce-scatter.57.cloned.1.call-update) | async-done | bytes 147472
  923.4 19.9 %all_gather.134 = bf16[384,768]{0,1:T(8,128)(2,1)S(1)} all-gather(bf16[384,192]{0,1:T(8,128)(2,1)} %bitcast.342), channel_id=1, replica_groups=mesh['dp'=4,'fsdp'=8] {'dp'}, dimensions={1}, use_global_device_ids=true | all-gather | bytes 737280 | tf_op jit(solution)/shard_map/all_gather | solution.py:95
  943.3 5.4 reduce-scatter.59.cloned.1.call-done
  948.7 20.1 %all_gather.135 = bf16[384,768]{0,1:T(8,128)(2,1)S(1)} all-gather(bf16[384,192]{0,1:T(8,128)(2,1)} %bitcast.343), channel_id=1, replica_groups=mesh['dp'=4,'fsdp'=8] {'dp'}, dimensions={1}, use_global_device_ids=true | all-gather | bytes 737280 | tf_op jit(solution)/shard_map/all_gather | solution.py:95
  971.0 3.3 reduce-scatter.43.cloned.1.call-done
  974.2 20.2 %all_gather.133 = bf16[96,3072]{1,0:T(8,128)(2,1)S(1)} all-gather(bf16[96,768]{1,0:T(8,128)(2,1)} %reduce-scatter.43.cloned.1.call-done), channel_id=1, replica_groups=mesh['dp'=4,'fsdp'=8] {'dp'}, dimensions={1}, use_global_device_ids=true | all-gather | bytes 737280 | tf_op jit(solution)/shard_map/all_gather | solution.py:92
  994.5 5.5 reduce-scatter.39.cloned.1.call-done
  999.9 16.4 %all_gather.132 = bf16[96,3072]{1,0:T(8,128)(2,1)S(1)} all-gather(bf16[96,768]{1,0:T(8,128)(2,1)} %reduce-scatter.39.cloned.1.call-done), channel_id=1, replica_groups=mesh['dp'=4,'fsdp'=8] {'dp'}, dimensions={1}, use_global_device_ids=true | all-gather | bytes 737280 | tf_op jit(solution)/shard_map/all_gather | solution.py:92
  (534 shorter events, 159.7 us)
Async XLA Ops:
  7.2 59.4 %all-gather.37.cloned.1.call-start = ((), (), s32[]{:S(2)}) async-start(), calls=%async_computation.26 | async-start | bytes 3981312 | tf_op jit(solution)/shard_map/all_gather | solution.py:41
  9.5 73.4 %all-gather.39.cloned.1.call-start = ((), (), s32[]{:S(2)}) async-start(), calls=%async_computation.27 | async-start | bytes 1327104 | tf_op jit(solution)/shard_map/all_gather | solution.py:44
  10.3 105.2 %all-gather.41.cloned.1.call-start = ((), (), s32[]{:S(2)}) async-start(), calls=%async_computation.28 | async-start | bytes 5308416 | tf_op jit(solution)/shard_map/all_gather | solution.py:48
  11.6 145.2 %all-gather.43.cloned.1.call-start = ((), (), s32[]{:S(2)}) async-start(), calls=%async_computation.29 | async-start | bytes 5308416 | tf_op jit(solution)/shard_map/all_gather | solution.py:50
  12.7 34.6 %copy-start.111 = (bf16[2,384]{1,0:T(2,128)(2,1)S(1)}, bf16[2,384]{1,0:T(2,128)(2,1)}, u32[]{:S(2)}) copy-start(bf16[2,384]{1,0:T(2,128)(2,1)} %param.27) | copy-start | bytes 4612
  12.8 179.8 %all-gather.45.cloned.1.call-start = ((), (), s32[]{:S(2)}) async-start(), calls=%async_computation.30 | async-start | bytes 3981312 | tf_op jit(solution)/shard_map/all_gather | solution.py:41
  13.4 212.7 %all-gather.47.cloned.1.call-start = ((), (), s32[]{:S(2)}) async-start(), calls=%async_computation.31 | async-start | bytes 1327104 | tf_op jit(solution)/shard_map/all_gather | solution.py:44
  13.9 245.8 %all-gather.49.cloned.1.call-start = ((), (), s32[]{:S(2)}) async-start(), calls=%async_computation.32 | async-start | bytes 5308416 | tf_op jit(solution)/shard_map/all_gather | solution.py:48
  14.7 286.0 %all-gather.51.cloned.1.call-start = ((), (), s32[]{:S(2)}) async-start(), calls=%async_computation.33 | async-start | bytes 5308416 | tf_op jit(solution)/shard_map/all_gather | solution.py:50
  15.4 438.1 %reduce-scatter.35.cloned.1.call-start = ((), (), s32[]{:S(2)}) async-start(), calls=%async_computation.19 | async-start | bytes 1327104 | tf_op jit(solution)/shard_map/reduce_scatter | solution.py:62
  15.9 54.4 %copy-start.72 = (f32[345]{0:T(512)}, f32[345]{0:T(512)S(1)}, u32[]{:S(2)}) copy-start(f32[345]{0:T(512)S(1)} %broadcast_multiply_fusion.3) | copy-start | bytes 4144
  16.2 31.2 %copy-start.88 = (f32[345]{0:T(512)}, f32[345]{0:T(512)S(1)}, u32[]{:S(2)}) copy-start(f32[345]{0:T(512)S(1)} %fusion.102) | copy-start | bytes 4144
  16.2 54.1 %copy-start.74 = (f32[345]{0:T(512)}, f32[345]{0:T(512)S(1)}, u32[]{:S(2)}) copy-start(f32[345]{0:T(512)S(1)} %fusion.140) | copy-start | bytes 4144
  47.4 22.9 %copy-start.70 = (f32[768]{0:T(1024)}, f32[768]{0:T(1024)S(1)}, u32[]{:S(2)}) copy-start(f32[768]{0:T(1024)S(1)} %convert_element_type.306) | copy-start | bytes 9220
  47.4 68.1 %copy-start.96 = (f32[768]{0:T(1024)}, f32[768]{0:T(1024)S(1)}, u32[]{:S(2)}) copy-start(f32[768]{0:T(1024)S(1)} %convert_element_type.309) | copy-start | bytes 9220
  47.4 145.1 %copy-start.101 = (f32[768]{0:T(1024)}, f32[768]{0:T(1024)S(1)}, u32[]{:S(2)}) copy-start(f32[768]{0:T(1024)S(1)} %convert_element_type.312) | copy-start | bytes 9220
  48.0 22.2 %copy-start.115 = (f32[768]{0:T(1024)}, f32[768]{0:T(1024)S(1)}, u32[]{:S(2)}) copy-start(f32[768]{0:T(1024)S(1)} %convert_element_type.307) | copy-start | bytes 9220
  48.0 67.5 %copy-start.112 = (f32[768]{0:T(1024)}, f32[768]{0:T(1024)S(1)}, u32[]{:S(2)}) copy-start(f32[768]{0:T(1024)S(1)} %convert_element_type.310) | copy-start | bytes 9220
  48.1 144.5 %copy-start.117 = (f32[768]{0:T(1024)}, f32[768]{0:T(1024)S(1)}, u32[]{:S(2)}) copy-start(f32[768]{0:T(1024)S(1)} %convert_element_type.313) | copy-start | bytes 9220
  85.6 44.8 %copy-start.78 = (f32[345]{0:T(512)}, f32[345]{0:T(512)S(1)}, u32[]{:S(2)}) copy-start(f32[345]{0:T(512)S(1)} %broadcast_multiply_fusion.2) | copy-start | bytes 4144
  86.9 43.6 %copy-start.90 = (f32[345]{0:T(512)}, f32[345]{0:T(512)S(1)}, u32[]{:S(2)}) copy-start(f32[345]{0:T(512)S(1)} %multiply_reduce_fusion.12) | copy-start | bytes 4144
  86.9 43.6 %copy-start.103 = (f32[345]{0:T(512)}, f32[345]{0:T(512)S(1)}, u32[]{:S(2)}) copy-start(f32[345]{0:T(512)S(1)} %fusion.141) | copy-start | bytes 4144
  162.0 34.4 %copy-start.84 = (f32[345]{0:T(512)}, f32[345]{0:T(512)S(1)}, u32[]{:S(2)}) copy-start(f32[345]{0:T(512)S(1)} %broadcast_multiply_fusion.1) | copy-start | bytes 4144
  163.3 33.1 %copy-start.92 = (f32[345]{0:T(512)}, f32[345]{0:T(512)S(1)}, u32[]{:S(2)}) copy-start(f32[345]{0:T(512)S(1)} %multiply_reduce_fusion.11) | copy-start | bytes 4144
  163.3 33.1 %copy-start.108 = (f32[345]{0:T(512)}, f32[345]{0:T(512)S(1)}, u32[]{:S(2)}) copy-start(f32[345]{0:T(512)S(1)} %fusion.142) | copy-start | bytes 4144
  300.7 8.7 copy-start.11
  300.7 8.7 copy-start.82
  300.7 8.7 copy-start.99
  300.7 8.7 copy-start.106
  300.7 8.7 copy-start.129
  335.6 119.8 %reduce-scatter.33.cloned.1.call-start = ((), (), s32[]{:S(2)}) async-start(), calls=%async_computation.18 | async-start | bytes 1327104 | tf_op jit(solution)/shard_map/reduce_scatter | solution.py:62
  344.0 8.5 copy-start.102
  344.0 8.5 copy-start.109
  358.5 10.8 %slice-start = ((s8[4718592]{0:T(1024)(128)(4,1)}), s8[4194304]{0:T(1024)(128)(4,1)S(1)}, s32[]{:S(2)}) async-start(s8[4718592]{0:T(1024)(128)(4,1)} %bitcast.348), calls=%async_computation.41 | async-start | bytes 8388608
  360.8 11.8 %copy-start.4 = (f32[345,768]{1,0:T(8,128)}, f32[345,768]{1,0:T(8,128)S(1)}, u32[]{:S(2)}) copy-start(f32[345,768]{1,0:T(8,128)S(1)} %get-tuple-element.96) | copy-start | bytes 3179524
  360.8 8.6 copy-start.23
  360.8 8.6 copy-start.79
  360.8 8.6 copy-start.97
  360.8 8.6 copy-start.104
  360.8 8.6 slice-start.1
  376.2 88.6 %reduce-scatter.31.cloned.1.call-start = ((), (), s32[]{:S(2)}) async-start(), calls=%async_computation.17 | async-start | bytes 3981312 | tf_op jit(solution)/shard_map/reduce_scatter | solution.py:59
  382.5 133.7 %reduce-scatter.29.cloned.1.call-start = ((), (), s32[]{:S(2)}) async-start(), calls=%async_computation.16 | async-start | bytes 3981312 | tf_op jit(solution)/shard_map/reduce_scatter | solution.py:59
  419.4 154.2 %reduce-scatter.45.cloned.1.call-start = ((), (), s32[]{:S(2)}) async-start(), calls=%async_computation.24 | async-start | bytes 5308416 | tf_op jit(solution)/shard_map/reduce_scatter | solution.py:68
  427.2 209.0 %all-reduce.39.cloned.1.call-start = ((), (), s32[]{:S(2)}) async-start(), calls=%async_computation.40 | async-start | bytes 180224
  437.0 8.9 copy-start.21
  439.4 255.1 %reduce-scatter.47.cloned.1.call-start = ((), (), s32[]{:S(2)}) async-start(), calls=%async_computation.25 | async-start | bytes 5308416 | tf_op jit(solution)/shard_map/reduce_scatter | solution.py:68
  445.9 306.2 %reduce-scatter.41.cloned.1.call-start = ((), (), s32[]{:S(2)}) async-start(), calls=%async_computation.22 | async-start | bytes 5308416 | tf_op jit(solution)/shard_map/reduce_scatter | solution.py:66
  453.4 65.0 %copy-start.24 = (f32[345,768]{1,0:T(8,128)S(1)}, f32[345,768]{1,0:T(8,128)}, u32[]{:S(2)}) copy-start(f32[345,768]{1,0:T(8,128)} %copy-done.22) | copy-start | bytes 3179524
  453.4 65.0 %copy-start.80 = (f32[345]{0:T(512)S(1)}, f32[345]{0:T(512)}, u32[]{:S(2)}) copy-start(f32[345]{0:T(512)} %copy-done.78) | copy-start | bytes 4144
  453.4 65.0 %copy-start.98 = (f32[768]{0:T(1024)S(1)}, f32[768]{0:T(1024)}, u32[]{:S(2)}) copy-start(f32[768]{0:T(1024)} %copy-done.96) | copy-start | bytes 9220
  453.4 65.0 %copy-start.105 = (f32[345]{0:T(512)S(1)}, f32[345]{0:T(512)}, u32[]{:S(2)}) copy-start(f32[345]{0:T(512)} %copy-done.103) | copy-start | bytes 4144
  453.4 65.0 %copy-start.113 = (f32[768]{0:T(1024)S(1)}, f32[768]{0:T(1024)}, u32[]{:S(2)}) copy-start(f32[768]{0:T(1024)} %copy-done.112) | copy-start | bytes 9220
  453.4 320.8 %reduce-scatter.55.cloned.1.call-start = ((), (), s32[]{:S(2)}) async-start(), calls=%async_computation.37 | async-start | bytes 245760
  455.3 338.7 %reduce-scatter.53.cloned.1.call-start = ((), (), s32[]{:S(2)}) async-start(), calls=%async_computation.36 | async-start | bytes 245760
  457.1 360.0 %reduce-scatter.51.cloned.1.call-start = ((), (), s32[]{:S(2)}) async-start(), calls=%async_computation.35 | async-start | bytes 737280
  466.9 374.8 %reduce-scatter.49.cloned.1.call-start = ((), (), s32[]{:S(2)}) async-start(), calls=%async_computation.34 | async-start | bytes 737280
  518.3 380.6 %reduce-scatter.37.cloned.1.call-start = ((), (), s32[]{:S(2)}) async-start(), calls=%async_computation.20 | async-start | bytes 5308416 | tf_op jit(solution)/shard_map/reduce_scatter | solution.py:66
  524.6 51.3 %copy-start.110 = (f32[345]{0:T(512)S(1)}, f32[345]{0:T(512)}, u32[]{:S(2)}) copy-start(f32[345]{0:T(512)} %get-tuple-element.37) | copy-start | bytes 4144
  524.6 51.3 %copy-start.7 = (f32[345,768]{1,0:T(8,128)S(1)}, f32[345,768]{1,0:T(8,128)}, u32[]{:S(2)}) copy-start(f32[345,768]{1,0:T(8,128)} %copy-done.6) | copy-start | bytes 3179524
  524.6 51.3 %copy-start.77 = (f32[345]{0:T(512)S(1)}, f32[345]{0:T(512)}, u32[]{:S(2)}) copy-start(f32[345]{0:T(512)} %copy-done.76) | copy-start | bytes 4144
  524.6 398.8 %reduce-scatter.57.cloned.1.call-start = ((), (), s32[]{:S(2)}) async-start(), calls=%async_computation.38 | async-start | bytes 737280
  575.8 372.9 %reduce-scatter.59.cloned.1.call-start = ((), (), s32[]{:S(2)}) async-start(), calls=%async_computation.39 | async-start | bytes 737280
  696.7 277.6 %reduce-scatter.43.cloned.1.call-start = ((), (), s32[]{:S(2)}) async-start(), calls=%async_computation.23 | async-start | bytes 737280 | tf_op jit(solution)/shard_map/reduce_scatter | solution.py:78
  752.2 247.8 %reduce-scatter.39.cloned.1.call-start = ((), (), s32[]{:S(2)}) async-start(), calls=%async_computation.21 | async-start | bytes 737280 | tf_op jit(solution)/shard_map/reduce_scatter | solution.py:78
  (97 other events, 240.4 us)
Sparse Core Ops, SparseCore 0:
  10.5 36.9 all-gather.36
  49.9 24.0 all-gather.38
  76.5 38.9 all-gather.40
  117.8 38.9 all-gather.42
  158.5 33.9 all-gather.44
  194.3 24.0 all-gather.46
  220.8 38.9 all-gather.48
  261.7 38.9 all-gather.50
  335.7 36.7 reduce-scatter.34
  376.4 36.7 reduce-scatter.32
  416.7 48.0 reduce-scatter.30
  468.1 48.0 reduce-scatter.28
  519.7 53.8 reduce-scatter.44
  579.5 56.6 all-reduce.38
  639.6 54.9 reduce-scatter.46
  698.2 53.8 reduce-scatter.40
  754.8 19.3 reduce-scatter.54
  776.4 17.5 reduce-scatter.52
  796.9 20.2 reduce-scatter.50
  819.3 22.3 reduce-scatter.48
  845.1 53.7 reduce-scatter.36
  901.3 21.9 reduce-scatter.56
  926.3 22.3 reduce-scatter.58
  951.0 23.2 reduce-scatter.42
  976.6 23.2 reduce-scatter.38

commit v2 on v1

--- a/solution.py
+++ b/solution.py
@@ -1,6 +1,10 @@
+import functools
+
 import jax
 import jax.numpy as jnp
 from jax import lax
+from jax.experimental import pallas as pl
+from jax.experimental.pallas import tpu as pltpu
 from jax.sharding import PartitionSpec as P
 
 D = 768
@@ -434,6 +438,885 @@
     )
 
 
+VMEM_BYTES = 63 * 1024 * 1024
+
+MESH = pl.DeviceIdType.MESH
+F32 = jnp.float32
+BF16 = jnp.bfloat16
+
+FF = 3072
+ROWS = 345
+PAD = 352
+STEP = 32
+SHARD = 96
+HALF = 48
+UNITS = 12
+LAYER_ROWS = UNITS * D
+DOWN_AT = 8 * D
+SLOTS = 3
+TOP_ROWS = 208
+KEYS = 256
+LOW_KEY = PAD - KEYS
+LOW_ROWS = PAD - TOP_ROWS
+V_G1, V_B1, V_QB, V_VB, V_OB, V_G2, V_B2, V_DB, V_UB = range(9)
+
+
+def nt(left, right):
+    return lax.dot_general(left, right, (((1,), (1,)), ((), ())), preferred_element_type=F32)
+
+
+def tn(left, right):
+    return lax.dot_general(left, right, (((0,), (0,)), ((), ())), preferred_element_type=F32)
+
+
+def nn(left, right):
+    return lax.dot_general(left, right, (((1,), (0,)), ((), ())), preferred_element_type=F32)
+
+
+def aligned(value, by):
+    return value if isinstance(value, int) else pl.multiple_of(value, by)
+
+
+def unit_row(layer, unit, owner):
+    is_down = unit // 8 if isinstance(unit, int) else lax.div(unit, 8)
+    plain = unit * D + owner * SHARD
+    down = DOWN_AT + owner * (4 * SHARD) + (unit - 8) * SHARD
+    return aligned(layer * LAYER_ROWS + (1 - is_down) * plain + is_down * down, 16)
+
+
+def forward_unit(index):
+    return lax.div(index, UNITS), lax.rem(index, UNITS)
+
+
+def backward_unit(layers, index):
+    turn, place = lax.div(index, UNITS), lax.rem(index, UNITS)
+    part = lax.div(place, 4)
+    is_down, is_late = lax.div(2 - part, 2), lax.div(part, 2)
+    unit = (
+        is_down * (8 + place)
+        + (1 - is_down - is_late) * place
+        + is_late * lax.rem(place + 3, 4)
+    )
+    return layers - 1 - turn, unit
+
+
+def stats(x):
+    mean = jnp.mean(x, axis=-1, keepdims=True)
+    centred = x - mean
+    scale = lax.rsqrt(jnp.mean(centred * centred, axis=-1, keepdims=True) + epsilon)
+    return centred * scale, scale
+
+
+def fold(x):
+    return jnp.sum(x.reshape(x.shape[0] // 8, 8, x.shape[1]), axis=0)
+
+
+def total(x):
+    return jnp.sum(x, axis=0, keepdims=True)
+
+
+def step_rows(step):
+    return pl.ds(aligned(step * STEP, STEP), STEP)
+
+
+def encoder_kernel(
+    layers,
+    tokens,
+    cotangent,
+    vec_shard,
+    w_qkv,
+    w_out,
+    w_up,
+    w_down,
+    encoded,
+    tokens_grad,
+    g_vec,
+    g_qkv,
+    g_out,
+    g_up,
+    g_down,
+    wb,
+    xs,
+    x1,
+    nr,
+    pj,
+    mx,
+    n2,
+    hd,
+    gp,
+    lse,
+    gb,
+    gm,
+    br,
+    acc,
+    kacc,
+    vacc,
+    mask_top,
+    mask_low,
+    vsg,
+    vec,
+    ubs,
+    vr,
+    rc,
+    r2,
+    rz,
+    ag_sem,
+    ag_send,
+    own_sem,
+    core_sem,
+    xy_sem,
+    last_sem,
+    z_sem,
+    s0_send,
+    rs_send,
+    out_sem,
+    vec_send,
+    vec_recv,
+    gv_send,
+    gv_recv,
+    credit,
+):
+    count = layers * UNITS
+    d = lax.axis_index("dp")
+    f = lax.axis_index("fsdp")
+    c = lax.rem(f, 2)
+    x = lax.rem(lax.div(f, 2), 2)
+    y = lax.div(f, 4)
+    fc = f + 1 - 2 * c
+    fx = f + 2 - 4 * x
+    fy = f + 4 - 8 * y
+    outer = d * (3 - d) == 0
+    inner = d * (3 - d) != 0
+    z_in = 1 + lax.div(d, 3)
+    z_out = 3 * lax.div(d, 2)
+    z_pair = 3 - d
+    in_plane = lambda who: {"fsdp": who}
+    along = lambda who: {"dp": who}
+    both = lambda a, b: jnp.logical_and(a, b)
+
+    def block(yy, xx, cc):
+        return yy * 4 + xx * 2 + cc
+
+    def send(source, target, sent, landed, who):
+        pltpu.make_async_remote_copy(
+            src_ref=source,
+            dst_ref=target,
+            send_sem=sent,
+            recv_sem=landed,
+            device_id=who,
+            device_id_type=MESH,
+        ).start()
+
+    def wait_rows(sem, rows):
+        span = wb.at[pl.ds(0, rows)]
+        pltpu.make_async_copy(span, span, sem).wait()
+
+    barrier = pltpu.get_barrier_semaphore()
+    peers = [lax.rem(f + hop, 8) for hop in range(1, 8)]
+    for peer in peers:
+        pl.semaphore_signal(barrier, inc=1, device_id=in_plane(peer), device_id_type=MESH)
+
+    for hop in (1, 3):
+        beside = lax.rem(d + hop, 4)
+        pl.semaphore_signal(barrier, inc=1, device_id=along(beside), device_id_type=MESH)
+
+    for layer in range(layers):
+        for unit in range(UNITS):
+            if unit < 3:
+                source = w_qkv.at[layer, :, pl.ds(unit * D, D)]
+            elif unit == 3:
+                source = w_out.at[layer]
+            elif unit < 8:
+                source = w_up.at[layer, :, pl.ds((unit - 4) * D, D)]
+            else:
+                source = w_down.at[layer, pl.ds((unit - 8) * SHARD, SHARD)]
+            pltpu.make_async_copy(
+                source,
+                wb.at[pl.ds(unit_row(layer, unit, f), SHARD)],
+                own_sem.at[layer * UNITS + unit],
+            ).start()
+    vsg[f] = vec_shard[...]
+    pl.semaphore_wait(barrier, 9)
+
+    def gather_tick(t):
+        @pl.when(t < count)
+        def _():
+            layer, unit = forward_unit(t)
+            row = unit_row(layer, unit, f)
+            wait_rows(own_sem.at[t], SHARD)
+            first = wb.at[pl.ds(row, HALF)]
+            second = wb.at[pl.ds(aligned(row + HALF, 16), HALF)]
+            whole = wb.at[pl.ds(row, SHARD)]
+            send(first, first, ag_send.at[t], ag_sem.at[t, 0], in_plane(fy))
+            send(second, second, ag_send.at[t], ag_sem.at[t, 1], in_plane(fx))
+            send(first, first, ag_send.at[t], ag_sem.at[t, 2], in_plane(fx))
+            send(second, second, ag_send.at[t], ag_sem.at[t, 2], in_plane(fy))
+            send(whole, whole, ag_send.at[t], ag_sem.at[t, 3], in_plane(fc))
+
+        @pl.when(both(t >= 2, t < count + 2))
+        def _():
+            i = t - 2
+            layer, unit = forward_unit(i)
+            wait_rows(ag_sem.at[i, 0], HALF)
+            wait_rows(ag_sem.at[i, 1], HALF)
+            first = wb.at[pl.ds(unit_row(layer, unit, block(1 - y, x, c)), HALF)]
+            other = unit_row(layer, unit, block(y, 1 - x, c))
+            second = wb.at[pl.ds(aligned(other + HALF, 16), HALF)]
+            send(first, first, ag_send.at[i], ag_sem.at[i, 2], in_plane(fx))
+            send(second, second, ag_send.at[i], ag_sem.at[i, 2], in_plane(fy))
+
+        @pl.when(both(t >= 4, t < count + 4))
+        def _():
+            i = t - 4
+            layer, unit = forward_unit(i)
+            wait_rows(ag_sem.at[i, 2], 4 * HALF)
+            for yy, xx in ((1 - y, x), (y, 1 - x), (1 - y, 1 - x)):
+                piece = wb.at[pl.ds(unit_row(layer, unit, block(yy, xx, c)), SHARD)]
+                send(piece, piece, ag_send.at[i], ag_sem.at[i, 3], in_plane(fc))
+
+        @pl.when(both(t >= 5, t < count + 5))
+        def _():
+            wait_rows(ag_sem.at[t - 5, 3], 4 * SHARD)
+
+    for hop, peer in enumerate(peers):
+        send(vec_shard, vsg.at[f], vec_send.at[hop], vec_recv.at[hop], in_plane(peer))
+
+    @pl.loop(0, 5)
+    def _(t):
+        gather_tick(t)
+
+    def crop_of(shape, dim, start):
+        at = lax.broadcasted_iota(jnp.int32, shape, dim) + start
+        which = jnp.zeros(shape, jnp.int32)
+        for edge in range(L_DEV + 1):
+            which = which + (at >= GLEN + edge * LLEN).astype(jnp.int32)
+        return which
+
+    for mask, rows, row_at, key_at in (
+        (mask_top, TOP_ROWS, 0, 0),
+        (mask_low, LOW_ROWS, TOP_ROWS, LOW_KEY),
+    ):
+        same = crop_of((rows, KEYS), 0, row_at) == crop_of((rows, KEYS), 1, key_at)
+        mask[...] = jnp.where(same, 0.0, -1e30).astype(F32)
+
+    xs[0, PAD - 8 :, :] = jnp.zeros((8, D), F32)
+    xs[0, 0:ROWS, :] = tokens[...].astype(F32)
+
+    for hop in range(7):
+        pltpu.make_async_copy(vec_shard, vec_shard, vec_recv.at[hop]).wait()
+    spread = jnp.zeros((8 * layers, D), F32)
+    for owner in range(8):
+        at_row = lax.broadcasted_iota(jnp.int32, (128, D), 0)
+        at_col = lax.broadcasted_iota(jnp.int32, (128, D), 1)
+        hit = jnp.logical_and(at_col == at_row + owner * SHARD, at_row < SHARD)
+        spread = spread + nn(vsg[owner, :, 0:128], jnp.where(hit, 1.0, 0.0).astype(BF16))
+        ubs[:, owner * 384 : (owner + 1) * 384] = vsg[owner, :, 128:512].astype(F32)
+    vec[...] = spread
+
+    def vector(layer, which):
+        return vec[pl.ds(layer * 8 + which, 1), :]
+
+    lane = lax.broadcasted_iota(jnp.int32, (1, 128), 1)
+    left_lane = lane < HEAD_DIM
+    score_scale = HEAD_DIM ** (-0.5)
+    head_scaled = [
+        jnp.where(left_lane, score_scale, 0.0).astype(BF16),
+        jnp.where(left_lane, 0.0, score_scale).astype(BF16),
+    ]
+    head_plain = [
+        jnp.where(left_lane, 1.0, 0.0).astype(BF16),
+        jnp.where(left_lane, 0.0, 1.0).astype(BF16),
+    ]
+    groups = (
+        (0, TOP_ROWS, 0, mask_top),
+        (TOP_ROWS, LOW_ROWS, LOW_KEY, mask_low),
+    )
+
+    def weight(layer, unit):
+        return pl.ds(aligned(layer * LAYER_ROWS + unit * D, 16), D)
+
+    @pl.loop(0, layers)
+    def _(layer):
+        base = layer * UNITS + 5
+
+        @pl.loop(0, PAD // STEP)
+        def _(step):
+            rows = step_rows(step)
+            normed, _unused = stats(xs[layer, rows, :])
+            nr[layer, rows, :] = (normed * vector(layer, V_G1) + vector(layer, V_B1)).astype(BF16)
+
+        @pl.loop(0, 3)
+        def _(part):
+            gather_tick(base + part)
+            is_q, is_v = lax.div(2 - part, 2), lax.div(part, 2)
+            bias = is_q.astype(F32) * vector(layer, V_QB) + is_v.astype(F32) * vector(layer, V_VB)
+            acc[...] = nn(nr[layer], wb[weight(layer, part), :])
+
+            @pl.loop(0, PAD // STEP)
+            def _(step):
+                rows = step_rows(step)
+                pj[layer, part, rows, :] = (acc[rows, :] + bias).astype(BF16)
+
+        @pl.loop(0, HEADS // 2)
+        def _(pair):
+            @pl.when(pair == 3)
+            def _():
+                gather_tick(base + 3)
+
+            lanes = pl.ds(aligned(pair * 128, 128), 128)
+            for row_at, rows, key_at, mask in groups:
+                here = pl.ds(row_at, rows)
+                keys = pj[layer, 1, pl.ds(key_at, KEYS), lanes]
+                values = pj[layer, 2, pl.ds(key_at, KEYS), lanes]
+                queries = pj[layer, 0, here, lanes]
+                results = []
+                for side in range(2):
+                    scores = nt(queries * head_scaled[side], keys) + mask[...]
+                    peak = jnp.max(scores, axis=-1, keepdims=True)
+                    raised = jnp.exp(scores - peak)
+                    exp_total = jnp.sum(raised, axis=-1, keepdims=True)
+                    probs = (raised * (1.0 / exp_total)).astype(BF16)
+                    results.append(nn(probs, values))
+                    log_total = peak + jnp.log(exp_total)
+                    lse[layer, here, :] = jnp.where(
+                        lane == pair * 2 + side, log_total, lse[layer, here, :]
+                    )
+                mx[layer, here, lanes] = jnp.where(left_lane, results[0], results[1]).astype(BF16)
+
+        acc[...] = nn(mx[layer], wb[weight(layer, 3), :])
+
+        @pl.loop(0, PAD // STEP)
+        def _(step):
+            rows = step_rows(step)
+            now = xs[layer, rows, :] + acc[rows, :] + vector(layer, V_OB)
+            x1[layer, rows, :] = now
+            normed, _unused = stats(now)
+            n2[layer, rows, :] = (normed * vector(layer, V_G2) + vector(layer, V_B2)).astype(BF16)
+
+        @pl.loop(0, 4)
+        def _(part):
+            gather_tick(base + 4 + part)
+            bias = ubs[pl.ds(layer * 8, 1), pl.ds(aligned(part * D, 128), D)]
+            acc[...] = nn(n2[layer], wb[weight(layer, 4 + part), :])
+
+            @pl.loop(0, PAD // STEP)
+            def _(step):
+                rows = step_rows(step)
+                pre = acc[rows, :] + bias
+                cdf = 0.5 + 0.5 * lax.erf(pre * (0.5**0.5))
+                bell = jnp.exp(-0.5 * pre * pre) * 0.3989422804014327
+                hd[layer, part, rows, :] = (pre * cdf).astype(BF16)
+                gp[layer, part, rows, :] = (cdf + pre * bell).astype(BF16)
+
+        @pl.loop(0, 4)
+        def _(part):
+            gather_tick(base + 8 + part)
+
+        acc[...] = x1[layer] + vector(layer, V_DB)
+
+        @pl.loop(0, 4)
+        def _(part):
+            acc[...] += nn(hd[layer, part], wb[weight(layer, 8 + part), :])
+
+        xs[layer + 1] = acc[...]
+
+    encoded[...] = xs[layers, 0:ROWS, :].astype(BF16)
+
+    @pl.loop(0, count)
+    def _(i):
+        wait_rows(ag_send.at[i], 7 * SHARD)
+
+    for hop in range(7):
+        pltpu.make_async_copy(vec_shard, vec_shard, vec_send.at[hop]).wait()
+
+    def here_row(i, owner):
+        layer, unit = backward_unit(layers, i)
+        return unit_row(layer, unit, owner)
+
+    def half_rows(row, half):
+        return pl.ds(aligned(row + half * HALF, 16), HALF)
+
+    def credit_wait(i, which):
+        @pl.when(i >= SLOTS)
+        def _():
+            pl.semaphore_wait(credit.at[which], 1)
+
+    def credit_give(i, which, who):
+        @pl.when(i + SLOTS < count)
+        def _():
+            pl.semaphore_signal(credit.at[which], inc=1, device_id=who, device_id_type=MESH)
+
+    def reduce_tick(t):
+        @pl.when(t < count)
+        def _():
+            slot = lax.rem(t, SLOTS)
+            credit_wait(t, 0)
+            for place in range(4):
+                source = wb.at[pl.ds(here_row(t, 2 * place + 1 - c), SHARD)]
+                send(
+                    source,
+                    rc.at[slot, pl.ds(place * SHARD, SHARD)],
+                    s0_send.at[t],
+                    core_sem.at[t],
+                    in_plane(fc),
+                )
+
+        @pl.when(both(t >= 11, t < count + 11))
+        def _():
+            i = t - 11
+            layer, unit = backward_unit(layers, i)
+
+            @pl.when(outer)
+            def _():
+                wait_rows(z_sem.at[i, 2], SHARD)
+
+            done = wb.at[pl.ds(unit_row(layer, unit, fc), SHARD)]
+
+            @pl.when(unit < 3)
+            def _():
+                target = g_qkv.at[layer, :, pl.ds(aligned(unit * D, 128), D)]
+                pltpu.make_async_copy(done, target, out_sem.at[i]).start()
+
+            @pl.when(unit == 3)
+            def _():
+                pltpu.make_async_copy(done, g_out.at[layer], out_sem.at[i]).start()
+
+            @pl.when(both(unit >= 4, unit < 8))
+            def _():
+                target = g_up.at[layer, :, pl.ds(aligned((unit - 4) * D, 128), D)]
+                pltpu.make_async_copy(done, target, out_sem.at[i]).start()
+
+            @pl.when(unit >= 8)
+            def _():
+                target = g_down.at[layer, pl.ds(aligned((unit - 8) * SHARD, 16), SHARD)]
+                pltpu.make_async_copy(done, target, out_sem.at[i]).start()
+
+        @pl.when(both(inner, both(t >= 9, t < count + 9)))
+        def _():
+            i = t - 9
+            slot = lax.rem(i, SLOTS)
+            wait_rows(z_sem.at[i, 1], SHARD)
+            own = here_row(i, f)
+            done = pl.ds(here_row(i, fc), SHARD)
+            wb[done, :] = wb[pl.ds(own, SHARD), :] + rz[slot, 1]
+            credit_give(i, 4, along(z_pair))
+            send(wb.at[done], wb.at[done], rs_send.at[i], z_sem.at[i, 2], along(z_out))
+
+        @pl.when(both(inner, both(t >= 7, t < count + 7)))
+        def _():
+            i = t - 7
+            slot = lax.rem(i, SLOTS)
+            wait_rows(z_sem.at[i, 0], SHARD)
+            own = pl.ds(here_row(i, f), SHARD)
+            wb[own, :] = wb[own, :] + rz[slot, 0]
+            credit_give(i, 3, along(z_out))
+            credit_wait(i, 4)
+            send(wb.at[own], rz.at[slot, 1], rs_send.at[i], z_sem.at[i, 1], along(z_pair))
+
+        @pl.when(both(t >= 5, t < count + 5))
+        def _():
+            i = t - 5
+            slot = lax.rem(i, SLOTS)
+            wait_rows(last_sem.at[i], SHARD)
+            own = pl.ds(here_row(i, f), SHARD)
+            spare = pl.ds(here_row(i, fc), SHARD)
+            wb[own, :] = wb[own, :] + wb[spare, :]
+
+            @pl.when(outer)
+            def _():
+                credit_wait(i, 3)
+                send(wb.at[own], rz.at[slot, 0], rs_send.at[i], z_sem.at[i, 0], along(z_in))
+
+        @pl.when(both(t >= 3, t < count + 3))
+        def _():
+            i = t - 3
+            slot = lax.rem(i, SLOTS)
+            wait_rows(xy_sem.at[i], 4 * HALF)
+            for other in range(2):
+                span = half_rows(here_row(i, block(other, x, c)), 0)
+                wb[span, :] = wb[span, :] + r2[slot, pl.ds(other * HALF, HALF), :]
+                span = half_rows(here_row(i, block(y, other, c)), 1)
+                wb[span, :] = wb[span, :] + r2[slot, pl.ds((2 + other) * HALF, HALF), :]
+            credit_give(i, 1, in_plane(fx))
+            credit_give(i, 2, in_plane(fy))
+            first = wb.at[half_rows(here_row(i, block(1 - y, x, c)), 0)]
+            second = wb.at[half_rows(here_row(i, block(y, 1 - x, c)), 1)]
+            spare_y = here_row(i, block(1 - y, x, 1 - c))
+            spare_x = here_row(i, block(y, 1 - x, 1 - c))
+            send(first, wb.at[half_rows(spare_y, 0)], rs_send.at[i], last_sem.at[i], in_plane(fy))
+            send(second, wb.at[half_rows(spare_x, 1)], rs_send.at[i], last_sem.at[i], in_plane(fx))
+
+        @pl.when(both(t >= 1, t < count + 1))
+        def _():
+            i = t - 1
+            slot = lax.rem(i, SLOTS)
+            wait_rows(core_sem.at[i], 4 * SHARD)
+            wait_rows(s0_send.at[i], 4 * SHARD)
+            for place in range(4):
+                span = pl.ds(here_row(i, 2 * place + c), SHARD)
+                wb[span, :] = wb[span, :] + rc[slot, pl.ds(place * SHARD, SHARD), :]
+            credit_give(i, 0, in_plane(fc))
+            credit_wait(i, 1)
+            credit_wait(i, 2)
+            for other in range(2):
+                send(
+                    wb.at[half_rows(here_row(i, block(other, 1 - x, c)), 0)],
+                    r2.at[slot, pl.ds(other * HALF, HALF)],
+                    rs_send.at[i],
+                    xy_sem.at[i],
+                    in_plane(fx),
+                )
+                send(
+                    wb.at[half_rows(here_row(i, block(1 - y, other, c)), 1)],
+                    r2.at[slot, pl.ds((2 + other) * HALF, HALF)],
+                    rs_send.at[i],
+                    xy_sem.at[i],
+                    in_plane(fy),
+                )
+
+    def vector_step(layer, step):
+        mine = g_vec.at[layer]
+
+        def arrive(at):
+            pltpu.make_async_copy(mine, mine, gv_recv.at[layer, at]).wait()
+
+        def leave(at):
+            pltpu.make_async_copy(mine, mine, gv_send.at[layer, at]).wait()
+
+        def go(at, target, landed, who):
+            send(mine, target, gv_send.at[layer, at], gv_recv.at[layer, landed], who)
+
+        def add(at):
+            g_vec[layer] = g_vec[layer] + vr[layer, at]
+
+        for at, who in enumerate((fc, fx, fy)):
+
+            @pl.when(step == at)
+            def _(at=at, who=who):
+                if at:
+                    leave(at - 1)
+                    arrive(at - 1)
+                    add(at - 1)
+                go(at, vr.at[layer, at], at, in_plane(who))
+
+        @pl.when(step == 3)
+        def _():
+            leave(2)
+            arrive(2)
+            add(2)
+
+            @pl.when(outer)
+            def _():
+                go(3, vr.at[layer, 3], 3, along(z_in))
+
+        @pl.when(both(inner, step == 4))
+        def _():
+            arrive(3)
+            add(3)
+            go(4, vr.at[layer, 4], 4, along(z_pair))
+
+        @pl.when(both(inner, step == 5))
+        def _():
+            leave(4)
+            arrive(4)
+            add(4)
+            go(3, vr.at[layer, 3], 3, along(z_out))
+
+        @pl.when(step == 6)
+        def _():
+            leave(3)
+
+            @pl.when(outer)
+            def _():
+                arrive(3)
+                g_vec[layer] = vr[layer, 3]
+
+    up = xs.at[layers]
+    up[PAD - 8 :, :] = jnp.zeros((8, D), F32)
+    up[0:ROWS, :] = cotangent[...].astype(F32)
+    none = jnp.zeros((8, D), F32)
+
+    def put_vector(layer, which, value):
+        g_vec[layer, pl.ds(which, 1), :] = total(value)
+
+    def weight_grad(rows_at, left, right):
+        @pl.loop(0, 3)
+        def _(third):
+            lanes = pl.ds(aligned(third * KEYS, 128), KEYS)
+            target = pl.ds(aligned(rows_at + third * KEYS, 16), KEYS)
+            wb[target, :] = tn(left[:, lanes], right[...]).astype(BF16)
+
+    @pl.loop(0, layers)
+    def _(turn):
+        layer = layers - 1 - turn
+        base = turn * UNITS
+        for row in range(12, 16):
+            g_vec[layer, row : row + 1, :] = jnp.zeros((1, D), F32)
+
+        def branch_two(step, carry):
+            rows = step_rows(step)
+            rounded = up[rows, :].astype(BF16)
+            br[rows, :] = rounded
+            return carry + fold(rounded.astype(F32))
+
+        put_vector(layer, V_DB, lax.fori_loop(0, PAD // STEP, branch_two, none))
+
+        @pl.loop(0, 4)
+        def _(part):
+            @pl.when(turn > 0)
+            def _():
+                vector_step(layer + 1, part)
+
+            acc[...] = nt(br[...], wb[weight(layer, 8 + part), :])
+
+            def through_gelu(step, carry):
+                rows = step_rows(step)
+                value = (acc[rows, :] * gp[layer, part, rows, :].astype(F32)).astype(BF16)
+                gb[part, rows, :] = value
+                return carry + fold(value.astype(F32))
+
+            put_vector(layer, V_UB + part, lax.fori_loop(0, PAD // STEP, through_gelu, none))
+            weight_grad(layer * LAYER_ROWS + DOWN_AT + part * D, hd.at[layer, part], br)
+
+        acc[...] = jnp.zeros((PAD, D), F32)
+
+        @pl.loop(0, 4)
+        def _(part):
+            @pl.when(both(turn > 0, part < 3))
+            def _():
+                vector_step(layer + 1, part + 4)
+
+            acc[...] += nt(gb[part], wb[weight(layer, 4 + part), :])
+            weight_grad(layer * LAYER_ROWS + (4 + part) * D, n2.at[layer], gb.at[part])
+            reduce_tick(base + part)
+
+        def norm_back(source, gain_at, shift_at):
+            def body(step, carry):
+                gain_sum, shift_sum = carry
+                rows = step_rows(step)
+                normed, scale = stats(source[layer, rows, :])
+                grad = acc[rows, :]
+                t = grad * vector(layer, gain_at)
+                inner_mean = jnp.mean(t * normed, axis=-1, keepdims=True)
+                back = scale * (t - jnp.mean(t, axis=-1, keepdims=True) - normed * inner_mean)
+                up[rows, :] = up[rows, :] + back
+                return gain_sum + fold(grad * normed), shift_sum + fold(grad)
+
+            gain_sum, shift_sum = lax.fori_loop(0, PAD // STEP, body, (none, none))
+            put_vector(layer, gain_at, gain_sum)
+            put_vector(layer, shift_at, shift_sum)
+
+        norm_back(x1, V_G2, V_B2)
+
+        put_vector(layer, V_OB, lax.fori_loop(0, PAD // STEP, branch_two, none))
+        gm[...] = nt(br[...], wb[weight(layer, 3), :]).astype(BF16)
+        weight_grad(layer * LAYER_ROWS + 3 * D, mx.at[layer], br)
+
+        @pl.loop(0, HEADS // 2)
+        def _(pair):
+            @pl.when(lax.rem(pair, 2) == 0)
+            def _():
+                reduce_tick(base + 4 + lax.div(pair, 2))
+
+            lanes = pl.ds(aligned(pair * 128, 128), 128)
+            kacc[...] = jnp.zeros((PAD, 128), F32)
+            vacc[...] = jnp.zeros((PAD, 128), F32)
+            for row_at, rows, key_at, mask in groups:
+                here = pl.ds(row_at, rows)
+                there = pl.ds(key_at, KEYS)
+                keys = pj[layer, 1, there, lanes]
+                values = pj[layer, 2, there, lanes]
+                queries = pj[layer, 0, here, lanes]
+                grads = gm[here, lanes]
+                q_parts, k_parts, v_parts = [], [], []
+                for side in range(2):
+                    log_total = jnp.sum(
+                        jnp.where(lane == pair * 2 + side, lse[layer, here, :], 0.0),
+                        axis=-1,
+                        keepdims=True,
+                    )
+                    scaled = queries * head_scaled[side]
+                    probs = jnp.exp(nt(scaled, keys) + mask[...] - log_total)
+                    grad_probs = nt(grads * head_plain[side], values)
+                    row_inner = jnp.sum(grad_probs * probs, axis=-1, keepdims=True)
+                    grad_scores = (probs * (grad_probs - row_inner)).astype(BF16)
+                    v_parts.append(tn(probs.astype(BF16), grads))
+                    k_parts.append(tn(grad_scores, queries))
+                    q_parts.append(nn(grad_scores, keys))
+                grad_queries = jnp.where(left_lane, q_parts[0], q_parts[1]) * score_scale
+                gb[0, here, lanes] = grad_queries.astype(BF16)
+                kacc[there, :] += jnp.where(left_lane, k_parts[0], k_parts[1]) * score_scale
+                vacc[there, :] += jnp.where(left_lane, v_parts[0], v_parts[1])
+            gb[1, :, lanes] = kacc[...].astype(BF16)
+            gb[2, :, lanes] = vacc[...].astype(BF16)
+
+        for which, part in ((V_QB, 0), (V_VB, 2)):
+
+            def column_sum(step, carry, part=part):
+                return carry + fold(gb[part, step_rows(step), :].astype(F32))
+
+            put_vector(layer, which, lax.fori_loop(0, PAD // STEP, column_sum, none))
+
+        acc[...] = jnp.zeros((PAD, D), F32)
+
+        @pl.loop(0, 3)
+        def _(part):
+            acc[...] += nt(gb[part], wb[weight(layer, part), :])
+            weight_grad(layer * LAYER_ROWS + part * D, nr.at[layer], gb.at[part])
+            reduce_tick(base + 7 + part)
+
+        norm_back(xs, V_G1, V_B1)
+
+        @pl.loop(0, 2)
+        def _(part):
+            reduce_tick(base + 10 + part)
+
+    tokens_grad[...] = up[0:ROWS, :]
+
+    @pl.loop(count, count + 11)
+    def _(t):
+        @pl.when(t < count + 7)
+        def _():
+            vector_step(0, t - count)
+
+        reduce_tick(t)
+
+    @pl.loop(0, count)
+    def _(i):
+        wait_rows(out_sem.at[i], SHARD)
+
+        @pl.when(outer)
+        def _():
+            wait_rows(rs_send.at[i], 4 * SHARD)
+
+        @pl.when(inner)
+        def _():
+            wait_rows(rs_send.at[i], 5 * SHARD)
+
+
+def kernel_local(
+    tokens,
+    cotangent,
+    norm1_gain,
+    norm1_bias,
+    qkv_weight,
+    query_bias,
+    value_bias,
+    out_weight,
+    out_bias,
+    norm2_gain,
+    norm2_bias,
+    up_weight,
+    up_bias,
+    down_weight,
+    down_bias,
+):
+    layers = qkv_weight.shape[0]
+    small = jnp.stack(
+        [
+            norm1_gain,
+            norm1_bias,
+            query_bias,
+            value_bias,
+            out_bias,
+            norm2_gain,
+            norm2_bias,
+            down_bias,
+        ],
+        axis=1,
+    ).reshape(8 * layers, SHARD)
+    small = jnp.pad(small, ((0, 0), (0, 128 - SHARD)))
+    wide = jnp.pad(up_bias[:, None, :], ((0, 0), (0, 7), (0, 0))).reshape(8 * layers, 4 * SHARD)
+    vec_shard = jnp.concatenate([small, wide], axis=1)
+
+    count = layers * UNITS
+    vmem = pl.BlockSpec(memory_space=pltpu.VMEM)
+    hbm = pl.BlockSpec(memory_space=pl.ANY)
+    dma = pltpu.SemaphoreType.DMA
+    results = pl.pallas_call(
+        functools.partial(encoder_kernel, layers),
+        out_shape=(
+            jax.ShapeDtypeStruct((ROWS, D), BF16),
+            jax.ShapeDtypeStruct((ROWS, D), F32),
+            jax.ShapeDtypeStruct((layers, 16, D), F32),
+            jax.ShapeDtypeStruct((layers, SHARD, 3 * D), BF16),
+            jax.ShapeDtypeStruct((layers, SHARD, D), BF16),
+            jax.ShapeDtypeStruct((layers, SHARD, FF), BF16),
+            jax.ShapeDtypeStruct((layers, 4 * SHARD, D), BF16),
+        ),
+        in_specs=[vmem] * 3 + [hbm] * 4,
+        out_specs=(vmem, vmem, vmem, hbm, hbm, hbm, hbm),
+        scratch_shapes=[
+            pltpu.VMEM((layers * LAYER_ROWS, D), BF16),
+            pltpu.VMEM((layers + 1, PAD, D), F32),
+            pltpu.VMEM((layers, PAD, D), F32),
+            pltpu.VMEM((layers, PAD, D), BF16),
+            pltpu.VMEM((layers, 3, PAD, D), BF16),
+            pltpu.VMEM((layers, PAD, D), BF16),
+            pltpu.VMEM((layers, PAD, D), BF16),
+            pltpu.VMEM((layers, 4, PAD, D), BF16),
+            pltpu.VMEM((layers, 4, PAD, D), BF16),
+            pltpu.VMEM((layers, PAD, 128), F32),
+            pltpu.VMEM((4, PAD, D), BF16),
+            pltpu.VMEM((PAD, D), BF16),
+            pltpu.VMEM((PAD, D), BF16),
+            pltpu.VMEM((PAD, D), F32),
+            pltpu.VMEM((PAD, 128), F32),
+            pltpu.VMEM((PAD, 128), F32),
+            pltpu.VMEM((TOP_ROWS, KEYS), F32),
+            pltpu.VMEM((LOW_ROWS, KEYS), F32),
+            pltpu.VMEM((8, 8 * layers, 512), BF16),
+            pltpu.VMEM((8 * layers, D), F32),
+            pltpu.VMEM((8 * layers, FF), F32),
+            pltpu.VMEM((layers, 5, 16, D), F32),
+            pltpu.VMEM((SLOTS, 4 * SHARD, D), BF16),
+            pltpu.VMEM((SLOTS, 4 * HALF, D), BF16),
+            pltpu.VMEM((SLOTS, 2, SHARD, D), BF16),
+            dma((count, 4)),
+            dma((count,)),
+            dma((count,)),
+            dma((count,)),
+            dma((count,)),
+            dma((count,)),
+            dma((count, 3)),
+            dma((count,)),
+            dma((count,)),
+            dma((count,)),
+            dma((7,)),
+            dma((7,)),
+            dma((layers, 5)),
+            dma((layers, 5)),
+            pltpu.SemaphoreType.REGULAR((5,)),
+        ],
+        compiler_params=pltpu.CompilerParams(
+            collective_id=0, has_side_effects=True, vmem_limit_bytes=VMEM_BYTES
+        ),
+    )(tokens, cotangent, vec_shard, qkv_weight, out_weight, up_weight, down_weight)
+    encoded, tokens_grad, g_vec, g_qkv, g_out, g_up, g_down = results
+    f = lax.axis_index("fsdp")
+    vectors = lax.dynamic_slice_in_dim(g_vec[:, :8], f * SHARD, SHARD, axis=2)
+    up_vector = lax.dynamic_slice_in_dim(
+        g_vec[:, 8:12].reshape(layers, FF), f * 4 * SHARD, 4 * SHARD, axis=1
+    )
+    return (
+        encoded,
+        tokens_grad,
+        vectors[:, V_G1],
+        vectors[:, V_B1],
+        g_qkv.astype(F32),
+        vectors[:, V_QB],
+        vectors[:, V_VB],
+        g_out.astype(F32),
+        vectors[:, V_OB],
+        vectors[:, V_G2],
+        vectors[:, V_B2],
+        g_up.astype(F32),
+        up_vector,
+        g_down.astype(F32),
+        vectors[:, V_DB],
+    )
+
+
 def solution(mesh):
     in_specs = (
         P(("dp", "fsdp"), None),
@@ -469,4 +1352,6 @@
         P(None, "fsdp", None),
         P(None, "fsdp"),
     )
-    return jax.shard_map(local, mesh=mesh, in_specs=in_specs, out_specs=out_specs, check_vma=False)
+    fits = mesh.shape["dp"] == 4 and mesh.shape["fsdp"] == 8
+    body = kernel_local if fits else local
+    return jax.shard_map(body, mesh=mesh, in_specs=in_specs, out_specs=out_specs, check_vma=False)

time: 1030 us -> 313 us (0.30)
  waiting for transfers between devices: 497 us -> 0 us
  Pallas kernels: 0 us -> 294 us
  blocking collectives: 202 us -> 0 us
  matrix products: 160 us -> 0 us
  local copies, waits for them, and re-layouts: 115 us -> 10.7 us
  other arithmetic: 31.5 us -> 7.4 us
  between operations: 18.1 us -> 0.68 us
    pallas_call x0 -> x1, Pallas kernels: none -> 294 us  [kernel_local(): pl.pallas_call(functools.partial(encoder_kernel, layers), out_shape=(jax....]
    reduce_scatter x10 -> x0, waiting for transfers between devices: 239 us -> none  [the longest x2 104 us: reduce_grads(): lax.psum_scatter(grads[11].astype(jnp.bfloat16), 'fsdp', scatter_dimensio...]
    dot_general x48 -> x0, matrix products: 160 us -> none  [the longest x8 39.5 us: contract_rows(): lax.dot_general(left, right, (((0,), (0,)), ((), ())), preferred_element_...]
    all_gather x10 -> x0, blocking collectives: 157 us -> none  [the longest x2 40 us: reduce_grads(): lax.all_gather(column_parts[3].astype(jnp.bfloat16), 'dp', axis=1, tiled=...]
    all_gather x8 -> x0, waiting for transfers between devices: 139 us -> none  [the longest x2 57.5 us: gather_forward(): lax.all_gather(pieces[9], 'fsdp', axis=0, tiled=True)]
    unnamed x32 -> x0, waiting for transfers between devices: 119 us -> none
    reshape x18 -> x1, local copies, waits for them, and re-layouts: 32 us -> 0.01 us  [kernel_local(): jnp.pad(up_bias[:, None, :], ((0, 0), (0, 7), (0, 0)))]
    unnamed x328 -> x22, local copies, waits for them, and re-layouts: 38 us -> 7.92 us
  transfers between devices with their start and end apart: 25 -> 0, of which waited for: 20 -> 0; matrix products, arithmetic and copies ran while one was open for 25% -> 0% of each run, Pallas kernels for 0% -> 0%
where the time goes in v2:
time: 313 us
  Pallas kernels  294 us (94%)
  local copies, waits for them, and re-layouts  10.7 us (3%)
  other arithmetic  7.4 us (2%)
    pallas_call x1, Pallas kernels, kernel_local(): pl.pallas_call(functools.partial(encoder_kernel, layers), out_shape=(jax....  294 us
    unnamed x22, local copies, waits for them, and re-layouts  7.92 us

profile of v2, /device:TPU:0, one launch (start us, length us, event | category | flops | bytes accessed | tf_op | source)
XLA Modules:
  0.0 312.9 jit_solution(14988586259144813213)
XLA Ops:
  0.7 0.7 constant_dynamic-update-slice_fusion.7
  1.3 0.7 constant_dynamic-update-slice_fusion.6
  2.0 0.7 constant_dynamic-update-slice_fusion.5
  2.6 0.7 constant_dynamic-update-slice_fusion.4
  3.3 0.7 constant_dynamic-update-slice_fusion.3
  4.0 0.7 constant_dynamic-update-slice_fusion.2
  4.6 0.7 constant_dynamic-update-slice_fusion.1
  5.3 0.7 constant_dynamic-update-slice_fusion
  6.0 0.7 copy.32
  6.6 0.6 fusion.1.vec_shard
  7.3 294.1 %shard_map.262 = (bf16[345,768]{1,0:T(8,128)(2,1)}, f32[345,768]{1,0:T(8,128)}, f32[2,16,768]{2,1,0:T(8,128)}, bf16[2,96,2304]{2,1,0:T(8,128)(2,1)}, bf16[2,96,7...) custom-call(bf16[345,768]{1,0:T(8,128)(2,1)} %tokens.1, bf16[345,768]{1,0:T(8,128)(2,1)} %cotangent.1, ...), custom_call_target="tpu_custom_call" | custom-call | tf_op jit(solution)/shard_map/pallas_call | solution.py:1236
  301.4 0.8 slice.30
  302.2 0.7 constant_dynamic-slice_fusion.8
  302.9 0.8 slice_bitcast_fusion
  303.7 0.6 constant_dynamic-slice_fusion.7
  304.3 0.0 copy-start
  304.3 3.0 convert_element_type.18
  307.3 0.0 copy-done
  307.3 0.0 copy-start.2
  307.3 1.6 convert_element_type.19
  308.9 0.0 copy-done.2
  308.9 0.0 copy-start.4
  308.9 0.0 copy-start.3
  308.9 1.3 convert_element_type.16
  310.2 0.0 copy-start.1
  310.2 0.0 copy-done.4
  310.2 0.9 convert_element_type.17
  311.1 0.0 copy-done.3
  311.1 0.8 copy.45
  311.9 0.0 copy-done.1
  311.9 1.0 copy.46
  (3 shorter events, 0.0 us)
Async XLA Ops:
  304.3 3.0 copy-start
  307.3 1.6 copy-start.2
  308.9 1.3 copy-start.4
  308.9 2.2 copy-start.3
  310.2 1.7 copy-start.1

commit v3 on v2

--- a/solution.py
+++ b/solution.py
@@ -448,12 +448,19 @@
 ROWS = 345
 PAD = 352
 STEP = 32
+UNROLL = True
 SHARD = 96
 HALF = 48
 UNITS = 12
 LAYER_ROWS = UNITS * D
 DOWN_AT = 8 * D
-SLOTS = 3
+SLOTS = 6
+PARTS = 2
+WIDE = D // PARTS
+LAG_XY, LAG_LAST, LAG_Z1, LAG_Z2, LAG_OUT = 3, 5, 7, 9, 11
+LAG_PASS, LAG_WHOLE = 8, 9
+HELD = 4
+EARLY = 3
 TOP_ROWS = 208
 KEYS = 256
 LOW_KEY = PAD - KEYS
@@ -489,7 +496,8 @@
 
 
 def backward_unit(layers, index):
-    turn, place = lax.div(index, UNITS), lax.rem(index, UNITS)
+    whole, half = lax.div(index, PARTS), lax.rem(index, PARTS)
+    turn, place = lax.div(whole, UNITS), lax.rem(whole, UNITS)
     part = lax.div(place, 4)
     is_down, is_late = lax.div(2 - part, 2), lax.div(part, 2)
     unit = (
@@ -497,7 +505,7 @@
         + (1 - is_down - is_late) * place
         + is_late * lax.rem(place + 3, 4)
     )
-    return layers - 1 - turn, unit
+    return layers - 1 - turn, unit, half
 
 
 def stats(x):
@@ -523,7 +531,15 @@
     layers,
     tokens,
     cotangent,
-    vec_shard,
+    n_g1,
+    n_b1,
+    n_qb,
+    n_vb,
+    n_ob,
+    n_g2,
+    n_b2,
+    n_db,
+    n_ub,
     w_qkv,
     w_out,
     w_up,
@@ -577,6 +593,7 @@
     credit,
 ):
     count = layers * UNITS
+    pieces = count * PARTS
     d = lax.axis_index("dp")
     f = lax.axis_index("fsdp")
     c = lax.rem(f, 2)
@@ -590,6 +607,8 @@
     z_in = 1 + lax.div(d, 3)
     z_out = 3 * lax.div(d, 2)
     z_pair = 3 - d
+    parity = lax.rem(d, 2)
+    z_near = d + 1 - 2 * parity
     in_plane = lambda who: {"fsdp": who}
     along = lambda who: {"dp": who}
     both = lambda a, b: jnp.logical_and(a, b)
@@ -635,8 +654,22 @@
                 wb.at[pl.ds(unit_row(layer, unit, f), SHARD)],
                 own_sem.at[layer * UNITS + unit],
             ).start()
-    vsg[f] = vec_shard[...]
+    vec[...] = jnp.zeros((8 * layers, D), F32)
+    for at, source in enumerate((n_g1, n_b1, n_qb, n_vb, n_ob, n_g2, n_b2, n_db)):
+        shard = source[...].astype(F32)
+        for layer in range(layers):
+            vec[8 * layer + at : 8 * layer + at + 1, 0:SHARD] = shard[layer : layer + 1]
+    shard = n_ub[...].astype(F32)
+    for layer in range(layers):
+        vec[8 * layer : 8 * layer + 1, 128:512] = shard[layer : layer + 1]
+    vsg[f] = vec[:, 0:512].astype(BF16)
     pl.semaphore_wait(barrier, 9)
+
+    def role(i):
+        return lax.rem(i, 3) * lax.div(2 * count - 3 - i, count)
+
+    def collects(i):
+        return role(i) != 2 - parity
 
     def gather_tick(t):
         @pl.when(t < count)
@@ -644,16 +677,20 @@
             layer, unit = forward_unit(t)
             row = unit_row(layer, unit, f)
             wait_rows(own_sem.at[t], SHARD)
-            first = wb.at[pl.ds(row, HALF)]
-            second = wb.at[pl.ds(aligned(row + HALF, 16), HALF)]
             whole = wb.at[pl.ds(row, SHARD)]
-            send(first, first, ag_send.at[t], ag_sem.at[t, 0], in_plane(fy))
-            send(second, second, ag_send.at[t], ag_sem.at[t, 1], in_plane(fx))
-            send(first, first, ag_send.at[t], ag_sem.at[t, 2], in_plane(fx))
-            send(second, second, ag_send.at[t], ag_sem.at[t, 2], in_plane(fy))
+
+            @pl.when(collects(t))
+            def _():
+                first = wb.at[pl.ds(row, HALF)]
+                second = wb.at[pl.ds(aligned(row + HALF, 16), HALF)]
+                send(first, first, ag_send.at[t], ag_sem.at[t, 0], in_plane(fy))
+                send(second, second, ag_send.at[t], ag_sem.at[t, 1], in_plane(fx))
+                send(first, first, ag_send.at[t], ag_sem.at[t, 2], in_plane(fx))
+                send(second, second, ag_send.at[t], ag_sem.at[t, 2], in_plane(fy))
+
             send(whole, whole, ag_send.at[t], ag_sem.at[t, 3], in_plane(fc))
 
-        @pl.when(both(t >= 2, t < count + 2))
+        @pl.when(both(both(t >= 2, t < count + 2), collects(t - 2)))
         def _():
             i = t - 2
             layer, unit = forward_unit(i)
@@ -665,23 +702,37 @@
             send(first, first, ag_send.at[i], ag_sem.at[i, 2], in_plane(fx))
             send(second, second, ag_send.at[i], ag_sem.at[i, 2], in_plane(fy))
 
-        @pl.when(both(t >= 4, t < count + 4))
+        @pl.when(both(both(t >= 4, t < count + 4), collects(t - 4)))
         def _():
             i = t - 4
             layer, unit = forward_unit(i)
             wait_rows(ag_sem.at[i, 2], 4 * HALF)
             for yy, xx in ((1 - y, x), (y, 1 - x), (1 - y, 1 - x)):
                 piece = wb.at[pl.ds(unit_row(layer, unit, block(yy, xx, c)), SHARD)]
+
+                @pl.when(role(i) > 0)
+                def _(piece=piece):
+                    send(piece, piece, ag_send.at[i], ag_sem.at[i, 0], along(z_near))
+
                 send(piece, piece, ag_send.at[i], ag_sem.at[i, 3], in_plane(fc))
 
-        @pl.when(both(t >= 5, t < count + 5))
-        def _():
-            wait_rows(ag_sem.at[t - 5, 3], 4 * SHARD)
+        @pl.when(both(both(t >= LAG_PASS, t < count + LAG_PASS), role(t - LAG_PASS) == 2 - parity))
+        def _():
+            i = t - LAG_PASS
+            layer, unit = forward_unit(i)
+            wait_rows(ag_sem.at[i, 0], 3 * SHARD)
+            for yy, xx in ((1 - y, x), (y, 1 - x), (1 - y, 1 - x)):
+                piece = wb.at[pl.ds(unit_row(layer, unit, block(yy, xx, c)), SHARD)]
+                send(piece, piece, ag_send.at[i], ag_sem.at[i, 3], in_plane(fc))
+
+        @pl.when(both(t >= LAG_WHOLE, t < count + LAG_WHOLE))
+        def _():
+            wait_rows(ag_sem.at[t - LAG_WHOLE, 3], 4 * SHARD)
 
     for hop, peer in enumerate(peers):
-        send(vec_shard, vsg.at[f], vec_send.at[hop], vec_recv.at[hop], in_plane(peer))
-
-    @pl.loop(0, 5)
+        send(vsg.at[f], vsg.at[f], vec_send.at[hop], vec_recv.at[hop], in_plane(peer))
+
+    @pl.loop(0, EARLY)
     def _(t):
         gather_tick(t)
 
@@ -703,7 +754,7 @@
     xs[0, 0:ROWS, :] = tokens[...].astype(F32)
 
     for hop in range(7):
-        pltpu.make_async_copy(vec_shard, vec_shard, vec_recv.at[hop]).wait()
+        pltpu.make_async_copy(vsg.at[0], vsg.at[0], vec_recv.at[hop]).wait()
     spread = jnp.zeros((8 * layers, D), F32)
     for owner in range(8):
         at_row = lax.broadcasted_iota(jnp.int32, (128, D), 0)
@@ -712,6 +763,10 @@
         spread = spread + nn(vsg[owner, :, 0:128], jnp.where(hit, 1.0, 0.0).astype(BF16))
         ubs[:, owner * 384 : (owner + 1) * 384] = vsg[owner, :, 128:512].astype(F32)
     vec[...] = spread
+
+    @pl.loop(EARLY, LAG_WHOLE)
+    def _(t):
+        gather_tick(t)
 
     def vector(layer, which):
         return vec[pl.ds(layer * 8 + which, 1), :]
@@ -737,9 +792,9 @@
 
     @pl.loop(0, layers)
     def _(layer):
-        base = layer * UNITS + 5
-
-        @pl.loop(0, PAD // STEP)
+        base = layer * UNITS + LAG_WHOLE
+
+        @pl.loop(0, PAD // STEP, unroll=UNROLL)
         def _(step):
             rows = step_rows(step)
             normed, _unused = stats(xs[layer, rows, :])
@@ -752,7 +807,7 @@
             bias = is_q.astype(F32) * vector(layer, V_QB) + is_v.astype(F32) * vector(layer, V_VB)
             acc[...] = nn(nr[layer], wb[weight(layer, part), :])
 
-            @pl.loop(0, PAD // STEP)
+            @pl.loop(0, PAD // STEP, unroll=UNROLL)
             def _(step):
                 rows = step_rows(step)
                 pj[layer, part, rows, :] = (acc[rows, :] + bias).astype(BF16)
@@ -785,7 +840,7 @@
 
         acc[...] = nn(mx[layer], wb[weight(layer, 3), :])
 
-        @pl.loop(0, PAD // STEP)
+        @pl.loop(0, PAD // STEP, unroll=UNROLL)
         def _(step):
             rows = step_rows(step)
             now = xs[layer, rows, :] + acc[rows, :] + vector(layer, V_OB)
@@ -799,7 +854,7 @@
             bias = ubs[pl.ds(layer * 8, 1), pl.ds(aligned(part * D, 128), D)]
             acc[...] = nn(n2[layer], wb[weight(layer, 4 + part), :])
 
-            @pl.loop(0, PAD // STEP)
+            @pl.loop(0, PAD // STEP, unroll=UNROLL)
             def _(step):
                 rows = step_rows(step)
                 pre = acc[rows, :] + bias
@@ -824,17 +879,41 @@
 
     @pl.loop(0, count)
     def _(i):
-        wait_rows(ag_send.at[i], 7 * SHARD)
+        @pl.when(role(i) == 0)
+        def _():
+            wait_rows(ag_send.at[i], 7 * SHARD)
+
+        @pl.when(role(i) == 1 + parity)
+        def _():
+            wait_rows(ag_send.at[i], 10 * SHARD)
+
+        @pl.when(role(i) == 2 - parity)
+        def _():
+            wait_rows(ag_send.at[i], 4 * SHARD)
 
     for hop in range(7):
-        pltpu.make_async_copy(vec_shard, vec_shard, vec_send.at[hop]).wait()
+        pltpu.make_async_copy(vsg.at[0], vsg.at[0], vec_send.at[hop]).wait()
 
     def here_row(i, owner):
-        layer, unit = backward_unit(layers, i)
+        layer, unit, _half = backward_unit(layers, i)
         return unit_row(layer, unit, owner)
 
-    def half_rows(row, half):
-        return pl.ds(aligned(row + half * HALF, 16), HALF)
+    def columns(i):
+        return pl.ds(aligned(lax.rem(i, PARTS) * WIDE, 128), WIDE)
+
+    def shard_at(i, owner):
+        return wb.at[pl.ds(here_row(i, owner), SHARD), columns(i)]
+
+    def half_at(i, owner, half):
+        row = here_row(i, owner) + half * HALF
+        return wb.at[pl.ds(aligned(row, 16), HALF), columns(i)]
+
+    def wait_piece(sem, rows):
+        span = wb.at[pl.ds(0, rows), pl.ds(0, WIDE)]
+        pltpu.make_async_copy(span, span, sem).wait()
+
+    def during(t, lag):
+        return both(t >= lag, t < pieces + lag)
 
     def credit_wait(i, which):
         @pl.when(i >= SLOTS)
@@ -842,137 +921,146 @@
             pl.semaphore_wait(credit.at[which], 1)
 
     def credit_give(i, which, who):
-        @pl.when(i + SLOTS < count)
+        @pl.when(i + SLOTS < pieces)
         def _():
             pl.semaphore_signal(credit.at[which], inc=1, device_id=who, device_id_type=MESH)
 
     def reduce_tick(t):
-        @pl.when(t < count)
+        @pl.when(t < pieces)
         def _():
             slot = lax.rem(t, SLOTS)
             credit_wait(t, 0)
             for place in range(4):
-                source = wb.at[pl.ds(here_row(t, 2 * place + 1 - c), SHARD)]
                 send(
-                    source,
+                    shard_at(t, 2 * place + 1 - c),
                     rc.at[slot, pl.ds(place * SHARD, SHARD)],
                     s0_send.at[t],
                     core_sem.at[t],
                     in_plane(fc),
                 )
 
-        @pl.when(both(t >= 11, t < count + 11))
-        def _():
-            i = t - 11
-            layer, unit = backward_unit(layers, i)
-
-            @pl.when(outer)
-            def _():
-                wait_rows(z_sem.at[i, 2], SHARD)
-
-            done = wb.at[pl.ds(unit_row(layer, unit, fc), SHARD)]
-
-            @pl.when(unit < 3)
-            def _():
-                target = g_qkv.at[layer, :, pl.ds(aligned(unit * D, 128), D)]
-                pltpu.make_async_copy(done, target, out_sem.at[i]).start()
-
-            @pl.when(unit == 3)
-            def _():
-                pltpu.make_async_copy(done, g_out.at[layer], out_sem.at[i]).start()
-
-            @pl.when(both(unit >= 4, unit < 8))
-            def _():
-                target = g_up.at[layer, :, pl.ds(aligned((unit - 4) * D, 128), D)]
-                pltpu.make_async_copy(done, target, out_sem.at[i]).start()
-
-            @pl.when(unit >= 8)
-            def _():
-                target = g_down.at[layer, pl.ds(aligned((unit - 8) * SHARD, 16), SHARD)]
-                pltpu.make_async_copy(done, target, out_sem.at[i]).start()
-
-        @pl.when(both(inner, both(t >= 9, t < count + 9)))
-        def _():
-            i = t - 9
+        @pl.when(during(t, LAG_XY))
+        def _():
+            i = t - LAG_XY
             slot = lax.rem(i, SLOTS)
-            wait_rows(z_sem.at[i, 1], SHARD)
-            own = here_row(i, f)
-            done = pl.ds(here_row(i, fc), SHARD)
-            wb[done, :] = wb[pl.ds(own, SHARD), :] + rz[slot, 1]
-            credit_give(i, 4, along(z_pair))
-            send(wb.at[done], wb.at[done], rs_send.at[i], z_sem.at[i, 2], along(z_out))
-
-        @pl.when(both(inner, both(t >= 7, t < count + 7)))
-        def _():
-            i = t - 7
-            slot = lax.rem(i, SLOTS)
-            wait_rows(z_sem.at[i, 0], SHARD)
-            own = pl.ds(here_row(i, f), SHARD)
-            wb[own, :] = wb[own, :] + rz[slot, 0]
-            credit_give(i, 3, along(z_out))
-            credit_wait(i, 4)
-            send(wb.at[own], rz.at[slot, 1], rs_send.at[i], z_sem.at[i, 1], along(z_pair))
-
-        @pl.when(both(t >= 5, t < count + 5))
-        def _():
-            i = t - 5
-            slot = lax.rem(i, SLOTS)
-            wait_rows(last_sem.at[i], SHARD)
-            own = pl.ds(here_row(i, f), SHARD)
-            spare = pl.ds(here_row(i, fc), SHARD)
-            wb[own, :] = wb[own, :] + wb[spare, :]
-
-            @pl.when(outer)
-            def _():
-                credit_wait(i, 3)
-                send(wb.at[own], rz.at[slot, 0], rs_send.at[i], z_sem.at[i, 0], along(z_in))
-
-        @pl.when(both(t >= 3, t < count + 3))
-        def _():
-            i = t - 3
-            slot = lax.rem(i, SLOTS)
-            wait_rows(xy_sem.at[i], 4 * HALF)
+            wait_piece(xy_sem.at[i], 4 * HALF)
             for other in range(2):
-                span = half_rows(here_row(i, block(other, x, c)), 0)
-                wb[span, :] = wb[span, :] + r2[slot, pl.ds(other * HALF, HALF), :]
-                span = half_rows(here_row(i, block(y, other, c)), 1)
-                wb[span, :] = wb[span, :] + r2[slot, pl.ds((2 + other) * HALF, HALF), :]
+                span = half_at(i, block(other, x, c), 0)
+                span[...] = span[...] + r2[slot, pl.ds(other * HALF, HALF), :]
+                span = half_at(i, block(y, other, c), 1)
+                span[...] = span[...] + r2[slot, pl.ds((2 + other) * HALF, HALF), :]
             credit_give(i, 1, in_plane(fx))
             credit_give(i, 2, in_plane(fy))
-            first = wb.at[half_rows(here_row(i, block(1 - y, x, c)), 0)]
-            second = wb.at[half_rows(here_row(i, block(y, 1 - x, c)), 1)]
-            spare_y = here_row(i, block(1 - y, x, 1 - c))
-            spare_x = here_row(i, block(y, 1 - x, 1 - c))
-            send(first, wb.at[half_rows(spare_y, 0)], rs_send.at[i], last_sem.at[i], in_plane(fy))
-            send(second, wb.at[half_rows(spare_x, 1)], rs_send.at[i], last_sem.at[i], in_plane(fx))
-
-        @pl.when(both(t >= 1, t < count + 1))
+            send(
+                half_at(i, block(1 - y, x, c), 0),
+                half_at(i, block(1 - y, x, 1 - c), 0),
+                rs_send.at[i],
+                last_sem.at[i],
+                in_plane(fy),
+            )
+            send(
+                half_at(i, block(y, 1 - x, c), 1),
+                half_at(i, block(y, 1 - x, 1 - c), 1),
+                rs_send.at[i],
+                last_sem.at[i],
+                in_plane(fx),
+            )
+
+        @pl.when(during(t, 1))
         def _():
             i = t - 1
             slot = lax.rem(i, SLOTS)
-            wait_rows(core_sem.at[i], 4 * SHARD)
-            wait_rows(s0_send.at[i], 4 * SHARD)
+            wait_piece(core_sem.at[i], 4 * SHARD)
+            wait_piece(s0_send.at[i], 4 * SHARD)
             for place in range(4):
-                span = pl.ds(here_row(i, 2 * place + c), SHARD)
-                wb[span, :] = wb[span, :] + rc[slot, pl.ds(place * SHARD, SHARD), :]
+                span = shard_at(i, 2 * place + c)
+                span[...] = span[...] + rc[slot, pl.ds(place * SHARD, SHARD), :]
             credit_give(i, 0, in_plane(fc))
             credit_wait(i, 1)
             credit_wait(i, 2)
             for other in range(2):
                 send(
-                    wb.at[half_rows(here_row(i, block(other, 1 - x, c)), 0)],
+                    half_at(i, block(other, 1 - x, c), 0),
                     r2.at[slot, pl.ds(other * HALF, HALF)],
                     rs_send.at[i],
                     xy_sem.at[i],
                     in_plane(fx),
                 )
                 send(
-                    wb.at[half_rows(here_row(i, block(1 - y, other, c)), 1)],
+                    half_at(i, block(1 - y, other, c), 1),
                     r2.at[slot, pl.ds((2 + other) * HALF, HALF)],
                     rs_send.at[i],
                     xy_sem.at[i],
                     in_plane(fy),
                 )
+
+        @pl.when(during(t, LAG_LAST))
+        def _():
+            i = t - LAG_LAST
+            slot = lax.rem(i, SLOTS)
+            wait_piece(last_sem.at[i], SHARD)
+            own = shard_at(i, f)
+            own[...] = own[...] + shard_at(i, fc)[...]
+
+            @pl.when(outer)
+            def _():
+                credit_wait(i, 3)
+                send(own, rz.at[slot, 0], rs_send.at[i], z_sem.at[i, 0], along(z_in))
+
+        @pl.when(both(inner, during(t, LAG_Z1)))
+        def _():
+            i = t - LAG_Z1
+            slot = lax.rem(i, SLOTS)
+            wait_piece(z_sem.at[i, 0], SHARD)
+            own = shard_at(i, f)
+            own[...] = own[...] + rz[slot, 0]
+            credit_give(i, 3, along(z_out))
+            credit_wait(i, 4)
+            send(own, rz.at[slot, 1], rs_send.at[i], z_sem.at[i, 1], along(z_pair))
+
+        @pl.when(both(inner, during(t, LAG_Z2)))
+        def _():
+            i = t - LAG_Z2
+            slot = lax.rem(i, SLOTS)
+            wait_piece(z_sem.at[i, 1], SHARD)
+            done = shard_at(i, fc)
+            done[...] = shard_at(i, f)[...] + rz[slot, 1]
+            credit_give(i, 4, along(z_pair))
+            send(done, done, rs_send.at[i], z_sem.at[i, 2], along(z_out))
+
+        @pl.when(during(t, LAG_OUT))
+        def _():
+            i = t - LAG_OUT
+            layer, unit, half = backward_unit(layers, i)
+
+            @pl.when(outer)
+            def _():
+                wait_piece(z_sem.at[i, 2], SHARD)
+
+            done = shard_at(i, fc)
+
+            def emit(target):
+                pltpu.make_async_copy(done, target, out_sem.at[i]).start()
+
+            def wide_at(first):
+                return pl.ds(aligned((unit - first) * D + half * WIDE, 128), WIDE)
+
+            @pl.when(unit < 3)
+            def _():
+                emit(g_qkv.at[layer, :, wide_at(0)])
+
+            @pl.when(unit == 3)
+            def _():
+                emit(g_out.at[layer, :, columns(i)])
+
+            @pl.when(both(unit >= 4, unit < 8))
+            def _():
+                emit(g_up.at[layer, :, wide_at(4)])
+
+            @pl.when(unit >= 8)
+            def _():
+                rows = pl.ds(aligned((unit - 8) * SHARD, 16), SHARD)
+                emit(g_down.at[layer, rows, columns(i)])
 
     def vector_step(layer, step):
         mine = g_vec.at[layer]
@@ -1049,7 +1137,7 @@
     @pl.loop(0, layers)
     def _(turn):
         layer = layers - 1 - turn
-        base = turn * UNITS
+        base = turn * UNITS * PARTS
         for row in range(12, 16):
             g_vec[layer, row : row + 1, :] = jnp.zeros((1, D), F32)
 
@@ -1059,7 +1147,26 @@
             br[rows, :] = rounded
             return carry + fold(rounded.astype(F32))
 
-        put_vector(layer, V_DB, lax.fori_loop(0, PAD // STEP, branch_two, none))
+        put_vector(layer, V_DB, lax.fori_loop(0, PAD // STEP, branch_two, none, unroll=UNROLL))
+
+        @pl.loop(0, 4)
+        def _(part):
+            @pl.when(turn > 0)
+            def _():
+                reduce_tick(base - HELD + part)
+
+            acc[...] = nt(br[...], wb[weight(layer, 8 + part), :])
+
+            def through_gelu(step, carry):
+                rows = step_rows(step)
+                value = (acc[rows, :] * gp[layer, part, rows, :].astype(F32)).astype(BF16)
+                gb[part, rows, :] = value
+                return carry + fold(value.astype(F32))
+
+            put_vector(layer, V_UB + part, lax.fori_loop(0, PAD // STEP, through_gelu, none, unroll=UNROLL))
+            weight_grad(layer * LAYER_ROWS + DOWN_AT + part * D, hd.at[layer, part], br)
+
+        acc[...] = jnp.zeros((PAD, D), F32)
 
         @pl.loop(0, 4)
         def _(part):
@@ -1067,28 +1174,12 @@
             def _():
                 vector_step(layer + 1, part)
 
-            acc[...] = nt(br[...], wb[weight(layer, 8 + part), :])
-
-            def through_gelu(step, carry):
-                rows = step_rows(step)
-                value = (acc[rows, :] * gp[layer, part, rows, :].astype(F32)).astype(BF16)
-                gb[part, rows, :] = value
-                return carry + fold(value.astype(F32))
-
-            put_vector(layer, V_UB + part, lax.fori_loop(0, PAD // STEP, through_gelu, none))
-            weight_grad(layer * LAYER_ROWS + DOWN_AT + part * D, hd.at[layer, part], br)
-
-        acc[...] = jnp.zeros((PAD, D), F32)
-
-        @pl.loop(0, 4)
-        def _(part):
-            @pl.when(both(turn > 0, part < 3))
-            def _():
-                vector_step(layer + 1, part + 4)
-
             acc[...] += nt(gb[part], wb[weight(layer, 4 + part), :])
             weight_grad(layer * LAYER_ROWS + (4 + part) * D, n2.at[layer], gb.at[part])
-            reduce_tick(base + part)
+
+            @pl.loop(0, 2)
+            def _(again):
+                reduce_tick(base + 2 * part + again)
 
         def norm_back(source, gain_at, shift_at):
             def body(step, carry):
@@ -1102,21 +1193,27 @@
                 up[rows, :] = up[rows, :] + back
                 return gain_sum + fold(grad * normed), shift_sum + fold(grad)
 
-            gain_sum, shift_sum = lax.fori_loop(0, PAD // STEP, body, (none, none))
+            gain_sum, shift_sum = lax.fori_loop(0, PAD // STEP, body, (none, none), unroll=UNROLL)
             put_vector(layer, gain_at, gain_sum)
             put_vector(layer, shift_at, shift_sum)
 
         norm_back(x1, V_G2, V_B2)
 
-        put_vector(layer, V_OB, lax.fori_loop(0, PAD // STEP, branch_two, none))
+        put_vector(layer, V_OB, lax.fori_loop(0, PAD // STEP, branch_two, none, unroll=UNROLL))
         gm[...] = nt(br[...], wb[weight(layer, 3), :]).astype(BF16)
         weight_grad(layer * LAYER_ROWS + 3 * D, mx.at[layer], br)
 
+        @pl.loop(0, 2)
+        def _(again):
+            reduce_tick(base + 8 + again)
+
         @pl.loop(0, HEADS // 2)
         def _(pair):
-            @pl.when(lax.rem(pair, 2) == 0)
+            reduce_tick(base + 10 + pair)
+
+            @pl.when(both(turn > 0, pair < 3))
             def _():
-                reduce_tick(base + 4 + lax.div(pair, 2))
+                vector_step(layer + 1, pair + 4)
 
             lanes = pl.ds(aligned(pair * 128, 128), 128)
             kacc[...] = jnp.zeros((PAD, 128), F32)
@@ -1155,7 +1252,7 @@
             def column_sum(step, carry, part=part):
                 return carry + fold(gb[part, step_rows(step), :].astype(F32))
 
-            put_vector(layer, which, lax.fori_loop(0, PAD // STEP, column_sum, none))
+            put_vector(layer, which, lax.fori_loop(0, PAD // STEP, column_sum, none, unroll=UNROLL))
 
         acc[...] = jnp.zeros((PAD, D), F32)
 
@@ -1163,35 +1260,96 @@
         def _(part):
             acc[...] += nt(gb[part], wb[weight(layer, part), :])
             weight_grad(layer * LAYER_ROWS + part * D, nr.at[layer], gb.at[part])
-            reduce_tick(base + 7 + part)
+
+            @pl.when(part == 0)
+            def _():
+                reduce_tick(base + 16)
+
+            reduce_tick(base + 17 + part)
 
         norm_back(xs, V_G1, V_B1)
 
-        @pl.loop(0, 2)
-        def _(part):
-            reduce_tick(base + 10 + part)
-
     tokens_grad[...] = up[0:ROWS, :]
 
-    @pl.loop(count, count + 11)
+    @pl.loop(pieces - HELD, pieces + LAG_OUT)
     def _(t):
-        @pl.when(t < count + 7)
-        def _():
-            vector_step(0, t - count)
+        step = t - (pieces - HELD)
+
+        @pl.when(both(lax.rem(step, 2) == 0, step < 14))
+        def _():
+            vector_step(0, lax.div(step, 2))
 
         reduce_tick(t)
 
-    @pl.loop(0, count)
+    @pl.loop(0, pieces)
     def _(i):
-        wait_rows(out_sem.at[i], SHARD)
+        wait_piece(out_sem.at[i], SHARD)
 
         @pl.when(outer)
         def _():
-            wait_rows(rs_send.at[i], 4 * SHARD)
+            wait_piece(rs_send.at[i], 4 * SHARD)
 
         @pl.when(inner)
         def _():
-            wait_rows(rs_send.at[i], 5 * SHARD)
+            wait_piece(rs_send.at[i], 5 * SHARD)
+
+
+def closing_kernel(layers, *refs):
+    encoded_in, tokens_in, vec_in = refs[:3]
+    grads_in = refs[3:7]
+    encoded_out, tokens_out = refs[7:9]
+    small_out = refs[9:18]
+    grads_out = refs[18:22]
+    vec = refs[22]
+    narrow = refs[23:27]
+    wide = refs[27:31]
+    held_encoded, held_tokens, few_sem, in_sem, out_sem = refs[31:]
+    f = lax.axis_index("fsdp")
+    copies = [
+        pltpu.make_async_copy(vec_in, vec, few_sem.at[0]),
+        pltpu.make_async_copy(encoded_in, held_encoded, few_sem.at[1]),
+        pltpu.make_async_copy(tokens_in, held_tokens, few_sem.at[2]),
+    ]
+    reads, writes = [], []
+    for layer in range(layers):
+        for at in range(4):
+            reads.append(
+                pltpu.make_async_copy(
+                    grads_in[at].at[layer], narrow[at].at[layer], in_sem.at[at, layer]
+                )
+            )
+            writes.append(
+                pltpu.make_async_copy(
+                    wide[at].at[layer], grads_out[at].at[layer], out_sem.at[at, layer]
+                )
+            )
+    for copy in reads + copies:
+        copy.start()
+    for layer in range(layers):
+        for at in range(4):
+            reads[4 * layer + at].wait()
+            wide[at][layer] = narrow[at][layer].astype(F32)
+            writes[4 * layer + at].start()
+    for copy in copies:
+        copy.wait()
+    writes.append(pltpu.make_async_copy(held_encoded, encoded_out, few_sem.at[1]))
+    writes.append(pltpu.make_async_copy(held_tokens, tokens_out, few_sem.at[2]))
+    writes[-2].start()
+    writes[-1].start()
+    for layer in range(layers):
+        mine = vec[layer]
+        shard = jnp.zeros((8, SHARD), F32)
+        ups = jnp.zeros((1, 4 * SHARD), F32)
+        for owner in range(8):
+            here = f == owner
+            shard = jnp.where(here, mine[0:8, owner * SHARD : (owner + 1) * SHARD], shard)
+            row, lane = 8 + owner // 2, (owner % 2) * 4 * SHARD
+            ups = jnp.where(here, mine[row : row + 1, lane : lane + 4 * SHARD], ups)
+        for which in range(8):
+            small_out[which][layer : layer + 1, :] = shard[which : which + 1]
+        small_out[8][layer : layer + 1, :] = ups
+    for copy in writes:
+        copy.wait()
 
 
 def kernel_local(
@@ -1212,26 +1370,11 @@
     down_bias,
 ):
     layers = qkv_weight.shape[0]
-    small = jnp.stack(
-        [
-            norm1_gain,
-            norm1_bias,
-            query_bias,
-            value_bias,
-            out_bias,
-            norm2_gain,
-            norm2_bias,
-            down_bias,
-        ],
-        axis=1,
-    ).reshape(8 * layers, SHARD)
-    small = jnp.pad(small, ((0, 0), (0, 128 - SHARD)))
-    wide = jnp.pad(up_bias[:, None, :], ((0, 0), (0, 7), (0, 0))).reshape(8 * layers, 4 * SHARD)
-    vec_shard = jnp.concatenate([small, wide], axis=1)
-
     count = layers * UNITS
+    pieces = count * PARTS
     vmem = pl.BlockSpec(memory_space=pltpu.VMEM)
-    hbm = pl.BlockSpec(memory_space=pl.ANY)
+    hbm = pl.BlockSpec(memory_space=pltpu.MemorySpace.HBM)
+    plain = pl.BlockSpec()
     dma = pltpu.SemaphoreType.DMA
     results = pl.pallas_call(
         functools.partial(encoder_kernel, layers),
@@ -1244,7 +1387,7 @@
             jax.ShapeDtypeStruct((layers, SHARD, FF), BF16),
             jax.ShapeDtypeStruct((layers, 4 * SHARD, D), BF16),
         ),
-        in_specs=[vmem] * 3 + [hbm] * 4,
+        in_specs=[vmem] * 2 + [plain] * 9 + [hbm] * 4,
         out_specs=(vmem, vmem, vmem, hbm, hbm, hbm, hbm),
         scratch_shapes=[
             pltpu.VMEM((layers * LAYER_ROWS, D), BF16),
@@ -1269,19 +1412,19 @@
             pltpu.VMEM((8 * layers, D), F32),
             pltpu.VMEM((8 * layers, FF), F32),
             pltpu.VMEM((layers, 5, 16, D), F32),
-            pltpu.VMEM((SLOTS, 4 * SHARD, D), BF16),
-            pltpu.VMEM((SLOTS, 4 * HALF, D), BF16),
-            pltpu.VMEM((SLOTS, 2, SHARD, D), BF16),
+            pltpu.VMEM((SLOTS, 4 * SHARD, WIDE), BF16),
+            pltpu.VMEM((SLOTS, 4 * HALF, WIDE), BF16),
+            pltpu.VMEM((SLOTS, 2, SHARD, WIDE), BF16),
             dma((count, 4)),
             dma((count,)),
             dma((count,)),
-            dma((count,)),
-            dma((count,)),
-            dma((count,)),
-            dma((count, 3)),
-            dma((count,)),
-            dma((count,)),
-            dma((count,)),
+            dma((pieces,)),
+            dma((pieces,)),
+            dma((pieces,)),
+            dma((pieces, 3)),
+            dma((pieces,)),
+            dma((pieces,)),
+            dma((pieces,)),
             dma((7,)),
             dma((7,)),
             dma((layers, 5)),
@@ -1291,29 +1434,58 @@
         compiler_params=pltpu.CompilerParams(
             collective_id=0, has_side_effects=True, vmem_limit_bytes=VMEM_BYTES
         ),
-    )(tokens, cotangent, vec_shard, qkv_weight, out_weight, up_weight, down_weight)
-    encoded, tokens_grad, g_vec, g_qkv, g_out, g_up, g_down = results
-    f = lax.axis_index("fsdp")
-    vectors = lax.dynamic_slice_in_dim(g_vec[:, :8], f * SHARD, SHARD, axis=2)
-    up_vector = lax.dynamic_slice_in_dim(
-        g_vec[:, 8:12].reshape(layers, FF), f * 4 * SHARD, 4 * SHARD, axis=1
-    )
+    )(
+        tokens,
+        cotangent,
+        norm1_gain,
+        norm1_bias,
+        query_bias,
+        value_bias,
+        out_bias,
+        norm2_gain,
+        norm2_bias,
+        down_bias,
+        up_bias,
+        qkv_weight,
+        out_weight,
+        up_weight,
+        down_weight,
+    )
+    shapes = [(layers, SHARD)] * 8 + [(layers, 4 * SHARD)]
+    shapes += [(layers, SHARD, 3 * D), (layers, SHARD, D), (layers, SHARD, FF)]
+    shapes += [(layers, 4 * SHARD, D)]
+    closing = pl.pallas_call(
+        functools.partial(closing_kernel, layers),
+        out_shape=[jax.ShapeDtypeStruct((ROWS, D), BF16), jax.ShapeDtypeStruct((ROWS, D), F32)]
+        + [jax.ShapeDtypeStruct(shape, F32) for shape in shapes],
+        in_specs=[hbm] * 7,
+        out_specs=[hbm] * 2 + [plain] * 9 + [hbm] * 4,
+        scratch_shapes=[pltpu.VMEM((layers, 16, D), F32)]
+        + [pltpu.VMEM(shape, BF16) for shape in shapes[9:]]
+        + [pltpu.VMEM(shape, F32) for shape in shapes[9:]]
+        + [pltpu.VMEM((ROWS, D), BF16), pltpu.VMEM((ROWS, D), F32)]
+        + [dma((3,)), dma((4, layers)), dma((4, layers))],
+        compiler_params=pltpu.CompilerParams(vmem_limit_bytes=VMEM_BYTES),
+    )(*results)
+    by = dict(zip(("encoded", "tokens_grad"), closing[:2]))
+    small = closing[2:11]
+    g_qkv, g_out, g_up, g_down = closing[11:]
     return (
-        encoded,
-        tokens_grad,
-        vectors[:, V_G1],
-        vectors[:, V_B1],
-        g_qkv.astype(F32),
-        vectors[:, V_QB],
-        vectors[:, V_VB],
-        g_out.astype(F32),
-        vectors[:, V_OB],
-        vectors[:, V_G2],
-        vectors[:, V_B2],
-        g_up.astype(F32),
-        up_vector,
-        g_down.astype(F32),
-        vectors[:, V_DB],
+        by["encoded"],
+        by["tokens_grad"],
+        small[V_G1],
+        small[V_B1],
+        g_qkv,
+        small[V_QB],
+        small[V_VB],
+        g_out,
+        small[V_OB],
+        small[V_G2],
+        small[V_B2],
+        g_up,
+        small[V_UB],
+        g_down,
+        small[V_DB],
     )
 
 

time: 313 us -> 267 us (0.85)
  Pallas kernels: 294 us -> 266 us
  local copies, waits for them, and re-layouts: 10.7 us -> 0 us
  other arithmetic: 7.4 us -> 0 us
    pallas_call x1, Pallas kernels: 294 us -> 261 us  [kernel_local(): pl.pallas_call(functools.partial(encoder_kernel, layers), out_shape=(jax....]
    unnamed x22 -> x0, local copies, waits for them, and re-layouts: 7.92 us -> none
    convert_element_type x4 -> x0, other arithmetic: 6.78 us -> none  [the longest x1 3.03 us: kernel_local(): g_up.astype(F32)]
    pallas_call x0 -> x1, Pallas kernels: none -> 5.74 us  [kernel_local(): pl.pallas_call(functools.partial(closing_kernel, layers), out_shape=[jax....]
where the time goes in v3:
time: 267 us
  Pallas kernels  266 us (100%)
    pallas_call x1, Pallas kernels, kernel_local(): pl.pallas_call(functools.partial(encoder_kernel, layers), out_shape=(jax....  261 us
    pallas_call x1, Pallas kernels, kernel_local(): pl.pallas_call(functools.partial(closing_kernel, layers), out_shape=[jax....  5.74 us

profile of v3, /device:TPU:0, one launch (start us, length us, event | category | flops | bytes accessed | tf_op | source)
XLA Modules:
  0.0 267.2 jit_solution(11927253672871462688)
XLA Ops:
  0.7 260.6 %shard_map.262 = (bf16[345,768]{1,0:T(8,128)(2,1)}, f32[345,768]{1,0:T(8,128)}, f32[2,16,768]{2,1,0:T(8,128)}, bf16[2,96,2304]{2,1,0:T(8,128)(2,1)}, bf16[2,96,7...) custom-call(bf16[345,768]{1,0:T(8,128)(2,1)} %tokens.1, bf16[345,768]{1,0:T(8,128)(2,1)} %cotangent.1, ...), custom_call_target="tpu_custom_call" | custom-call | tf_op jit(solution)/shard_map/pallas_call | solution.py:1379
  261.3 5.7 %shard_map.263 = (bf16[345,768]{1,0:T(8,128)(2,1)}, f32[345,768]{1,0:T(8,128)}, f32[2,96]{1,0:T(2,128)}, f32[2,96]{1,0:T(2,128)}, f32[2,96]{1,0:T(2,128)}, /*ind...) custom-call(bf16[345,768]{1,0:T(8,128)(2,1)} %get-tuple-element.37.r, ...), custom_call_target="tpu_custom_call" | custom-call | tf_op jit(solution)/shard_map/pallas_call | solution.py:1457

commit v4 on v3

--- a/solution.py
+++ b/solution.py
@@ -438,7 +438,7 @@
     )
 
 
-VMEM_BYTES = 63 * 1024 * 1024
+VMEM_BYTES = 65408 * 1024
 
 MESH = pl.DeviceIdType.MESH
 F32 = jnp.float32
@@ -452,15 +452,16 @@
 SHARD = 96
 HALF = 48
 UNITS = 12
-LAYER_ROWS = UNITS * D
-DOWN_AT = 8 * D
 SLOTS = 6
+CORE_SLOTS = 4
+RING = 8
 PARTS = 2
 WIDE = D // PARTS
-LAG_XY, LAG_LAST, LAG_Z1, LAG_Z2, LAG_OUT = 3, 5, 7, 9, 11
+LAG_XY, LAG_LAST, LAG_Z1, LAG_Z2, LAG_OUT = 4, 6, 8, 10, 12
 LAG_PASS, LAG_WHOLE = 8, 9
-HELD = 4
+EARLY_UNITS = 2
 EARLY = 3
+VEC_EVERY = 5
 TOP_ROWS = 208
 KEYS = 256
 LOW_KEY = PAD - KEYS
@@ -484,27 +485,20 @@
     return value if isinstance(value, int) else pl.multiple_of(value, by)
 
 
-def unit_row(layer, unit, owner):
-    is_down = unit // 8 if isinstance(unit, int) else lax.div(unit, 8)
-    plain = unit * D + owner * SHARD
-    down = DOWN_AT + owner * (4 * SHARD) + (unit - 8) * SHARD
-    return aligned(layer * LAYER_ROWS + (1 - is_down) * plain + is_down * down, 16)
-
-
-def forward_unit(index):
-    return lax.div(index, UNITS), lax.rem(index, UNITS)
+def twelfth(index):
+    return lax.div(index * 43, 512)
 
 
 def backward_unit(layers, index):
-    whole, half = lax.div(index, PARTS), lax.rem(index, PARTS)
-    turn, place = lax.div(whole, UNITS), lax.rem(whole, UNITS)
+    whole = lax.div(index, PARTS)
+    half = index - PARTS * whole
+    turn = twelfth(whole)
+    place = whole - UNITS * turn
     part = lax.div(place, 4)
+    within = place - 4 * part
     is_down, is_late = lax.div(2 - part, 2), lax.div(part, 2)
-    unit = (
-        is_down * (8 + place)
-        + (1 - is_down - is_late) * place
-        + is_late * lax.rem(place + 3, 4)
-    )
+    late = within + 3 - 4 * lax.div(within + 3, 4)
+    unit = is_down * 8 + (1 - is_late) * place + is_late * late
     return layers - 1 - turn, unit, half
 
 
@@ -572,7 +566,13 @@
     vsg,
     vec,
     ubs,
+    gv,
+    gvs,
     vr,
+    vz,
+    held,
+    held_cot,
+    held_grad,
     rc,
     r2,
     rz,
@@ -586,11 +586,9 @@
     s0_send,
     rs_send,
     out_sem,
-    vec_send,
-    vec_recv,
-    gv_send,
-    gv_recv,
-    credit,
+    vec_sem,
+    gv_sem,
+    io_sem,
 ):
     count = layers * UNITS
     pieces = count * PARTS
@@ -613,8 +611,8 @@
     along = lambda who: {"dp": who}
     both = lambda a, b: jnp.logical_and(a, b)
 
-    def block(yy, xx, cc):
-        return yy * 4 + xx * 2 + cc
+    first_rows = pl.ds(0, HALF)
+    second_rows = pl.ds(HALF, HALF)
 
     def send(source, target, sent, landed, who):
         pltpu.make_async_remote_copy(
@@ -626,16 +624,23 @@
             device_id_type=MESH,
         ).start()
 
-    def wait_rows(sem, rows):
-        span = wb.at[pl.ds(0, rows)]
+    def wait_blocks(sem, blocks):
+        span = wb.at[pl.ds(0, blocks), 0, 0, 0]
+        pltpu.make_async_copy(span, span, sem).wait()
+
+    def wait_half(sem):
+        span = wb.at[0, 0, 0, 0, pl.ds(0, HALF)]
+        pltpu.make_async_copy(span, span, sem).wait()
+
+    def wait_piece(sem, blocks):
+        span = wb.at[pl.ds(0, blocks), 0, 0, 0, :, pl.ds(0, WIDE)]
         pltpu.make_async_copy(span, span, sem).wait()
 
     barrier = pltpu.get_barrier_semaphore()
     peers = [lax.rem(f + hop, 8) for hop in range(1, 8)]
     for peer in peers:
         pl.semaphore_signal(barrier, inc=1, device_id=in_plane(peer), device_id_type=MESH)
-
-    for hop in (1, 3):
+    for hop in range(1, 4):
         beside = lax.rem(d + hop, 4)
         pl.semaphore_signal(barrier, inc=1, device_id=along(beside), device_id_type=MESH)
 
@@ -651,7 +656,7 @@
                 source = w_down.at[layer, pl.ds((unit - 8) * SHARD, SHARD)]
             pltpu.make_async_copy(
                 source,
-                wb.at[pl.ds(unit_row(layer, unit, f), SHARD)],
+                wb.at[layer * UNITS + unit, y, x, c],
                 own_sem.at[layer * UNITS + unit],
             ).start()
     vec[...] = jnp.zeros((8 * layers, D), F32)
@@ -663,7 +668,14 @@
     for layer in range(layers):
         vec[8 * layer : 8 * layer + 1, 128:512] = shard[layer : layer + 1]
     vsg[f] = vec[:, 0:512].astype(BF16)
-    pl.semaphore_wait(barrier, 9)
+    tokens_in = pltpu.make_async_copy(tokens, held, io_sem.at[0])
+    cotangent_in = pltpu.make_async_copy(cotangent, held_cot, io_sem.at[1])
+    encoded_out = pltpu.make_async_copy(held, encoded, io_sem.at[2])
+    tokens_out = pltpu.make_async_copy(held_grad, tokens_grad, io_sem.at[3])
+    tokens_in.start()
+    cotangent_in.start()
+    gvs[...] = jnp.zeros((8, 8, 512), F32)
+    pl.semaphore_wait(barrier, 10)
 
     def role(i):
         return lax.rem(i, 3) * lax.div(2 * count - 3 - i, count)
@@ -674,41 +686,35 @@
     def gather_tick(t):
         @pl.when(t < count)
         def _():
-            layer, unit = forward_unit(t)
-            row = unit_row(layer, unit, f)
-            wait_rows(own_sem.at[t], SHARD)
-            whole = wb.at[pl.ds(row, SHARD)]
+            own = wb.at[t, y, x, c]
+            wait_blocks(own_sem.at[t], 1)
 
             @pl.when(collects(t))
             def _():
-                first = wb.at[pl.ds(row, HALF)]
-                second = wb.at[pl.ds(aligned(row + HALF, 16), HALF)]
+                first = wb.at[t, y, x, c, first_rows]
+                second = wb.at[t, y, x, c, second_rows]
                 send(first, first, ag_send.at[t], ag_sem.at[t, 0], in_plane(fy))
                 send(second, second, ag_send.at[t], ag_sem.at[t, 1], in_plane(fx))
                 send(first, first, ag_send.at[t], ag_sem.at[t, 2], in_plane(fx))
                 send(second, second, ag_send.at[t], ag_sem.at[t, 2], in_plane(fy))
 
-            send(whole, whole, ag_send.at[t], ag_sem.at[t, 3], in_plane(fc))
+            send(own, own, ag_send.at[t], ag_sem.at[t, 3], in_plane(fc))
 
         @pl.when(both(both(t >= 2, t < count + 2), collects(t - 2)))
         def _():
             i = t - 2
-            layer, unit = forward_unit(i)
-            wait_rows(ag_sem.at[i, 0], HALF)
-            wait_rows(ag_sem.at[i, 1], HALF)
-            first = wb.at[pl.ds(unit_row(layer, unit, block(1 - y, x, c)), HALF)]
-            other = unit_row(layer, unit, block(y, 1 - x, c))
-            second = wb.at[pl.ds(aligned(other + HALF, 16), HALF)]
+            wait_half(ag_sem.at[i, 0])
+            wait_half(ag_sem.at[i, 1])
+            first = wb.at[i, 1 - y, x, c, first_rows]
+            second = wb.at[i, y, 1 - x, c, second_rows]
             send(first, first, ag_send.at[i], ag_sem.at[i, 2], in_plane(fx))
             send(second, second, ag_send.at[i], ag_sem.at[i, 2], in_plane(fy))
 
         @pl.when(both(both(t >= 4, t < count + 4), collects(t - 4)))
         def _():
             i = t - 4
-            layer, unit = forward_unit(i)
-            wait_rows(ag_sem.at[i, 2], 4 * HALF)
-            for yy, xx in ((1 - y, x), (y, 1 - x), (1 - y, 1 - x)):
-                piece = wb.at[pl.ds(unit_row(layer, unit, block(yy, xx, c)), SHARD)]
+            wait_blocks(ag_sem.at[i, 2], 2)
+            for piece in (wb.at[i, 1 - y, :, c], wb.at[i, y, 1 - x, c]):
 
                 @pl.when(role(i) > 0)
                 def _(piece=piece):
@@ -719,18 +725,16 @@
         @pl.when(both(both(t >= LAG_PASS, t < count + LAG_PASS), role(t - LAG_PASS) == 2 - parity))
         def _():
             i = t - LAG_PASS
-            layer, unit = forward_unit(i)
-            wait_rows(ag_sem.at[i, 0], 3 * SHARD)
-            for yy, xx in ((1 - y, x), (y, 1 - x), (1 - y, 1 - x)):
-                piece = wb.at[pl.ds(unit_row(layer, unit, block(yy, xx, c)), SHARD)]
+            wait_blocks(ag_sem.at[i, 0], 3)
+            for piece in (wb.at[i, 1 - y, :, c], wb.at[i, y, 1 - x, c]):
                 send(piece, piece, ag_send.at[i], ag_sem.at[i, 3], in_plane(fc))
 
         @pl.when(both(t >= LAG_WHOLE, t < count + LAG_WHOLE))
         def _():
-            wait_rows(ag_sem.at[t - LAG_WHOLE, 3], 4 * SHARD)
-
-    for hop, peer in enumerate(peers):
-        send(vsg.at[f], vsg.at[f], vec_send.at[hop], vec_recv.at[hop], in_plane(peer))
+            wait_blocks(ag_sem.at[t - LAG_WHOLE, 3], 4)
+
+    for peer in peers:
+        send(vsg.at[f], vsg.at[f], vec_sem.at[0], vec_sem.at[1], in_plane(peer))
 
     @pl.loop(0, EARLY)
     def _(t):
@@ -751,17 +755,21 @@
         mask[...] = jnp.where(same, 0.0, -1e30).astype(F32)
 
     xs[0, PAD - 8 :, :] = jnp.zeros((8, D), F32)
-    xs[0, 0:ROWS, :] = tokens[...].astype(F32)
-
-    for hop in range(7):
-        pltpu.make_async_copy(vsg.at[0], vsg.at[0], vec_recv.at[hop]).wait()
+    tokens_in.wait()
+    xs[0, 0:ROWS, :] = held[...].astype(F32)
+
+    seven = vsg.at[pl.ds(0, 7)]
+    pltpu.make_async_copy(seven, seven, vec_sem.at[1]).wait()
     spread = jnp.zeros((8 * layers, D), F32)
     for owner in range(8):
         at_row = lax.broadcasted_iota(jnp.int32, (128, D), 0)
         at_col = lax.broadcasted_iota(jnp.int32, (128, D), 1)
         hit = jnp.logical_and(at_col == at_row + owner * SHARD, at_row < SHARD)
         spread = spread + nn(vsg[owner, :, 0:128], jnp.where(hit, 1.0, 0.0).astype(BF16))
-        ubs[:, owner * 384 : (owner + 1) * 384] = vsg[owner, :, 128:512].astype(F32)
+        wide = vsg[owner, :, 128:512].astype(F32)
+        for layer in range(layers):
+            row, lane = 8 * layer, owner * 4 * SHARD
+            ubs[layer : layer + 1, lane : lane + 4 * SHARD] = wide[row : row + 1]
     vec[...] = spread
 
     @pl.loop(EARLY, LAG_WHOLE)
@@ -788,7 +796,175 @@
     )
 
     def weight(layer, unit):
-        return pl.ds(aligned(layer * LAYER_ROWS + unit * D, 16), D)
+        return wb[layer * UNITS + unit].reshape(D, D)
+
+    def down_places(part):
+        return [(unit, lax.div(part, 2), lax.rem(part, 2), core) for core in range(2) for unit in range(4)]
+
+    def down_weight(layer, part):
+        blocks = [wb[layer * UNITS + 8 + u, yy, xx, cc] for u, yy, xx, cc in down_places(part)]
+        return jnp.concatenate(blocks, axis=0)
+
+    def put_down(first, units, part, grad):
+        for at, (u, yy, xx, cc) in enumerate(down_places(part)):
+            if u < units:
+                wb[first + u, yy, xx, cc] = grad[at * SHARD : (at + 1) * SHARD]
+
+    def piece_at(i):
+        layer, unit, half = backward_unit(layers, i)
+        early = lax.div(pieces + EARLY_UNITS * PARTS - 1 - i, pieces)
+        ahead = layers * UNITS + lax.div(i, PARTS)
+        at = early * ahead + (1 - early) * (layer * UNITS + unit)
+        return at, pl.ds(aligned(half * WIDE, 128), WIDE)
+
+    def during(t, lag):
+        return both(t >= lag, t < pieces + lag)
+
+    def ring(i):
+        return lax.rem(i, RING)
+
+    def long_ring(i):
+        return lax.rem(i, 2 * RING)
+
+    def reduce_tick(t):
+        @pl.when(t < pieces)
+        def _():
+            n, cols = piece_at(t)
+            send(
+                wb.at[n, :, :, 1 - c, :, cols],
+                rc.at[lax.rem(t, CORE_SLOTS)],
+                s0_send.at[ring(t)],
+                core_sem.at[ring(t)],
+                in_plane(fc),
+            )
+
+        @pl.when(during(t, LAG_XY))
+        def _():
+            i = t - LAG_XY
+            n, cols = piece_at(i)
+            slot = lax.rem(i, SLOTS)
+            wait_piece(xy_sem.at[ring(i)], 2)
+            along_x = wb.at[n, :, x, c, first_rows, cols]
+            along_y = wb.at[n, y, :, c, second_rows, cols]
+            along_x[...] = along_x[...] + r2[slot, 0]
+            along_y[...] = along_y[...] + r2[slot, 1]
+            send(
+                wb.at[n, 1 - y, x, c, first_rows, cols],
+                wb.at[n, 1 - y, x, 1 - c, first_rows, cols],
+                rs_send.at[long_ring(i)],
+                last_sem.at[ring(i)],
+                in_plane(fy),
+            )
+            send(
+                wb.at[n, y, 1 - x, c, second_rows, cols],
+                wb.at[n, y, 1 - x, 1 - c, second_rows, cols],
+                rs_send.at[long_ring(i)],
+                last_sem.at[ring(i)],
+                in_plane(fx),
+            )
+
+        @pl.when(during(t, 1))
+        def _():
+            i = t - 1
+            n, cols = piece_at(i)
+            slot = lax.rem(i, SLOTS)
+            wait_piece(core_sem.at[ring(i)], 4)
+            wait_piece(s0_send.at[ring(i)], 4)
+            mine = wb.at[n, :, :, c, :, cols]
+            mine[...] = mine[...] + rc[lax.rem(i, CORE_SLOTS)]
+            send(
+                wb.at[n, :, 1 - x, c, first_rows, cols],
+                r2.at[slot, 0],
+                rs_send.at[long_ring(i)],
+                xy_sem.at[ring(i)],
+                in_plane(fx),
+            )
+            send(
+                wb.at[n, 1 - y, :, c, second_rows, cols],
+                r2.at[slot, 1],
+                rs_send.at[long_ring(i)],
+                xy_sem.at[ring(i)],
+                in_plane(fy),
+            )
+
+        @pl.when(during(t, LAG_OUT))
+        def _():
+            i = t - LAG_OUT
+            n, cols = piece_at(i)
+            layer, unit, half = backward_unit(layers, i)
+
+            @pl.when(outer)
+            def _():
+                wait_piece(z_sem.at[ring(i), 2], 1)
+
+            done = wb.at[n, y, x, 1 - c, :, cols]
+
+            @pl.when(outer)
+            def _():
+                wait_piece(rs_send.at[long_ring(i)], 4)
+
+            @pl.when(inner)
+            def _():
+                wait_piece(rs_send.at[long_ring(i)], 5)
+
+            @pl.when(i >= RING)
+            def _():
+                wait_piece(out_sem.at[ring(i)], 1)
+
+            def emit(target):
+                pltpu.make_async_copy(done, target, out_sem.at[ring(i)]).start()
+
+            def wide_at(first):
+                return pl.ds(aligned((unit - first) * D + half * WIDE, 128), WIDE)
+
+            @pl.when(unit < 3)
+            def _():
+                emit(g_qkv.at[layer, :, wide_at(0)])
+
+            @pl.when(unit == 3)
+            def _():
+                emit(g_out.at[layer, :, cols])
+
+            @pl.when(both(unit >= 4, unit < 8))
+            def _():
+                emit(g_up.at[layer, :, wide_at(4)])
+
+            @pl.when(unit >= 8)
+            def _():
+                rows = pl.ds(aligned((unit - 8) * SHARD, 16), SHARD)
+                emit(g_down.at[layer, rows, cols])
+
+        @pl.when(during(t, LAG_LAST))
+        def _():
+            i = t - LAG_LAST
+            n, cols = piece_at(i)
+            wait_piece(last_sem.at[ring(i)], 1)
+            own = wb.at[n, y, x, c, :, cols]
+            own[...] = own[...] + wb[n, y, x, 1 - c, :, cols]
+
+            @pl.when(outer)
+            def _():
+                to = rz.at[lax.rem(i, SLOTS), 0]
+                send(own, to, rs_send.at[long_ring(i)], z_sem.at[ring(i), 0], along(z_in))
+
+        @pl.when(both(inner, during(t, LAG_Z1)))
+        def _():
+            i = t - LAG_Z1
+            n, cols = piece_at(i)
+            slot = lax.rem(i, SLOTS)
+            wait_piece(z_sem.at[ring(i), 0], 1)
+            own = wb.at[n, y, x, c, :, cols]
+            own[...] = own[...] + rz[slot, 0]
+            send(own, rz.at[slot, 1], rs_send.at[long_ring(i)], z_sem.at[ring(i), 1], along(z_pair))
+
+        @pl.when(both(inner, during(t, LAG_Z2)))
+        def _():
+            i = t - LAG_Z2
+            n, cols = piece_at(i)
+            wait_piece(z_sem.at[ring(i), 1], 1)
+            done = wb.at[n, y, x, 1 - c, :, cols]
+            done[...] = wb[n, y, x, c, :, cols] + rz[lax.rem(i, SLOTS), 1]
+            send(done, done, rs_send.at[long_ring(i)], z_sem.at[ring(i), 2], along(z_out))
 
     @pl.loop(0, layers)
     def _(layer):
@@ -805,7 +981,7 @@
             gather_tick(base + part)
             is_q, is_v = lax.div(2 - part, 2), lax.div(part, 2)
             bias = is_q.astype(F32) * vector(layer, V_QB) + is_v.astype(F32) * vector(layer, V_VB)
-            acc[...] = nn(nr[layer], wb[weight(layer, part), :])
+            acc[...] = nn(nr[layer], weight(layer, part))
 
             @pl.loop(0, PAD // STEP, unroll=UNROLL)
             def _(step):
@@ -838,7 +1014,7 @@
                     )
                 mx[layer, here, lanes] = jnp.where(left_lane, results[0], results[1]).astype(BF16)
 
-        acc[...] = nn(mx[layer], wb[weight(layer, 3), :])
+        acc[...] = nn(mx[layer], weight(layer, 3))
 
         @pl.loop(0, PAD // STEP, unroll=UNROLL)
         def _(step):
@@ -851,8 +1027,8 @@
         @pl.loop(0, 4)
         def _(part):
             gather_tick(base + 4 + part)
-            bias = ubs[pl.ds(layer * 8, 1), pl.ds(aligned(part * D, 128), D)]
-            acc[...] = nn(n2[layer], wb[weight(layer, 4 + part), :])
+            bias = ubs[pl.ds(layer, 1), pl.ds(aligned(part * D, 128), D)]
+            acc[...] = nn(n2[layer], weight(layer, 4 + part))
 
             @pl.loop(0, PAD // STEP, unroll=UNROLL)
             def _(step):
@@ -863,283 +1039,116 @@
                 hd[layer, part, rows, :] = (pre * cdf).astype(BF16)
                 gp[layer, part, rows, :] = (cdf + pre * bell).astype(BF16)
 
+        @pl.when(layer == layers - 1)
+        def _():
+            acc[PAD - 8 :, :] = jnp.zeros((8, D), F32)
+            cotangent_in.wait()
+            acc[0:ROWS, :] = held_cot[...].astype(F32)
+            br[...] = acc[...].astype(BF16)
+
+            @pl.loop(0, 4)
+            def _(part):
+                grad = tn(hd[layer, part], br[...]).astype(BF16)
+                put_down(layers * UNITS, EARLY_UNITS, part, grad)
+
         @pl.loop(0, 4)
         def _(part):
             gather_tick(base + 8 + part)
 
+        @pl.when(layer == layers - 1)
+        def _():
+            @pl.loop(0, 2)
+            def _(t):
+                reduce_tick(t)
+
         acc[...] = x1[layer] + vector(layer, V_DB)
 
         @pl.loop(0, 4)
         def _(part):
-            acc[...] += nn(hd[layer, part], wb[weight(layer, 8 + part), :])
+            acc[...] += nn(hd[layer, part], down_weight(layer, part))
 
         xs[layer + 1] = acc[...]
 
-    encoded[...] = xs[layers, 0:ROWS, :].astype(BF16)
+    reduce_tick(2)
+    held[...] = xs[layers, 0:ROWS, :].astype(BF16)
+    encoded_out.start()
 
     @pl.loop(0, count)
     def _(i):
         @pl.when(role(i) == 0)
         def _():
-            wait_rows(ag_send.at[i], 7 * SHARD)
+            wait_blocks(ag_send.at[i], 7)
 
         @pl.when(role(i) == 1 + parity)
         def _():
-            wait_rows(ag_send.at[i], 10 * SHARD)
+            wait_blocks(ag_send.at[i], 10)
 
         @pl.when(role(i) == 2 - parity)
         def _():
-            wait_rows(ag_send.at[i], 4 * SHARD)
-
-    for hop in range(7):
-        pltpu.make_async_copy(vsg.at[0], vsg.at[0], vec_send.at[hop]).wait()
-
-    def here_row(i, owner):
-        layer, unit, _half = backward_unit(layers, i)
-        return unit_row(layer, unit, owner)
-
-    def columns(i):
-        return pl.ds(aligned(lax.rem(i, PARTS) * WIDE, 128), WIDE)
-
-    def shard_at(i, owner):
-        return wb.at[pl.ds(here_row(i, owner), SHARD), columns(i)]
-
-    def half_at(i, owner, half):
-        row = here_row(i, owner) + half * HALF
-        return wb.at[pl.ds(aligned(row, 16), HALF), columns(i)]
-
-    def wait_piece(sem, rows):
-        span = wb.at[pl.ds(0, rows), pl.ds(0, WIDE)]
-        pltpu.make_async_copy(span, span, sem).wait()
-
-    def during(t, lag):
-        return both(t >= lag, t < pieces + lag)
-
-    def credit_wait(i, which):
-        @pl.when(i >= SLOTS)
-        def _():
-            pl.semaphore_wait(credit.at[which], 1)
-
-    def credit_give(i, which, who):
-        @pl.when(i + SLOTS < pieces)
-        def _():
-            pl.semaphore_signal(credit.at[which], inc=1, device_id=who, device_id_type=MESH)
-
-    def reduce_tick(t):
-        @pl.when(t < pieces)
-        def _():
-            slot = lax.rem(t, SLOTS)
-            credit_wait(t, 0)
-            for place in range(4):
+            wait_blocks(ag_send.at[i], 4)
+
+    pltpu.make_async_copy(seven, seven, vec_sem.at[0]).wait()
+
+    def vector_step(layer, step):
+        def wait_vec(at, copies):
+            span = gvs.at[pl.ds(0, copies)]
+            pltpu.make_async_copy(span, span, gv_sem.at[layer, at]).wait()
+
+        @pl.when(step == 0)
+        def _():
+            for owner in range(8):
+                gvs[owner, :, 0:SHARD] = gv[layer, 0:8, owner * SHARD : (owner + 1) * SHARD]
+                row, lane = 8 + owner // 2, (owner % 2) * 4 * SHARD
+                gvs[owner, 0:1, 128:512] = gv[layer, row : row + 1, lane : lane + 4 * SHARD]
+            vr[layer, f] = gvs[f]
+            for peer in peers:
                 send(
-                    shard_at(t, 2 * place + 1 - c),
-                    rc.at[slot, pl.ds(place * SHARD, SHARD)],
-                    s0_send.at[t],
-                    core_sem.at[t],
-                    in_plane(fc),
+                    gvs.at[peer],
+                    vr.at[layer, f],
+                    gv_sem.at[layer, 0],
+                    gv_sem.at[layer, 1],
+                    in_plane(peer),
                 )
 
-        @pl.when(during(t, LAG_XY))
-        def _():
-            i = t - LAG_XY
-            slot = lax.rem(i, SLOTS)
-            wait_piece(xy_sem.at[i], 4 * HALF)
-            for other in range(2):
-                span = half_at(i, block(other, x, c), 0)
-                span[...] = span[...] + r2[slot, pl.ds(other * HALF, HALF), :]
-                span = half_at(i, block(y, other, c), 1)
-                span[...] = span[...] + r2[slot, pl.ds((2 + other) * HALF, HALF), :]
-            credit_give(i, 1, in_plane(fx))
-            credit_give(i, 2, in_plane(fy))
-            send(
-                half_at(i, block(1 - y, x, c), 0),
-                half_at(i, block(1 - y, x, 1 - c), 0),
-                rs_send.at[i],
-                last_sem.at[i],
-                in_plane(fy),
-            )
-            send(
-                half_at(i, block(y, 1 - x, c), 1),
-                half_at(i, block(y, 1 - x, 1 - c), 1),
-                rs_send.at[i],
-                last_sem.at[i],
-                in_plane(fx),
-            )
-
-        @pl.when(during(t, 1))
-        def _():
-            i = t - 1
-            slot = lax.rem(i, SLOTS)
-            wait_piece(core_sem.at[i], 4 * SHARD)
-            wait_piece(s0_send.at[i], 4 * SHARD)
-            for place in range(4):
-                span = shard_at(i, 2 * place + c)
-                span[...] = span[...] + rc[slot, pl.ds(place * SHARD, SHARD), :]
-            credit_give(i, 0, in_plane(fc))
-            credit_wait(i, 1)
-            credit_wait(i, 2)
-            for other in range(2):
+        @pl.when(step == 1)
+        def _():
+            wait_vec(0, 7)
+            wait_vec(1, 7)
+            in_sum = vr[layer, 0]
+            for source in range(1, 8):
+                in_sum = in_sum + vr[layer, source]
+            vz[layer, d] = in_sum
+            for hop in range(3):
                 send(
-                    half_at(i, block(other, 1 - x, c), 0),
-                    r2.at[slot, pl.ds(other * HALF, HALF)],
-                    rs_send.at[i],
-                    xy_sem.at[i],
-                    in_plane(fx),
+                    vz.at[layer, d],
+                    vz.at[layer, d],
+                    gv_sem.at[layer, 2],
+                    gv_sem.at[layer, 3],
+                    along(lax.rem(d + 1 + hop, 4)),
                 )
-                send(
-                    half_at(i, block(1 - y, other, c), 1),
-                    r2.at[slot, pl.ds((2 + other) * HALF, HALF)],
-                    rs_send.at[i],
-                    xy_sem.at[i],
-                    in_plane(fy),
-                )
-
-        @pl.when(during(t, LAG_LAST))
-        def _():
-            i = t - LAG_LAST
-            slot = lax.rem(i, SLOTS)
-            wait_piece(last_sem.at[i], SHARD)
-            own = shard_at(i, f)
-            own[...] = own[...] + shard_at(i, fc)[...]
-
-            @pl.when(outer)
-            def _():
-                credit_wait(i, 3)
-                send(own, rz.at[slot, 0], rs_send.at[i], z_sem.at[i, 0], along(z_in))
-
-        @pl.when(both(inner, during(t, LAG_Z1)))
-        def _():
-            i = t - LAG_Z1
-            slot = lax.rem(i, SLOTS)
-            wait_piece(z_sem.at[i, 0], SHARD)
-            own = shard_at(i, f)
-            own[...] = own[...] + rz[slot, 0]
-            credit_give(i, 3, along(z_out))
-            credit_wait(i, 4)
-            send(own, rz.at[slot, 1], rs_send.at[i], z_sem.at[i, 1], along(z_pair))
-
-        @pl.when(both(inner, during(t, LAG_Z2)))
-        def _():
-            i = t - LAG_Z2
-            slot = lax.rem(i, SLOTS)
-            wait_piece(z_sem.at[i, 1], SHARD)
-            done = shard_at(i, fc)
-            done[...] = shard_at(i, f)[...] + rz[slot, 1]
-            credit_give(i, 4, along(z_pair))
-            send(done, done, rs_send.at[i], z_sem.at[i, 2], along(z_out))
-
-        @pl.when(during(t, LAG_OUT))
-        def _():
-            i = t - LAG_OUT
-            layer, unit, half = backward_unit(layers, i)
-
-            @pl.when(outer)
-            def _():
-                wait_piece(z_sem.at[i, 2], SHARD)
-
-            done = shard_at(i, fc)
-
-            def emit(target):
-                pltpu.make_async_copy(done, target, out_sem.at[i]).start()
-
-            def wide_at(first):
-                return pl.ds(aligned((unit - first) * D + half * WIDE, 128), WIDE)
-
-            @pl.when(unit < 3)
-            def _():
-                emit(g_qkv.at[layer, :, wide_at(0)])
-
-            @pl.when(unit == 3)
-            def _():
-                emit(g_out.at[layer, :, columns(i)])
-
-            @pl.when(both(unit >= 4, unit < 8))
-            def _():
-                emit(g_up.at[layer, :, wide_at(4)])
-
-            @pl.when(unit >= 8)
-            def _():
-                rows = pl.ds(aligned((unit - 8) * SHARD, 16), SHARD)
-                emit(g_down.at[layer, rows, columns(i)])
-
-    def vector_step(layer, step):
-        mine = g_vec.at[layer]
-
-        def arrive(at):
-            pltpu.make_async_copy(mine, mine, gv_recv.at[layer, at]).wait()
-
-        def leave(at):
-            pltpu.make_async_copy(mine, mine, gv_send.at[layer, at]).wait()
-
-        def go(at, target, landed, who):
-            send(mine, target, gv_send.at[layer, at], gv_recv.at[layer, landed], who)
-
-        def add(at):
-            g_vec[layer] = g_vec[layer] + vr[layer, at]
-
-        for at, who in enumerate((fc, fx, fy)):
-
-            @pl.when(step == at)
-            def _(at=at, who=who):
-                if at:
-                    leave(at - 1)
-                    arrive(at - 1)
-                    add(at - 1)
-                go(at, vr.at[layer, at], at, in_plane(who))
-
-        @pl.when(step == 3)
-        def _():
-            leave(2)
-            arrive(2)
-            add(2)
-
-            @pl.when(outer)
-            def _():
-                go(3, vr.at[layer, 3], 3, along(z_in))
-
-        @pl.when(both(inner, step == 4))
-        def _():
-            arrive(3)
-            add(3)
-            go(4, vr.at[layer, 4], 4, along(z_pair))
-
-        @pl.when(both(inner, step == 5))
-        def _():
-            leave(4)
-            arrive(4)
-            add(4)
-            go(3, vr.at[layer, 3], 3, along(z_out))
-
-        @pl.when(step == 6)
-        def _():
-            leave(3)
-
-            @pl.when(outer)
-            def _():
-                arrive(3)
-                g_vec[layer] = vr[layer, 3]
+
+        @pl.when(step == 2)
+        def _():
+            wait_vec(2, 3)
+            wait_vec(3, 3)
+            g_vec[layer] = (vz[layer, 0] + vz[layer, 1]) + (vz[layer, 2] + vz[layer, 3])
 
     up = xs.at[layers]
     up[PAD - 8 :, :] = jnp.zeros((8, D), F32)
-    up[0:ROWS, :] = cotangent[...].astype(F32)
+    up[0:ROWS, :] = held_cot[...].astype(F32)
     none = jnp.zeros((8, D), F32)
 
     def put_vector(layer, which, value):
-        g_vec[layer, pl.ds(which, 1), :] = total(value)
-
-    def weight_grad(rows_at, left, right):
-        @pl.loop(0, 3)
-        def _(third):
-            lanes = pl.ds(aligned(third * KEYS, 128), KEYS)
-            target = pl.ds(aligned(rows_at + third * KEYS, 16), KEYS)
-            wb[target, :] = tn(left[:, lanes], right[...]).astype(BF16)
+        gv[layer, pl.ds(which, 1), :] = total(value)
+
+    def weight_grad(unit, left, right):
+        grad = tn(left[...], right[...]).astype(BF16)
+        wb[unit] = grad.reshape(2, 2, 2, SHARD, D)
 
     @pl.loop(0, layers)
     def _(turn):
         layer = layers - 1 - turn
-        base = turn * UNITS * PARTS
-        for row in range(12, 16):
-            g_vec[layer, row : row + 1, :] = jnp.zeros((1, D), F32)
+        base = 4 + turn * (UNITS * PARTS - 4)
 
         def branch_two(step, carry):
             rows = step_rows(step)
@@ -1151,11 +1160,11 @@
 
         @pl.loop(0, 4)
         def _(part):
-            @pl.when(turn > 0)
+            @pl.when(both(part < 3, 2 * turn + part >= 2))
             def _():
-                reduce_tick(base - HELD + part)
-
-            acc[...] = nt(br[...], wb[weight(layer, 8 + part), :])
+                reduce_tick(base - 3 + part)
+
+            acc[...] = nt(br[...], down_weight(layer, part))
 
             def through_gelu(step, carry):
                 rows = step_rows(step)
@@ -1164,18 +1173,19 @@
                 return carry + fold(value.astype(F32))
 
             put_vector(layer, V_UB + part, lax.fori_loop(0, PAD // STEP, through_gelu, none, unroll=UNROLL))
-            weight_grad(layer * LAYER_ROWS + DOWN_AT + part * D, hd.at[layer, part], br)
+            grad = tn(hd[layer, part], br[...]).astype(BF16)
+            put_down(layer * UNITS + 8, 4, part, grad)
 
         acc[...] = jnp.zeros((PAD, D), F32)
 
         @pl.loop(0, 4)
         def _(part):
-            @pl.when(turn > 0)
+            @pl.when(both(turn > 0, part == 0))
             def _():
-                vector_step(layer + 1, part)
-
-            acc[...] += nt(gb[part], wb[weight(layer, 4 + part), :])
-            weight_grad(layer * LAYER_ROWS + (4 + part) * D, n2.at[layer], gb.at[part])
+                vector_step(layer + 1, 0)
+
+            acc[...] += nt(gb[part], weight(layer, 4 + part))
+            weight_grad(layer * UNITS + 4 + part, n2.at[layer], gb.at[part])
 
             @pl.loop(0, 2)
             def _(again):
@@ -1200,8 +1210,8 @@
         norm_back(x1, V_G2, V_B2)
 
         put_vector(layer, V_OB, lax.fori_loop(0, PAD // STEP, branch_two, none, unroll=UNROLL))
-        gm[...] = nt(br[...], wb[weight(layer, 3), :]).astype(BF16)
-        weight_grad(layer * LAYER_ROWS + 3 * D, mx.at[layer], br)
+        gm[...] = nt(br[...], weight(layer, 3)).astype(BF16)
+        weight_grad(layer * UNITS + 3, mx.at[layer], br)
 
         @pl.loop(0, 2)
         def _(again):
@@ -1209,11 +1219,13 @@
 
         @pl.loop(0, HEADS // 2)
         def _(pair):
-            reduce_tick(base + 10 + pair)
-
-            @pl.when(both(turn > 0, pair < 3))
+            @pl.when(lax.rem(pair, 3) < 2)
             def _():
-                vector_step(layer + 1, pair + 4)
+                reduce_tick(base + 10 + pair - lax.div(pair, 3))
+
+            @pl.when(both(turn > 0, lax.rem(pair, 5) == 0))
+            def _():
+                vector_step(layer + 1, 1 + lax.div(pair, 5))
 
             lanes = pl.ds(aligned(pair * 128, 128), 128)
             kacc[...] = jnp.zeros((PAD, 128), F32)
@@ -1258,40 +1270,31 @@
 
         @pl.loop(0, 3)
         def _(part):
-            acc[...] += nt(gb[part], wb[weight(layer, part), :])
-            weight_grad(layer * LAYER_ROWS + part * D, nr.at[layer], gb.at[part])
-
-            @pl.when(part == 0)
-            def _():
-                reduce_tick(base + 16)
-
-            reduce_tick(base + 17 + part)
+            acc[...] += nt(gb[part], weight(layer, part))
+            weight_grad(layer * UNITS + part, nr.at[layer], gb.at[part])
+
+            reduce_tick(base + 14 + part)
 
         norm_back(xs, V_G1, V_B1)
 
-    tokens_grad[...] = up[0:ROWS, :]
-
-    @pl.loop(pieces - HELD, pieces + LAG_OUT)
+    held_grad[...] = up[0:ROWS, :]
+    tokens_out.start()
+    encoded_out.wait()
+
+    @pl.loop(pieces - 7, pieces + LAG_OUT)
     def _(t):
-        step = t - (pieces - HELD)
-
-        @pl.when(both(lax.rem(step, 2) == 0, step < 14))
-        def _():
-            vector_step(0, lax.div(step, 2))
+        step = t - (pieces - 7)
+
+        @pl.when(both(lax.rem(step, VEC_EVERY) == 0, step < 3 * VEC_EVERY))
+        def _():
+            vector_step(0, lax.div(step, VEC_EVERY))
 
         reduce_tick(t)
 
-    @pl.loop(0, pieces)
-    def _(i):
-        wait_piece(out_sem.at[i], SHARD)
-
-        @pl.when(outer)
-        def _():
-            wait_piece(rs_send.at[i], 4 * SHARD)
-
-        @pl.when(inner)
-        def _():
-            wait_piece(rs_send.at[i], 5 * SHARD)
+    for at in range(RING):
+        wait_piece(out_sem.at[at], 1)
+
+    tokens_out.wait()
 
 
 def closing_kernel(layers, *refs):
@@ -1304,7 +1307,6 @@
     narrow = refs[23:27]
     wide = refs[27:31]
     held_encoded, held_tokens, few_sem, in_sem, out_sem = refs[31:]
-    f = lax.axis_index("fsdp")
     copies = [
         pltpu.make_async_copy(vec_in, vec, few_sem.at[0]),
         pltpu.make_async_copy(encoded_in, held_encoded, few_sem.at[1]),
@@ -1338,16 +1340,9 @@
     writes[-1].start()
     for layer in range(layers):
         mine = vec[layer]
-        shard = jnp.zeros((8, SHARD), F32)
-        ups = jnp.zeros((1, 4 * SHARD), F32)
-        for owner in range(8):
-            here = f == owner
-            shard = jnp.where(here, mine[0:8, owner * SHARD : (owner + 1) * SHARD], shard)
-            row, lane = 8 + owner // 2, (owner % 2) * 4 * SHARD
-            ups = jnp.where(here, mine[row : row + 1, lane : lane + 4 * SHARD], ups)
         for which in range(8):
-            small_out[which][layer : layer + 1, :] = shard[which : which + 1]
-        small_out[8][layer : layer + 1, :] = ups
+            small_out[which][layer : layer + 1, :] = mine[which : which + 1, 0:SHARD]
+        small_out[8][layer : layer + 1, :] = mine[0:1, 128:512]
     for copy in writes:
         copy.wait()
 
@@ -1372,7 +1367,6 @@
     layers = qkv_weight.shape[0]
     count = layers * UNITS
     pieces = count * PARTS
-    vmem = pl.BlockSpec(memory_space=pltpu.VMEM)
     hbm = pl.BlockSpec(memory_space=pltpu.MemorySpace.HBM)
     plain = pl.BlockSpec()
     dma = pltpu.SemaphoreType.DMA
@@ -1381,16 +1375,16 @@
         out_shape=(
             jax.ShapeDtypeStruct((ROWS, D), BF16),
             jax.ShapeDtypeStruct((ROWS, D), F32),
-            jax.ShapeDtypeStruct((layers, 16, D), F32),
+            jax.ShapeDtypeStruct((layers, 8, 512), F32),
             jax.ShapeDtypeStruct((layers, SHARD, 3 * D), BF16),
             jax.ShapeDtypeStruct((layers, SHARD, D), BF16),
             jax.ShapeDtypeStruct((layers, SHARD, FF), BF16),
             jax.ShapeDtypeStruct((layers, 4 * SHARD, D), BF16),
         ),
-        in_specs=[vmem] * 2 + [plain] * 9 + [hbm] * 4,
-        out_specs=(vmem, vmem, vmem, hbm, hbm, hbm, hbm),
+        in_specs=[hbm] * 2 + [plain] * 9 + [hbm] * 4,
+        out_specs=(hbm, hbm, plain, hbm, hbm, hbm, hbm),
         scratch_shapes=[
-            pltpu.VMEM((layers * LAYER_ROWS, D), BF16),
+            pltpu.VMEM((count + EARLY_UNITS, 2, 2, 2, SHARD, D), BF16),
             pltpu.VMEM((layers + 1, PAD, D), F32),
             pltpu.VMEM((layers, PAD, D), F32),
             pltpu.VMEM((layers, PAD, D), BF16),
@@ -1410,26 +1404,30 @@
             pltpu.VMEM((LOW_ROWS, KEYS), F32),
             pltpu.VMEM((8, 8 * layers, 512), BF16),
             pltpu.VMEM((8 * layers, D), F32),
-            pltpu.VMEM((8 * layers, FF), F32),
-            pltpu.VMEM((layers, 5, 16, D), F32),
-            pltpu.VMEM((SLOTS, 4 * SHARD, WIDE), BF16),
-            pltpu.VMEM((SLOTS, 4 * HALF, WIDE), BF16),
+            pltpu.VMEM((layers, FF), F32),
+            pltpu.VMEM((layers, 16, D), F32),
+            pltpu.VMEM((8, 8, 512), F32),
+            pltpu.VMEM((layers, 8, 8, 512), F32),
+            pltpu.VMEM((layers, 4, 8, 512), F32),
+            pltpu.VMEM((ROWS, D), BF16),
+            pltpu.VMEM((ROWS, D), BF16),
+            pltpu.VMEM((ROWS, D), F32),
+            pltpu.VMEM((CORE_SLOTS, 2, 2, SHARD, WIDE), BF16),
+            pltpu.VMEM((SLOTS, 2, 2, HALF, WIDE), BF16),
             pltpu.VMEM((SLOTS, 2, SHARD, WIDE), BF16),
             dma((count, 4)),
             dma((count,)),
             dma((count,)),
-            dma((pieces,)),
-            dma((pieces,)),
-            dma((pieces,)),
-            dma((pieces, 3)),
-            dma((pieces,)),
-            dma((pieces,)),
-            dma((pieces,)),
-            dma((7,)),
-            dma((7,)),
-            dma((layers, 5)),
-            dma((layers, 5)),
-            pltpu.SemaphoreType.REGULAR((5,)),
+            dma((RING,)),
+            dma((RING,)),
+            dma((RING,)),
+            dma((RING, 3)),
+            dma((RING,)),
+            dma((2 * RING,)),
+            dma((RING,)),
+            dma((2,)),
+            dma((layers, 4)),
+            dma((4,)),
         ],
         compiler_params=pltpu.CompilerParams(
             collective_id=0, has_side_effects=True, vmem_limit_bytes=VMEM_BYTES
@@ -1460,7 +1458,7 @@
         + [jax.ShapeDtypeStruct(shape, F32) for shape in shapes],
         in_specs=[hbm] * 7,
         out_specs=[hbm] * 2 + [plain] * 9 + [hbm] * 4,
-        scratch_shapes=[pltpu.VMEM((layers, 16, D), F32)]
+        scratch_shapes=[pltpu.VMEM((layers, 8, 512), F32)]
         + [pltpu.VMEM(shape, BF16) for shape in shapes[9:]]
         + [pltpu.VMEM(shape, F32) for shape in shapes[9:]]
         + [pltpu.VMEM((ROWS, D), BF16), pltpu.VMEM((ROWS, D), F32)]

time: 267 us -> 253 us (0.948)
  Pallas kernels: 266 us -> 252 us
    pallas_call x1, Pallas kernels: 261 us -> 246 us  [kernel_local(): pl.pallas_call(functools.partial(encoder_kernel, layers), out_shape=(jax....]
where the time goes in v4:
time: 253 us; the launch traced here: 252 us
  Pallas kernels  252 us (100%)
    pallas_call x1, Pallas kernels, kernel_local(): pl.pallas_call(functools.partial(encoder_kernel, layers), out_shape=(jax....  246 us
    pallas_call x1, Pallas kernels, kernel_local(): pl.pallas_call(functools.partial(closing_kernel, layers), out_shape=[jax....  5.71 us

profile of v4, /device:TPU:0, one launch (start us, length us, event | category | flops | bytes accessed | tf_op | source)
XLA Modules:
  0.0 252.3 jit_solution(646329493732724545)
XLA Ops:
  0.7 245.8 %shard_map.262 = (bf16[345,768]{1,0:T(8,128)(2,1)}, f32[345,768]{1,0:T(8,128)}, f32[2,8,512]{2,1,0:T(8,128)}, bf16[2,96,2304]{2,1,0:T(8,128)(2,1)}, bf16[2,96,76...) custom-call(bf16[345,768]{1,0:T(8,128)(2,1)} %tokens.1, bf16[345,768]{1,0:T(8,128)(2,1)} %cotangent.1, ...), custom_call_target="tpu_custom_call" | custom-call | tf_op jit(solution)/shard_map/pallas_call | solution.py:1373
  246.5 5.7 %shard_map.263 = (bf16[345,768]{1,0:T(8,128)(2,1)}, f32[345,768]{1,0:T(8,128)}, f32[2,96]{1,0:T(2,128)}, f32[2,96]{1,0:T(2,128)}, f32[2,96]{1,0:T(2,128)}, /*ind...) custom-call(bf16[345,768]{1,0:T(8,128)(2,1)} %get-tuple-element.37.r, ...), custom_call_target="tpu_custom_call" | custom-call | tf_op jit(solution)/shard_map/pallas_call | solution.py:1455

commit v5 on v4

--- a/solution.py
+++ b/solution.py
@@ -659,22 +659,26 @@
                 wb.at[layer * UNITS + unit, y, x, c],
                 own_sem.at[layer * UNITS + unit],
             ).start()
-    vec[...] = jnp.zeros((8 * layers, D), F32)
+    small = acc.at[0 : 16 * layers, 0:128]
+    small[...] = jnp.zeros((16 * layers, 128), F32)
     for at, source in enumerate((n_g1, n_b1, n_qb, n_vb, n_ob, n_g2, n_b2, n_db)):
         shard = source[...].astype(F32)
         for layer in range(layers):
-            vec[8 * layer + at : 8 * layer + at + 1, 0:SHARD] = shard[layer : layer + 1]
+            row = 8 * layer + at
+            acc[row : row + 1, 0:SHARD] = shard[layer : layer + 1]
     shard = n_ub[...].astype(F32)
     for layer in range(layers):
-        vec[8 * layer : 8 * layer + 1, 128:512] = shard[layer : layer + 1]
-    vsg[f] = vec[:, 0:512].astype(BF16)
+        for third in range(3):
+            row = 8 * layers + 3 * layer + third
+            acc[row : row + 1, 0:128] = shard[layer : layer + 1, third * 128 : third * 128 + 128]
+    vsg[f] = small[...].astype(BF16)
     tokens_in = pltpu.make_async_copy(tokens, held, io_sem.at[0])
     cotangent_in = pltpu.make_async_copy(cotangent, held_cot, io_sem.at[1])
     encoded_out = pltpu.make_async_copy(held, encoded, io_sem.at[2])
     tokens_out = pltpu.make_async_copy(held_grad, tokens_grad, io_sem.at[3])
     tokens_in.start()
     cotangent_in.start()
-    gvs[...] = jnp.zeros((8, 8, 512), F32)
+    gvs[...] = jnp.zeros((8, 16, 128), F32)
     pl.semaphore_wait(barrier, 10)
 
     def role(i):
@@ -765,11 +769,12 @@
         at_row = lax.broadcasted_iota(jnp.int32, (128, D), 0)
         at_col = lax.broadcasted_iota(jnp.int32, (128, D), 1)
         hit = jnp.logical_and(at_col == at_row + owner * SHARD, at_row < SHARD)
-        spread = spread + nn(vsg[owner, :, 0:128], jnp.where(hit, 1.0, 0.0).astype(BF16))
-        wide = vsg[owner, :, 128:512].astype(F32)
+        spread = spread + nn(vsg[owner, 0 : 8 * layers, :], jnp.where(hit, 1.0, 0.0).astype(BF16))
+        wide = vsg[owner, 8 * layers :, :].astype(F32)
         for layer in range(layers):
-            row, lane = 8 * layer, owner * 4 * SHARD
-            ubs[layer : layer + 1, lane : lane + 4 * SHARD] = wide[row : row + 1]
+            for third in range(3):
+                row, lane = 3 * layer + third, owner * 4 * SHARD + third * 128
+                ubs[layer : layer + 1, lane : lane + 128] = wide[row : row + 1]
     vec[...] = spread
 
     @pl.loop(EARLY, LAG_WHOLE)
@@ -1024,6 +1029,13 @@
             normed, _unused = stats(now)
             n2[layer, rows, :] = (normed * vector(layer, V_G2) + vector(layer, V_B2)).astype(BF16)
 
+        @pl.when(layer == layers - 1)
+        def _():
+            acc[PAD - 8 :, :] = jnp.zeros((8, D), F32)
+            cotangent_in.wait()
+            acc[0:ROWS, :] = held_cot[...].astype(F32)
+            br[...] = acc[...].astype(BF16)
+
         @pl.loop(0, 4)
         def _(part):
             gather_tick(base + 4 + part)
@@ -1039,15 +1051,8 @@
                 hd[layer, part, rows, :] = (pre * cdf).astype(BF16)
                 gp[layer, part, rows, :] = (cdf + pre * bell).astype(BF16)
 
-        @pl.when(layer == layers - 1)
-        def _():
-            acc[PAD - 8 :, :] = jnp.zeros((8, D), F32)
-            cotangent_in.wait()
-            acc[0:ROWS, :] = held_cot[...].astype(F32)
-            br[...] = acc[...].astype(BF16)
-
-            @pl.loop(0, 4)
-            def _(part):
+            @pl.when(layer == layers - 1)
+            def _():
                 grad = tn(hd[layer, part], br[...]).astype(BF16)
                 put_down(layers * UNITS, EARLY_UNITS, part, grad)
 
@@ -1097,9 +1102,12 @@
         @pl.when(step == 0)
         def _():
             for owner in range(8):
-                gvs[owner, :, 0:SHARD] = gv[layer, 0:8, owner * SHARD : (owner + 1) * SHARD]
-                row, lane = 8 + owner // 2, (owner % 2) * 4 * SHARD
-                gvs[owner, 0:1, 128:512] = gv[layer, row : row + 1, lane : lane + 4 * SHARD]
+                gvs[owner, 0:8, 0:SHARD] = gv[layer, 0:8, owner * SHARD : (owner + 1) * SHARD]
+                row = 8 + owner // 2
+                for third in range(3):
+                    lane = (owner % 2) * 4 * SHARD + third * 128
+                    wide = gv[layer, row : row + 1, lane : lane + 128]
+                    gvs[owner, 8 + third : 9 + third, :] = wide
             vr[layer, f] = gvs[f]
             for peer in peers:
                 send(
@@ -1160,9 +1168,9 @@
 
         @pl.loop(0, 4)
         def _(part):
-            @pl.when(both(part < 3, 2 * turn + part >= 2))
+            @pl.when(4 * turn + part >= 3)
             def _():
-                reduce_tick(base - 3 + part)
+                reduce_tick(base - 4 + part)
 
             acc[...] = nt(br[...], down_weight(layer, part))
 
@@ -1186,10 +1194,7 @@
 
             acc[...] += nt(gb[part], weight(layer, 4 + part))
             weight_grad(layer * UNITS + 4 + part, n2.at[layer], gb.at[part])
-
-            @pl.loop(0, 2)
-            def _(again):
-                reduce_tick(base + 2 * part + again)
+            reduce_tick(base + part)
 
         def norm_back(source, gain_at, shift_at):
             def body(step, carry):
@@ -1215,13 +1220,11 @@
 
         @pl.loop(0, 2)
         def _(again):
-            reduce_tick(base + 8 + again)
+            reduce_tick(base + 4 + again)
 
         @pl.loop(0, HEADS // 2)
         def _(pair):
-            @pl.when(lax.rem(pair, 3) < 2)
-            def _():
-                reduce_tick(base + 10 + pair - lax.div(pair, 3))
+            reduce_tick(base + 6 + pair)
 
             @pl.when(both(turn > 0, lax.rem(pair, 5) == 0))
             def _():
@@ -1273,17 +1276,18 @@
             acc[...] += nt(gb[part], weight(layer, part))
             weight_grad(layer * UNITS + part, nr.at[layer], gb.at[part])
 
-            reduce_tick(base + 14 + part)
+            reduce_tick(base + 12 + part)
 
         norm_back(xs, V_G1, V_B1)
+        reduce_tick(base + 15)
 
     held_grad[...] = up[0:ROWS, :]
     tokens_out.start()
     encoded_out.wait()
 
-    @pl.loop(pieces - 7, pieces + LAG_OUT)
+    @pl.loop(pieces - 8, pieces + LAG_OUT)
     def _(t):
-        step = t - (pieces - 7)
+        step = t - (pieces - 8)
 
         @pl.when(both(lax.rem(step, VEC_EVERY) == 0, step < 3 * VEC_EVERY))
         def _():
@@ -1342,7 +1346,9 @@
         mine = vec[layer]
         for which in range(8):
             small_out[which][layer : layer + 1, :] = mine[which : which + 1, 0:SHARD]
-        small_out[8][layer : layer + 1, :] = mine[0:1, 128:512]
+        for third in range(3):
+            lanes = slice(third * 128, third * 128 + 128)
+            small_out[8][layer : layer + 1, lanes] = mine[8 + third : 9 + third]
     for copy in writes:
         copy.wait()
 
@@ -1375,7 +1381,7 @@
         out_shape=(
             jax.ShapeDtypeStruct((ROWS, D), BF16),
             jax.ShapeDtypeStruct((ROWS, D), F32),
-            jax.ShapeDtypeStruct((layers, 8, 512), F32),
+            jax.ShapeDtypeStruct((layers, 16, 128), F32),
             jax.ShapeDtypeStruct((layers, SHARD, 3 * D), BF16),
             jax.ShapeDtypeStruct((layers, SHARD, D), BF16),
             jax.ShapeDtypeStruct((layers, SHARD, FF), BF16),
@@ -1402,13 +1408,13 @@
             pltpu.VMEM((PAD, 128), F32),
             pltpu.VMEM((TOP_ROWS, KEYS), F32),
             pltpu.VMEM((LOW_ROWS, KEYS), F32),
-            pltpu.VMEM((8, 8 * layers, 512), BF16),
+            pltpu.VMEM((8, 16 * layers, 128), BF16),
             pltpu.VMEM((8 * layers, D), F32),
             pltpu.VMEM((layers, FF), F32),
             pltpu.VMEM((layers, 16, D), F32),
-            pltpu.VMEM((8, 8, 512), F32),
-            pltpu.VMEM((layers, 8, 8, 512), F32),
-            pltpu.VMEM((layers, 4, 8, 512), F32),
+            pltpu.VMEM((8, 16, 128), F32),
+            pltpu.VMEM((layers, 8, 16, 128), F32),
+            pltpu.VMEM((layers, 4, 16, 128), F32),
             pltpu.VMEM((ROWS, D), BF16),
             pltpu.VMEM((ROWS, D), BF16),
             pltpu.VMEM((ROWS, D), F32),
@@ -1458,7 +1464,7 @@
         + [jax.ShapeDtypeStruct(shape, F32) for shape in shapes],
         in_specs=[hbm] * 7,
         out_specs=[hbm] * 2 + [plain] * 9 + [hbm] * 4,
-        scratch_shapes=[pltpu.VMEM((layers, 8, 512), F32)]
+        scratch_shapes=[pltpu.VMEM((layers, 16, 128), F32)]
         + [pltpu.VMEM(shape, BF16) for shape in shapes[9:]]
         + [pltpu.VMEM(shape, F32) for shape in shapes[9:]]
         + [pltpu.VMEM((ROWS, D), BF16), pltpu.VMEM((ROWS, D), F32)]

time: 253 us -> 243 us (0.960)
  Pallas kernels: 252 us -> 242 us
    pallas_call x1, Pallas kernels: 246 us -> 236 us  [kernel_local(): pl.pallas_call(functools.partial(encoder_kernel, layers), out_shape=(jax....]
where the time goes in v5:
time: 243 us
  Pallas kernels  242 us (100%)
    pallas_call x1, Pallas kernels, kernel_local(): pl.pallas_call(functools.partial(encoder_kernel, layers), out_shape=(jax....  236 us
    pallas_call x1, Pallas kernels, kernel_local(): pl.pallas_call(functools.partial(closing_kernel, layers), out_shape=[jax....  5.71 us

profile of v5, /device:TPU:0, one launch (start us, length us, event | category | flops | bytes accessed | tf_op | source)
XLA Modules:
  0.0 242.9 jit_solution(15005801912788750867)
XLA Ops:
  0.7 236.4 %shard_map.262 = (bf16[345,768]{1,0:T(8,128)(2,1)}, f32[345,768]{1,0:T(8,128)}, f32[2,16,128]{2,1,0:T(8,128)}, bf16[2,96,2304]{2,1,0:T(8,128)(2,1)}, bf16[2,96,7...) custom-call(bf16[345,768]{1,0:T(8,128)(2,1)} %tokens.1, bf16[345,768]{1,0:T(8,128)(2,1)} %cotangent.1, ...), custom_call_target="tpu_custom_call" | custom-call | tf_op jit(solution)/shard_map/pallas_call | solution.py:1379
  237.0 5.7 %shard_map.263 = (bf16[345,768]{1,0:T(8,128)(2,1)}, f32[345,768]{1,0:T(8,128)}, f32[2,96]{1,0:T(2,128)}, f32[2,96]{1,0:T(2,128)}, f32[2,96]{1,0:T(2,128)}, /*ind...) custom-call(bf16[345,768]{1,0:T(8,128)(2,1)} %get-tuple-element.37.r, ...), custom_call_target="tpu_custom_call" | custom-call | tf_op jit(solution)/shard_map/pallas_call | solution.py:1461

commit v6 on v5

--- a/solution.py
+++ b/solution.py
@@ -458,10 +458,12 @@
 PARTS = 2
 WIDE = D // PARTS
 LAG_XY, LAG_LAST, LAG_Z1, LAG_Z2, LAG_OUT = 4, 6, 8, 10, 12
-LAG_PASS, LAG_WHOLE = 8, 9
+LAG_NEXT, LAG_PLANE, LAG_PASS, LAG_WHOLE = 2, 4, 8, 9
 EARLY_UNITS = 2
+EARLY_PIECES = EARLY_UNITS * PARTS
+GAP = 3
 EARLY = 3
-VEC_EVERY = 5
+VEC_EVERY = 4
 TOP_ROWS = 208
 KEYS = 256
 LOW_KEY = PAD - KEYS
@@ -640,9 +642,15 @@
     peers = [lax.rem(f + hop, 8) for hop in range(1, 8)]
     for peer in peers:
         pl.semaphore_signal(barrier, inc=1, device_id=in_plane(peer), device_id_type=MESH)
-    for hop in range(1, 4):
-        beside = lax.rem(d + hop, 4)
-        pl.semaphore_signal(barrier, inc=1, device_id=along(beside), device_id_type=MESH)
+
+    @pl.when(outer)
+    def _():
+        pl.semaphore_signal(barrier, inc=1, device_id=along(z_in), device_id_type=MESH)
+
+    @pl.when(inner)
+    def _():
+        pl.semaphore_signal(barrier, inc=1, device_id=along(z_out), device_id_type=MESH)
+        pl.semaphore_signal(barrier, inc=1, device_id=along(z_pair), device_id_type=MESH)
 
     for layer in range(layers):
         for unit in range(UNITS):
@@ -657,7 +665,7 @@
             pltpu.make_async_copy(
                 source,
                 wb.at[layer * UNITS + unit, y, x, c],
-                own_sem.at[layer * UNITS + unit],
+                own_sem.at[layer],
             ).start()
     small = acc.at[0 : 16 * layers, 0:128]
     small[...] = jnp.zeros((16 * layers, 128), F32)
@@ -679,7 +687,7 @@
     tokens_in.start()
     cotangent_in.start()
     gvs[...] = jnp.zeros((8, 16, 128), F32)
-    pl.semaphore_wait(barrier, 10)
+    pl.semaphore_wait(barrier, 8 + lax.div(d * (3 - d), 2))
 
     def role(i):
         return lax.rem(i, 3) * lax.div(2 * count - 3 - i, count)
@@ -691,47 +699,50 @@
         @pl.when(t < count)
         def _():
             own = wb.at[t, y, x, c]
-            wait_blocks(own_sem.at[t], 1)
+
+            @pl.when(lax.rem(t, UNITS) == 0)
+            def _():
+                wait_blocks(own_sem.at[lax.div(t, UNITS)], UNITS)
 
             @pl.when(collects(t))
             def _():
                 first = wb.at[t, y, x, c, first_rows]
                 second = wb.at[t, y, x, c, second_rows]
-                send(first, first, ag_send.at[t], ag_sem.at[t, 0], in_plane(fy))
-                send(second, second, ag_send.at[t], ag_sem.at[t, 1], in_plane(fx))
-                send(first, first, ag_send.at[t], ag_sem.at[t, 2], in_plane(fx))
-                send(second, second, ag_send.at[t], ag_sem.at[t, 2], in_plane(fy))
-
-            send(own, own, ag_send.at[t], ag_sem.at[t, 3], in_plane(fc))
-
-        @pl.when(both(both(t >= 2, t < count + 2), collects(t - 2)))
-        def _():
-            i = t - 2
+                send(first, first, ag_send.at[0], ag_sem.at[t, 0], in_plane(fy))
+                send(second, second, ag_send.at[0], ag_sem.at[t, 1], in_plane(fx))
+                send(first, first, ag_send.at[0], ag_sem.at[t, 2], in_plane(fx))
+                send(second, second, ag_send.at[0], ag_sem.at[t, 2], in_plane(fy))
+
+            send(own, own, ag_send.at[0], ag_sem.at[t, 3], in_plane(fc))
+
+        @pl.when(both(both(t >= LAG_NEXT, t < count + LAG_NEXT), collects(t - LAG_NEXT)))
+        def _():
+            i = t - LAG_NEXT
             wait_half(ag_sem.at[i, 0])
             wait_half(ag_sem.at[i, 1])
             first = wb.at[i, 1 - y, x, c, first_rows]
             second = wb.at[i, y, 1 - x, c, second_rows]
-            send(first, first, ag_send.at[i], ag_sem.at[i, 2], in_plane(fx))
-            send(second, second, ag_send.at[i], ag_sem.at[i, 2], in_plane(fy))
-
-        @pl.when(both(both(t >= 4, t < count + 4), collects(t - 4)))
-        def _():
-            i = t - 4
+            send(first, first, ag_send.at[0], ag_sem.at[i, 2], in_plane(fx))
+            send(second, second, ag_send.at[0], ag_sem.at[i, 2], in_plane(fy))
+
+        @pl.when(both(both(t >= LAG_PLANE, t < count + LAG_PLANE), collects(t - LAG_PLANE)))
+        def _():
+            i = t - LAG_PLANE
             wait_blocks(ag_sem.at[i, 2], 2)
             for piece in (wb.at[i, 1 - y, :, c], wb.at[i, y, 1 - x, c]):
 
                 @pl.when(role(i) > 0)
                 def _(piece=piece):
-                    send(piece, piece, ag_send.at[i], ag_sem.at[i, 0], along(z_near))
-
-                send(piece, piece, ag_send.at[i], ag_sem.at[i, 3], in_plane(fc))
+                    send(piece, piece, ag_send.at[0], ag_sem.at[i, 0], along(z_near))
+
+                send(piece, piece, ag_send.at[0], ag_sem.at[i, 3], in_plane(fc))
 
         @pl.when(both(both(t >= LAG_PASS, t < count + LAG_PASS), role(t - LAG_PASS) == 2 - parity))
         def _():
             i = t - LAG_PASS
             wait_blocks(ag_sem.at[i, 0], 3)
             for piece in (wb.at[i, 1 - y, :, c], wb.at[i, y, 1 - x, c]):
-                send(piece, piece, ag_send.at[i], ag_sem.at[i, 3], in_plane(fc))
+                send(piece, piece, ag_send.at[0], ag_sem.at[i, 3], in_plane(fc))
 
         @pl.when(both(t >= LAG_WHOLE, t < count + LAG_WHOLE))
         def _():
@@ -823,7 +834,14 @@
         return at, pl.ds(aligned(half * WIDE, 128), WIDE)
 
     def during(t, lag):
-        return both(t >= lag, t < pieces + lag)
+        at = t - lag
+        begun = jnp.logical_or(at < EARLY_PIECES, at >= EARLY_PIECES + GAP)
+        return both(begun, both(at >= 0, at < pieces + GAP))
+
+    def piece_of(t, lag):
+        at = t - lag
+        span = 4 * pieces
+        return at - GAP * lax.div(at + span - (EARLY_PIECES + GAP), span)
 
     def ring(i):
         return lax.rem(i, RING)
@@ -832,20 +850,21 @@
         return lax.rem(i, 2 * RING)
 
     def reduce_tick(t):
-        @pl.when(t < pieces)
-        def _():
-            n, cols = piece_at(t)
+        @pl.when(during(t, 0))
+        def _():
+            i = piece_of(t, 0)
+            n, cols = piece_at(i)
             send(
                 wb.at[n, :, :, 1 - c, :, cols],
-                rc.at[lax.rem(t, CORE_SLOTS)],
-                s0_send.at[ring(t)],
-                core_sem.at[ring(t)],
+                rc.at[lax.rem(i, CORE_SLOTS)],
+                s0_send.at[ring(i)],
+                core_sem.at[ring(i)],
                 in_plane(fc),
             )
 
         @pl.when(during(t, LAG_XY))
         def _():
-            i = t - LAG_XY
+            i = piece_of(t, LAG_XY)
             n, cols = piece_at(i)
             slot = lax.rem(i, SLOTS)
             wait_piece(xy_sem.at[ring(i)], 2)
@@ -870,7 +889,7 @@
 
         @pl.when(during(t, 1))
         def _():
-            i = t - 1
+            i = piece_of(t, 1)
             n, cols = piece_at(i)
             slot = lax.rem(i, SLOTS)
             wait_piece(core_sem.at[ring(i)], 4)
@@ -894,7 +913,7 @@
 
         @pl.when(during(t, LAG_OUT))
         def _():
-            i = t - LAG_OUT
+            i = piece_of(t, LAG_OUT)
             n, cols = piece_at(i)
             layer, unit, half = backward_unit(layers, i)
 
@@ -941,7 +960,7 @@
 
         @pl.when(during(t, LAG_LAST))
         def _():
-            i = t - LAG_LAST
+            i = piece_of(t, LAG_LAST)
             n, cols = piece_at(i)
             wait_piece(last_sem.at[ring(i)], 1)
             own = wb.at[n, y, x, c, :, cols]
@@ -954,7 +973,7 @@
 
         @pl.when(both(inner, during(t, LAG_Z1)))
         def _():
-            i = t - LAG_Z1
+            i = piece_of(t, LAG_Z1)
             n, cols = piece_at(i)
             slot = lax.rem(i, SLOTS)
             wait_piece(z_sem.at[ring(i), 0], 1)
@@ -964,7 +983,7 @@
 
         @pl.when(both(inner, during(t, LAG_Z2)))
         def _():
-            i = t - LAG_Z2
+            i = piece_of(t, LAG_Z2)
             n, cols = piece_at(i)
             wait_piece(z_sem.at[ring(i), 1], 1)
             done = wb.at[n, y, x, 1 - c, :, cols]
@@ -1078,26 +1097,23 @@
     held[...] = xs[layers, 0:ROWS, :].astype(BF16)
     encoded_out.start()
 
-    @pl.loop(0, count)
-    def _(i):
-        @pl.when(role(i) == 0)
-        def _():
-            wait_blocks(ag_send.at[i], 7)
-
-        @pl.when(role(i) == 1 + parity)
-        def _():
-            wait_blocks(ag_send.at[i], 10)
-
-        @pl.when(role(i) == 2 - parity)
-        def _():
-            wait_blocks(ag_send.at[i], 4)
-
+    span = wb.at[pl.ds(0, 7 * count // 8)]
+    pltpu.make_async_copy(span, span, ag_send.at[0]).wait()
     pltpu.make_async_copy(seven, seven, vec_sem.at[0]).wait()
 
     def vector_step(layer, step):
         def wait_vec(at, copies):
             span = gvs.at[pl.ds(0, copies)]
             pltpu.make_async_copy(span, span, gv_sem.at[layer, at]).wait()
+
+        def z_go(source, target, at, who):
+            send(
+                vz.at[layer, source],
+                vz.at[layer, target],
+                gv_sem.at[layer, at],
+                gv_sem.at[layer, at + 1],
+                along(who),
+            )
 
         @pl.when(step == 0)
         def _():
@@ -1125,21 +1141,37 @@
             in_sum = vr[layer, 0]
             for source in range(1, 8):
                 in_sum = in_sum + vr[layer, source]
-            vz[layer, d] = in_sum
-            for hop in range(3):
-                send(
-                    vz.at[layer, d],
-                    vz.at[layer, d],
-                    gv_sem.at[layer, 2],
-                    gv_sem.at[layer, 3],
-                    along(lax.rem(d + 1 + hop, 4)),
-                )
-
-        @pl.when(step == 2)
-        def _():
-            wait_vec(2, 3)
-            wait_vec(3, 3)
-            g_vec[layer] = (vz[layer, 0] + vz[layer, 1]) + (vz[layer, 2] + vz[layer, 3])
+            vz[layer, 0] = in_sum
+
+            @pl.when(outer)
+            def _():
+                z_go(0, 1, 2, z_in)
+
+        @pl.when(both(inner, step == 2))
+        def _():
+            wait_vec(3, 1)
+            vz[layer, 0] = vz[layer, 0] + vz[layer, 1]
+            z_go(0, 2, 4, z_pair)
+
+        @pl.when(both(inner, step == 3))
+        def _():
+            wait_vec(4, 1)
+            wait_vec(5, 1)
+            vz[layer, 3] = vz[layer, 0] + vz[layer, 2]
+            z_go(3, 3, 6, z_out)
+
+        @pl.when(step == 4)
+        def _():
+            @pl.when(outer)
+            def _():
+                wait_vec(2, 1)
+                wait_vec(7, 1)
+
+            @pl.when(inner)
+            def _():
+                wait_vec(6, 1)
+
+            g_vec[layer] = vz[layer, 3]
 
     up = xs.at[layers]
     up[PAD - 8 :, :] = jnp.zeros((8, D), F32)
@@ -1156,7 +1188,7 @@
     @pl.loop(0, layers)
     def _(turn):
         layer = layers - 1 - turn
-        base = 4 + turn * (UNITS * PARTS - 4)
+        base = EARLY_PIECES + GAP + turn * (UNITS * PARTS - 4)
 
         def branch_two(step, carry):
             rows = step_rows(step)
@@ -1168,9 +1200,7 @@
 
         @pl.loop(0, 4)
         def _(part):
-            @pl.when(4 * turn + part >= 3)
-            def _():
-                reduce_tick(base - 4 + part)
+            reduce_tick(base - 4 + part)
 
             acc[...] = nt(br[...], down_weight(layer, part))
 
@@ -1226,9 +1256,9 @@
         def _(pair):
             reduce_tick(base + 6 + pair)
 
-            @pl.when(both(turn > 0, lax.rem(pair, 5) == 0))
-            def _():
-                vector_step(layer + 1, 1 + lax.div(pair, 5))
+            @pl.when(both(turn > 0, lax.rem(pair, 2) == 0))
+            def _():
+                vector_step(layer + 1, 1 + lax.div(pair, 2))
 
             lanes = pl.ds(aligned(pair * 128, 128), 128)
             kacc[...] = jnp.zeros((PAD, 128), F32)
@@ -1278,6 +1308,10 @@
 
             reduce_tick(base + 12 + part)
 
+            @pl.when(both(turn > 0, part == 1))
+            def _():
+                vector_step(layer + 1, 4)
+
         norm_back(xs, V_G1, V_B1)
         reduce_tick(base + 15)
 
@@ -1285,11 +1319,11 @@
     tokens_out.start()
     encoded_out.wait()
 
-    @pl.loop(pieces - 8, pieces + LAG_OUT)
+    @pl.loop(pieces + GAP - 8, pieces + GAP + LAG_OUT)
     def _(t):
-        step = t - (pieces - 8)
-
-        @pl.when(both(lax.rem(step, VEC_EVERY) == 0, step < 3 * VEC_EVERY))
+        step = t - (pieces + GAP - 8)
+
+        @pl.when(both(lax.rem(step, VEC_EVERY) == 0, step < 5 * VEC_EVERY))
         def _():
             vector_step(0, lax.div(step, VEC_EVERY))
 
@@ -1422,8 +1456,8 @@
             pltpu.VMEM((SLOTS, 2, 2, HALF, WIDE), BF16),
             pltpu.VMEM((SLOTS, 2, SHARD, WIDE), BF16),
             dma((count, 4)),
-            dma((count,)),
-            dma((count,)),
+            dma((1,)),
+            dma((layers,)),
             dma((RING,)),
             dma((RING,)),
             dma((RING,)),
@@ -1432,7 +1466,7 @@
             dma((2 * RING,)),
             dma((RING,)),
             dma((2,)),
-            dma((layers, 4)),
+            dma((layers, 8)),
             dma((4,)),
         ],
         compiler_params=pltpu.CompilerParams(

time: 243 us -> 240 us (0.988)
  Pallas kernels: 242 us -> 239 us
    pallas_call x1, Pallas kernels: 236 us -> 234 us  [kernel_local(): pl.pallas_call(functools.partial(encoder_kernel, layers), out_shape=(jax....]
where the time goes in v6:
time: 240 us
  Pallas kernels  239 us (100%)
    pallas_call x1, Pallas kernels, kernel_local(): pl.pallas_call(functools.partial(encoder_kernel, layers), out_shape=(jax....  234 us
    pallas_call x1, Pallas kernels, kernel_local(): pl.pallas_call(functools.partial(closing_kernel, layers), out_shape=[jax....  5.71 us

profile of v6, /device:TPU:0, one launch (start us, length us, event | category | flops | bytes accessed | tf_op | source)
XLA Modules:
  0.0 240.3 jit_solution(14394245146981736176)
XLA Ops:
  0.7 233.8 %shard_map.262 = (bf16[345,768]{1,0:T(8,128)(2,1)}, f32[345,768]{1,0:T(8,128)}, f32[2,16,128]{2,1,0:T(8,128)}, bf16[2,96,2304]{2,1,0:T(8,128)(2,1)}, bf16[2,96,7...) custom-call(bf16[345,768]{1,0:T(8,128)(2,1)} %tokens.1, bf16[345,768]{1,0:T(8,128)(2,1)} %cotangent.1, ...), custom_call_target="tpu_custom_call" | custom-call | tf_op jit(solution)/shard_map/pallas_call | solution.py:1413
  234.4 5.7 %shard_map.263 = (bf16[345,768]{1,0:T(8,128)(2,1)}, f32[345,768]{1,0:T(8,128)}, f32[2,96]{1,0:T(2,128)}, f32[2,96]{1,0:T(2,128)}, f32[2,96]{1,0:T(2,128)}, /*ind...) custom-call(bf16[345,768]{1,0:T(8,128)(2,1)} %get-tuple-element.37.r, ...), custom_call_target="tpu_custom_call" | custom-call | tf_op jit(solution)/shard_map/pallas_call | solution.py:1495

commit v7 on v6

--- a/solution.py
+++ b/solution.py
@@ -487,19 +487,27 @@
     return value if isinstance(value, int) else pl.multiple_of(value, by)
 
 
-def twelfth(index):
-    return lax.div(index * 43, 512)
+def shift(value, by):
+    return lax.shift_right_arithmetic(value, jnp.int32(by))
+
+
+def low_bits(value, by):
+    return value - shift(value, by) * (1 << by)
+
+
+def power_above(value):
+    return (value - 1).bit_length()
 
 
 def backward_unit(layers, index):
-    whole = lax.div(index, PARTS)
+    whole = shift(index, 1)
     half = index - PARTS * whole
-    turn = twelfth(whole)
+    turn = shift(whole * 43, 9)
     place = whole - UNITS * turn
-    part = lax.div(place, 4)
+    part = shift(place, 2)
     within = place - 4 * part
-    is_down, is_late = lax.div(2 - part, 2), lax.div(part, 2)
-    late = within + 3 - 4 * lax.div(within + 3, 4)
+    is_down, is_late = shift(2 - part, 1), shift(part, 1)
+    late = low_bits(within + 3, 2)
     unit = is_down * 8 + (1 - is_late) * place + is_late * late
     return layers - 1 - turn, unit, half
 
@@ -690,7 +698,9 @@
     pl.semaphore_wait(barrier, 8 + lax.div(d * (3 - d), 2))
 
     def role(i):
-        return lax.rem(i, 3) * lax.div(2 * count - 3 - i, count)
+        bits = power_above(count)
+        of_three = i - 3 * shift(i * 43, 7)
+        return of_three * shift((1 << bits) + count - 3 - i, bits)
 
     def collects(i):
         return role(i) != 2 - parity
@@ -828,8 +838,9 @@
 
     def piece_at(i):
         layer, unit, half = backward_unit(layers, i)
-        early = lax.div(pieces + EARLY_UNITS * PARTS - 1 - i, pieces)
-        ahead = layers * UNITS + lax.div(i, PARTS)
+        bits = power_above(pieces)
+        early = shift((1 << bits) + EARLY_PIECES - 1 - i, bits)
+        ahead = layers * UNITS + shift(i, 1)
         at = early * ahead + (1 - early) * (layer * UNITS + unit)
         return at, pl.ds(aligned(half * WIDE, 128), WIDE)
 
@@ -840,14 +851,17 @@
 
     def piece_of(t, lag):
         at = t - lag
-        span = 4 * pieces
-        return at - GAP * lax.div(at + span - (EARLY_PIECES + GAP), span)
+        bits = power_above(2 * pieces)
+        return at - GAP * shift(at + (1 << bits) - (EARLY_PIECES + GAP), bits)
 
     def ring(i):
-        return lax.rem(i, RING)
+        return low_bits(i, 3)
 
     def long_ring(i):
-        return lax.rem(i, 2 * RING)
+        return low_bits(i, 4)
+
+    def slot_of(i):
+        return i - SLOTS * shift(i * 43, 8)
 
     def reduce_tick(t):
         @pl.when(during(t, 0))
@@ -856,7 +870,7 @@
             n, cols = piece_at(i)
             send(
                 wb.at[n, :, :, 1 - c, :, cols],
-                rc.at[lax.rem(i, CORE_SLOTS)],
+                rc.at[low_bits(i, 2)],
                 s0_send.at[ring(i)],
                 core_sem.at[ring(i)],
                 in_plane(fc),
@@ -866,7 +880,7 @@
         def _():
             i = piece_of(t, LAG_XY)
             n, cols = piece_at(i)
-            slot = lax.rem(i, SLOTS)
+            slot = slot_of(i)
             wait_piece(xy_sem.at[ring(i)], 2)
             along_x = wb.at[n, :, x, c, first_rows, cols]
             along_y = wb.at[n, y, :, c, second_rows, cols]
@@ -891,11 +905,11 @@
         def _():
             i = piece_of(t, 1)
             n, cols = piece_at(i)
-            slot = lax.rem(i, SLOTS)
+            slot = slot_of(i)
             wait_piece(core_sem.at[ring(i)], 4)
             wait_piece(s0_send.at[ring(i)], 4)
             mine = wb.at[n, :, :, c, :, cols]
-            mine[...] = mine[...] + rc[lax.rem(i, CORE_SLOTS)]
+            mine[...] = mine[...] + rc[low_bits(i, 2)]
             send(
                 wb.at[n, :, 1 - x, c, first_rows, cols],
                 r2.at[slot, 0],
@@ -968,14 +982,14 @@
 
             @pl.when(outer)
             def _():
-                to = rz.at[lax.rem(i, SLOTS), 0]
+                to = rz.at[slot_of(i), 0]
                 send(own, to, rs_send.at[long_ring(i)], z_sem.at[ring(i), 0], along(z_in))
 
         @pl.when(both(inner, during(t, LAG_Z1)))
         def _():
             i = piece_of(t, LAG_Z1)
             n, cols = piece_at(i)
-            slot = lax.rem(i, SLOTS)
+            slot = slot_of(i)
             wait_piece(z_sem.at[ring(i), 0], 1)
             own = wb.at[n, y, x, c, :, cols]
             own[...] = own[...] + rz[slot, 0]
@@ -987,7 +1001,7 @@
             n, cols = piece_at(i)
             wait_piece(z_sem.at[ring(i), 1], 1)
             done = wb.at[n, y, x, 1 - c, :, cols]
-            done[...] = wb[n, y, x, c, :, cols] + rz[lax.rem(i, SLOTS), 1]
+            done[...] = wb[n, y, x, c, :, cols] + rz[slot_of(i), 1]
             send(done, done, rs_send.at[long_ring(i)], z_sem.at[ring(i), 2], along(z_out))
 
     @pl.loop(0, layers)

time: 240 us -> 240 us (level)
  no operation moved by 1% of the time
where the time goes in v7:
time: 240 us
  Pallas kernels  239 us (100%)
    pallas_call x1, Pallas kernels, kernel_local(): pl.pallas_call(functools.partial(encoder_kernel, layers), out_shape=(jax....  233 us
    pallas_call x1, Pallas kernels, kernel_local(): pl.pallas_call(functools.partial(closing_kernel, layers), out_shape=[jax....  5.71 us

profile of v7, /device:TPU:0, one launch (start us, length us, event | category | flops | bytes accessed | tf_op | source)
XLA Modules:
  0.0 240.0 jit_solution(17510843236315370810)
XLA Ops:
  0.7 233.4 %shard_map.262 = (bf16[345,768]{1,0:T(8,128)(2,1)}, f32[345,768]{1,0:T(8,128)}, f32[2,16,128]{2,1,0:T(8,128)}, bf16[2,96,2304]{2,1,0:T(8,128)(2,1)}, bf16[2,96,7...) custom-call(bf16[345,768]{1,0:T(8,128)(2,1)} %tokens.1, bf16[345,768]{1,0:T(8,128)(2,1)} %cotangent.1, ...), custom_call_target="tpu_custom_call" | custom-call | tf_op jit(solution)/shard_map/pallas_call | solution.py:1427
  234.1 5.7 %shard_map.263 = (bf16[345,768]{1,0:T(8,128)(2,1)}, f32[345,768]{1,0:T(8,128)}, f32[2,96]{1,0:T(2,128)}, f32[2,96]{1,0:T(2,128)}, f32[2,96]{1,0:T(2,128)}, /*ind...) custom-call(bf16[345,768]{1,0:T(8,128)(2,1)} %get-tuple-element.37.r, ...), custom_call_target="tpu_custom_call" | custom-call | tf_op jit(solution)/shard_map/pallas_call | solution.py:1509

commit v8 on v7

--- a/solution.py
+++ b/solution.py
@@ -452,12 +452,12 @@
 SHARD = 96
 HALF = 48
 UNITS = 12
-SLOTS = 6
+SLOTS = 7
 CORE_SLOTS = 4
 RING = 8
 PARTS = 2
 WIDE = D // PARTS
-LAG_XY, LAG_LAST, LAG_Z1, LAG_Z2, LAG_OUT = 4, 6, 8, 10, 12
+LAG_XY, LAG_LAST, LAG_Z1, LAG_Z2, LAG_OUT = 4, 6, 8, 10, 13
 LAG_NEXT, LAG_PLANE, LAG_PASS, LAG_WHOLE = 2, 4, 8, 9
 EARLY_UNITS = 2
 EARLY_PIECES = EARLY_UNITS * PARTS
@@ -861,7 +861,7 @@
         return low_bits(i, 4)
 
     def slot_of(i):
-        return i - SLOTS * shift(i * 43, 8)
+        return i - SLOTS * shift(i * 37, 8)
 
     def reduce_tick(t):
         @pl.when(during(t, 0))

time: 240 us -> 239 us (level)
  no operation moved by 1% of the time
where the time goes in v8:
time: 239 us
  Pallas kernels  238 us (100%)
    pallas_call x1, Pallas kernels, kernel_local(): pl.pallas_call(functools.partial(encoder_kernel, layers), out_shape=(jax....  232 us
    pallas_call x1, Pallas kernels, kernel_local(): pl.pallas_call(functools.partial(closing_kernel, layers), out_shape=[jax....  5.71 us

profile of v8, /device:TPU:0, one launch (start us, length us, event | category | flops | bytes accessed | tf_op | source)
XLA Modules:
  0.0 239.0 jit_solution(2282578071007518695)
XLA Ops:
  0.7 232.5 %shard_map.262 = (bf16[345,768]{1,0:T(8,128)(2,1)}, f32[345,768]{1,0:T(8,128)}, f32[2,16,128]{2,1,0:T(8,128)}, bf16[2,96,2304]{2,1,0:T(8,128)(2,1)}, bf16[2,96,7...) custom-call(bf16[345,768]{1,0:T(8,128)(2,1)} %tokens.1, bf16[345,768]{1,0:T(8,128)(2,1)} %cotangent.1, ...), custom_call_target="tpu_custom_call" | custom-call | tf_op jit(solution)/shard_map/pallas_call | solution.py:1427
  233.1 5.7 %shard_map.263 = (bf16[345,768]{1,0:T(8,128)(2,1)}, f32[345,768]{1,0:T(8,128)}, f32[2,96]{1,0:T(2,128)}, f32[2,96]{1,0:T(2,128)}, f32[2,96]{1,0:T(2,128)}, /*ind...) custom-call(bf16[345,768]{1,0:T(8,128)(2,1)} %get-tuple-element.37.r, ...), custom_call_target="tpu_custom_call" | custom-call | tf_op jit(solution)/shard_map/pallas_call | solution.py:1509
